TPU v7x, 128 devices: a whole 4x4x4 slice. The times are simulated.
128 devices in a mesh: band: 32 (over x, y_hi, z), clip: 4 (over y_lo, core).
Axes of the slice: x: 4, y: 4 (y_hi: 2, y_lo: 2; y = y_hi * 2 + y_lo), z: 4, core: 2. Of those that a mesh axis runs over, the one named last changes fastest.
Arguments:
- latent: bfloat16 [16, 64, 512, 128], P('clip', 'band'), parts along dimension 0, may hold values from -6 to 6
- dec_kernel: bfloat16 [3, 3, 3, 128, 128], replicated, may hold values from -0.109375 to 0.109375
- rgb_kernel: bfloat16 [3, 3, 3, 128, 3], replicated, may hold values from -0.4375 to 0.4375
- target: bfloat16 [16, 64, 512, 3], P('clip', 'band'), parts along dimension 0, may hold values from -8 to 8
- vgg_first: bfloat16 [3, 3, 3, 64], replicated, may hold values from -1.25 to 1.25
- vgg_second: bfloat16 [3, 3, 64, 128], replicated, may hold values from -0.25 to 0.25
- critic_kernel: bfloat16 [3, 3, 3, 3, 64], replicated, may hold values from -0.625 to 0.625
- critic_head: float32 [64], replicated, may hold values from -2 to 2
Outputs:
- grad_latent: float32 [16, 64, 512, 128], P('clip', 'band'), parts along dimension 0
- grad_dec: float32 [12, 3, 3, 128, 128], P('clip'), parts along dimension 0
- grad_rgb: float32 [12, 3, 3, 128, 3], P('clip'), parts along dimension 0
There are 4 independent parts, one for each index of `clip`. A program takes and returns all parts, laid end to end along the dimension named above; an argument that names none is the same for every part. Nothing has to cross between parts.
All inputs are finite; a program needn't handle non-finite values.
Results may differ from a plain program's by a relative error of at most 0.025.
Values may be sent and summed in bfloat16 or wider, within the bound.
No kernel may reach another device: no remote copies, remote signals or barrier semaphores. Data moves between devices by JAX's collectives and lax.ppermute only.
A program may use at most 128 MiB of HBM per device.

v0:
```python
import jax
import jax.numpy as jnp
from jax import lax
from jax.sharding import PartitionSpec as P

HIGH = lax.Precision.HIGHEST
DEC_SPEC = ("NDHWC", "DHWIO", "NDHWC")
IMG_SPEC = ("NHWC", "HWIO", "NHWC")


def with_halo(shard, sides, width):
    for axis, dim in sides:
        size, length = (lax.axis_size(axis), shard.shape[dim])
        up = [(i, (i + 1) % size) for i in range(size - 1)]
        down = [(j, i) for i, j in up]
        last = lax.slice_in_dim(shard, length - width, length, axis=dim)
        first = lax.slice_in_dim(shard, 0, width, axis=dim)
        before = lax.ppermute(last, axis, up)
        after = lax.ppermute(first, axis, down)
        shard = jnp.concatenate([before, shard, after], axis=dim)
    return shard


def conv_valid(field, kernel, spec):
    spatial = kernel.ndim - 2
    return lax.conv_general_dilated(
        field,
        kernel,
        (1,) * spatial,
        "VALID",
        dimension_numbers=spec,
        preferred_element_type=jnp.float32,
    )


def flipped(kernel):
    spatial = kernel.ndim - 2
    turned = jnp.flip(kernel, axis=tuple(range(spatial)))
    return jnp.swapaxes(turned, -1, -2)


def silu_slope(value):
    gate_value = jax.nn.sigmoid(value)
    return gate_value * (1.0 + value * (1.0 - gate_value))


def decoder_pad(field):
    extended = with_halo(field, (("band", 1),), 1)
    return jnp.pad(extended, ((1, 1), (0, 0), (1, 1), (0, 0)))


def decoder_conv(padded, kernel):
    return conv_valid(padded[None], kernel, DEC_SPEC)[0]


def branch_pad(field):
    extended = with_halo(field, (("band", 1),), 1)
    return jnp.pad(extended, ((0, 0), (0, 0), (1, 1), (0, 0)))


def critic_conv(padded, kernel):
    timed = jnp.pad(padded, ((1, 1), (0, 0), (0, 0), (0, 0)))
    return conv_valid(timed[None], kernel, DEC_SPEC)[0]


def kernel_grad(padded, grad_out):
    frames_n, rows_n, cols_n = (grad_out.shape[0], grad_out.shape[1], grad_out.shape[2])
    blocks = []
    for first in range(3):
        for second in range(3):
            for third in range(3):
                window = padded[
                    first : first + frames_n, second : second + rows_n, third : third + cols_n
                ]
                blocks.append(
                    jnp.einsum(
                        "fhwi,fhwo->io", window, grad_out, preferred_element_type=jnp.float32
                    )
                )
    return jnp.stack(blocks).reshape((3, 3, 3) + blocks[0].shape)


def per_device(
    latent, dec_kernel, rgb_kernel, target, vgg_first, vgg_second, critic_kernel, critic_head
):
    frames_n = latent.shape[0]
    latent_pad = decoder_pad(latent)
    pre_one = decoder_conv(latent_pad, dec_kernel)
    act_one = jax.nn.silu(pre_one).astype(jnp.bfloat16)
    act_pad = decoder_pad(act_one)
    frames = decoder_conv(act_pad, rgb_kernel).astype(jnp.bfloat16)
    joined = jnp.concatenate([frames, target], axis=0)
    joined_pad = branch_pad(joined)
    pre_vone = conv_valid(joined_pad, vgg_first, IMG_SPEC)
    feat_one = jax.nn.silu(pre_vone).astype(jnp.bfloat16)
    pre_vtwo = conv_valid(branch_pad(feat_one), vgg_second, IMG_SPEC)
    feat_two = jax.nn.silu(pre_vtwo)
    spread = feat_two[:frames_n] - feat_two[frames_n:]
    grad_two = (0.25 * spread * silu_slope(pre_vtwo[:frames_n])).astype(jnp.bfloat16)
    back_one = conv_valid(branch_pad(grad_two), flipped(vgg_second), IMG_SPEC)
    grad_one = (back_one * silu_slope(pre_vone[:frames_n])).astype(jnp.bfloat16)
    vgg_back = conv_valid(branch_pad(grad_one), flipped(vgg_first), IMG_SPEC)
    crit_pre = critic_conv(joined_pad[:frames_n], critic_kernel)
    logits = jnp.dot(jax.nn.silu(crit_pre), critic_head, precision=HIGH)
    slope = -jax.nn.sigmoid(-logits)
    grad_crit = (slope[..., None] * critic_head * silu_slope(crit_pre)).astype(jnp.bfloat16)
    crit_back = critic_conv(branch_pad(grad_crit), flipped(critic_kernel))
    grad_frames = (vgg_back + crit_back).astype(jnp.bfloat16)
    grad_act = decoder_conv(decoder_pad(grad_frames), flipped(rgb_kernel))
    grad_pre = (grad_act * silu_slope(pre_one)).astype(jnp.bfloat16)
    grad_latent = decoder_conv(decoder_pad(grad_pre), flipped(dec_kernel))
    local_dec = kernel_grad(latent_pad, grad_pre)
    local_rgb = kernel_grad(act_pad, grad_frames)
    summed_dec, summed_rgb = (
        lax.psum(local_dec.astype(jnp.bfloat16), "band").astype(jnp.float32),
        lax.psum(local_rgb.astype(jnp.bfloat16), "band").astype(jnp.float32),
    )
    pixels = frames_n * latent.shape[1] * lax.axis_size("band") * latent.shape[2]
    factor = float(pixels) ** (-0.5)
    return (grad_latent, summed_dec * factor, summed_rgb * factor)


def solution(mesh):
    placed = (
        P("clip", "band", None, None),
        P(),
        P(),
        P("clip", "band", None, None),
        P(),
        P(),
        P(),
        P(),
    )
    return jax.shard_map(
        per_device,
        mesh=mesh,
        in_specs=placed,
        out_specs=(
            P("clip", "band", None, None),
            P("clip", None, None, None, None),
            P("clip", None, None, None, None),
        ),
        check_vma=False,
    )
```

profile of v0, /device:TPU:0, one launch (start us, length us, event | category | flops | bytes accessed | tf_op | source)
XLA Modules:
  0.0 980.2 jit_solution(3108771661807561027)
XLA Ops:
  8.9 3.9 collective-permute-start
  14.1 9.8 %collective-permute-done = bf16[4,1,512,128]{2,3,1,0:T(8,128)(2,1)S(1)} collective-permute-done((bf16[4,1,512,128]{2,3,1,0:T(8,128)(2,1)S(1)}, bf16[4,1,512,128]{2,3,1,0:T(8,128)(2,1)S(1)}, u32[]{:S(2)}, u32[]{:S(2)}) %collective-permute-start) | collective-permute-done | bytes 524320 | tf_op jit(solution)/shard_map/ppermute | solution.py:18
  24.0 4.3 collective-permute-done.1
  28.3 3.1 fusion.479
  31.4 7.6 copy.813
  39.0 3.1 pad.43.clone
  42.8 8.3 fusion.103
  54.3 3.7 collective-permute-start.2
  59.3 8.6 collective-permute-done.2
  67.9 4.2 collective-permute-done.3
  72.9 2.5 fusion.478
  78.6 66.6 %fusion.41 = bf16[4,2,8,65,3]{2,4,3,1,0:T(4,128)(2,1)} fusion(bf16[3,3,3,128,3]{3,4,2,1,0:T(4,128)(2,1)S(1)} %copy-done.30, bf16[6,4,1,7,2,128]{5,3,4,1,0,2:T(8,128)(2,1)S(1)} %slice.334, bf16[6,4,1,8,65,128]{5,3,4,1,0,2:T(8,128)(2,1)S(1)} %copy.670), kind=kOutput, calls=%fused_computation.58 | convolution fusion | flops 96141312 | bytes 3326592 | tf_op jit(solution)/shard_map/conv_general_dilated | solution.py:26
  145.3 1.9 copy.671
  151.0 7.1 collective-permute-start.4
  159.5 4.1 select_maximum_fusion
  164.0 2.4 copy.675
  166.7 2.2 copy.693
  169.9 7.2 fusion.94
  177.0 3.0 copy.694
  180.1 2.8 reshape.43
  182.9 2.3 fusion.359
  185.2 5.2 multiply_convert_fusion
  193.2 2.7 copy.676
  195.8 6.4 collective-permute-start.6
  202.2 2.7 copy.677
  206.1 1.6 multiply_convert_fusion.2
  208.7 5.3 collective-permute-start.12
  215.2 2.7 copy.678
  218.0 2.5 collective-permute-done.7
  220.5 2.7 copy.679
  223.2 5.0 fusion.11
  231.4 4.7 collective-permute-start.8
  237.5 3.3 select_maximum_fusion.4
  242.4 2.7 copy.810
  245.1 1.7 fusion.107
  248.6 6.3 reshape.46
  254.9 6.5 copy.697
  262.9 1.8 maximum_bitcast_fusion
  264.7 1.6 copy.815
  268.3 4.0 fusion.91
  272.3 4.2 copy.685
  276.5 3.3 reshape.66
  281.3 1.7 fusion.358
  283.8 5.3 collective-permute-start.10
  290.6 66.7 %fusion.43 = f32[4,2,8,65,3]{2,4,3,1,0:T(4,128)} fusion(bf16[3,3,3,3,64]{4,3,2,1,0:T(4,128)(2,1)S(1)} %copy-done.29, bf16[6,4,1,7,2,64]{5,3,4,1,0,2:T(8,128)(2,1)S(1)} %copy-done.23, bf16[6,4,1,8,65,64]{5,3,4,1,0,2:T(8,128)(2,1)S(1)} %copy-done.7), kind=kOutput, calls=%fused_computation.59 | convolution fusion | flops 48070656 | bytes 1700736 | tf_op jit(solution)/shard_map/conv_general_dilated | solution.py:26
  357.3 2.2 copy.698
  361.0 1.6 reshape.174
  363.8 1.7 pad.49
  365.5 4.7 reshape.34
  370.2 2.4 slice.350
  372.6 2.7 fusion.54
  375.3 6.1 copy.688
  381.4 8.6 fusion.108
  390.4 1.6 fusion.296
  401.7 185.5 %psum.15 = bf16[3,3,3,128,3]{3,4,2,1,0:T(4,128)(2,1)S(1)} all-reduce(bf16[3,3,3,128,3]{3,4,2,1,0:T(4,128)(2,1)S(1)} %bitcast.952), channel_id=1, replica_groups=mesh['band'=32,'clip'=4] {'band'}, use_global_device_ids=true, to_apply=%region_1.2 | all-reduce | flops 10368 | bytes 41472 | tf_op jit(solution)/shard_map/psum | solution.py:116
  590.4 3.7 collective-permute-done.15
  594.4 2.4 copy.703
  597.8 5.8 fusion.97
  625.4 3.6 collective-permute-done.16
  629.0 4.1 collective-permute-done.17
  633.1 2.3 fusion.45
  638.4 8.3 fusion.100
  649.4 321.2 %all-reduce.10.cloned.1.call-done = bf16[3,3,3,128,128]{4,3,2,1,0:T(8,128)(2,1)} async-done(((bf16[3,3,3,128,128]{4,3,2,1,0:T(8,128)(2,1)}), bf16[3,3,3,128,128]{4,3,2,1,0:T(8,128)(2,1)}) %all-reduce.10.cloned.1.call-update) | async-done | bytes 884752 | tf_op jit(solution)/shard_map/psum | solution.py:115
  970.6 2.6 convert_multiply_fusion
  (213 shorter events, 84.5 us)
Async XLA Ops:
  7.2 35.4 %copy-start = (bf16[3,3,3,128,128]{4,3,2,1,0:T(8,128)(2,1)S(1)}, bf16[3,3,3,128,128]{4,3,2,1,0:T(8,128)(2,1)}, u32[]{:S(2)}) copy-start(bf16[3,3,3,128,128]{4,3,2,1,0:T(8,128)(2,1)} %param.9) | copy-start | bytes 2654212
  7.2 963.4 %all-reduce.10.cloned.1.call-start = ((), (), s32[]{:S(2)}) async-start(), calls=%async_computation | async-start | bytes 1769472 | tf_op jit(solution)/shard_map/psum | solution.py:115
  8.9 15.1 %collective-permute-start = (bf16[4,1,512,128]{2,3,1,0:T(8,128)(2,1)S(1)}, bf16[4,1,512,128]{2,3,1,0:T(8,128)(2,1)S(1)}, u32[]{:S(2)}, u32[]{:S(2)}) collective-permute-start(bf16[4,1,512,128]{2,3,1,0:T(8,128)(2,1)S(1)} %get-tuple-element.31), channel_id=1, source_target_pairs={{0,4},{4,8},{8,12},{12,16},{16,20},{20,24},{24,28},{28,32},{32,36}... | collective-permute-start | bytes 1572872 | tf_op jit(solution)/shard_map/ppermute | solution.py:18
  12.8 15.4 %collective-permute-start.1 = (bf16[4,1,512,128]{2,3,1,0:T(8,128)(2,1)S(1)}, bf16[4,1,512,128]{2,3,1,0:T(8,128)(2,1)S(1)}, u32[]{:S(2)}, u32[]{:S(2)}) collective-permute-start(bf16[4,1,512,128]{2,3,1,0:T(8,128)(2,1)S(1)} %get-tuple-element.32), channel_id=1, source_target_pairs={{4,0},{8,4},{12,8},{16,12},{20,16},{24,20},{28,24},{32,28},{36,32}... | collective-permute-start | bytes 1572872 | tf_op jit(solution)/shard_map/ppermute | solution.py:19
  24.0 15.0 %copy-start.11 = (bf16[4,1,512,128]{2,3,1,0:T(8,128)(2,1)}, bf16[4,1,512,128]{2,3,1,0:T(8,128)(2,1)S(1)}, u32[]{:S(2)}) copy-start(bf16[4,1,512,128]{2,3,1,0:T(8,128)(2,1)S(1)} %collective-permute-done) | copy-start | bytes 1572868
  28.3 131.2 %copy-start.9 = (bf16[4,1,512,128]{2,3,1,0:T(8,128)(2,1)}, bf16[4,1,512,128]{2,3,1,0:T(8,128)(2,1)S(1)}, u32[]{:S(2)}) copy-start(bf16[4,1,512,128]{2,3,1,0:T(8,128)(2,1)S(1)} %collective-permute-done.1) | copy-start | bytes 1572868
  42.1 0.7 copy-start.33
  52.4 1.3 copy-start.2
  53.7 5.6 copy-start.24
  54.3 13.6 %collective-permute-start.2 = (bf16[4,1,512,128]{3,2,1,0:T(8,128)(2,1)S(1)}, bf16[4,1,512,128]{3,2,1,0:T(8,128)(2,1)S(1)}, u32[]{:S(2)}, u32[]{:S(2)}) collective-permute-start(bf16[4,1,512,128]{3,2,1,0:T(8,128)(2,1)S(1)} %get-tuple-element.29), channel_id=1, source_target_pairs={{0,4},{4,8},{8,12},{12,16},{16,20},{20,24},{24,28},{28,32},{32,36}... | collective-permute-start | bytes 1572872 | tf_op jit(solution)/shard_map/ppermute | solution.py:18
  58.0 14.2 %collective-permute-start.3 = (bf16[4,1,512,128]{3,2,1,0:T(8,128)(2,1)S(1)}, bf16[4,1,512,128]{3,2,1,0:T(8,128)(2,1)S(1)}, u32[]{:S(2)}, u32[]{:S(2)}) collective-permute-start(bf16[4,1,512,128]{3,2,1,0:T(8,128)(2,1)S(1)} %get-tuple-element.30), channel_id=1, source_target_pairs={{4,0},{8,4},{12,8},{16,12},{20,16},{24,20},{28,24},{32,28},{36,32}... | collective-permute-start | bytes 1572872 | tf_op jit(solution)/shard_map/ppermute | solution.py:19
  67.9 4.2 copy-start.16
  72.1 0.8 copy-start.13
  77.9 0.7 copy-start.30
  78.6 68.5 %copy-start.25 = (pred[8,65]{1,0:T(8,128)(4,1)S(1)}, pred[8,65]{1,0:T(8,128)(4,1)}, u32[]{:S(2)}) copy-start(pred[8,65]{1,0:T(8,128)(4,1)} %constant.70) | copy-start | bytes 1564
  151.0 12.6 %collective-permute-start.4 = (bf16[8,1,512,3]{2,0,3,1:T(8,128)(2,1)S(1)}, bf16[8,1,512,3]{2,0,3,1:T(8,128)(2,1)S(1)}, u32[]{:S(2)}, u32[]{:S(2)}) collective-permute-start(bf16[8,1,512,3]{2,0,3,1:T(8,128)(2,1)S(1)} %get-tuple-element.37), channel_id=1, source_target_pairs={{0,4},{4,8},{8,12},{12,16},{16,20},{20,24},{24,28},{28,32},{32,36}... | collective-permute-start | bytes 73736 | tf_op jit(solution)/shard_map/ppermute | solution.py:18
  158.1 5.7 collective-permute-start.5
  163.5 6.3 copy-start.28
  177.0 5.8 copy-start.26
  182.9 2.3 copy-start.20
  182.9 2.3 copy-start.32
  190.4 1.3 copy-start.19
  195.8 19.4 %collective-permute-start.6 = (bf16[8,1,512,64]{2,3,1,0:T(8,128)(2,1)}, bf16[8,1,512,64]{2,3,1,0:T(8,128)(2,1)}, u32[]{:S(2)}, u32[]{:S(2)}) collective-permute-start(bf16[8,1,512,64]{2,3,1,0:T(8,128)(2,1)} %copy.676), channel_id=1, source_target_pairs={{0,4},{4,8},{8,12},{12,16},{16,20},{20,24},{24,28},{28,32},{32,36}... | collective-permute-start | bytes 1572872 | tf_op jit(solution)/shard_map/ppermute | solution.py:18
  204.9 15.6 %collective-permute-start.7 = (bf16[8,1,512,64]{2,3,1,0:T(8,128)(2,1)}, bf16[8,1,512,64]{2,3,1,0:T(8,128)(2,1)}, u32[]{:S(2)}, u32[]{:S(2)}) collective-permute-start(bf16[8,1,512,64]{2,3,1,0:T(8,128)(2,1)} %copy.677), channel_id=1, source_target_pairs={{4,0},{8,4},{12,8},{16,12},{20,16},{24,20},{28,24},{32,28},{36,32}... | collective-permute-start | bytes 1572872 | tf_op jit(solution)/shard_map/ppermute | solution.py:19
  208.7 36.5 %collective-permute-start.12 = (bf16[4,1,512,64]{2,3,1,0:T(8,128)(2,1)}, bf16[4,1,512,64]{2,3,1,0:T(8,128)(2,1)}, u32[]{:S(2)}, u32[]{:S(2)}) collective-permute-start(bf16[4,1,512,64]{2,3,1,0:T(8,128)(2,1)} %get-tuple-element.33), channel_id=1, source_target_pairs={{0,4},{4,8},{8,12},{12,16},{16,20},{20,24},{24,28},{28,32},{32,36}... | collective-permute-start | bytes 786440 | tf_op jit(solution)/shard_map/ppermute | solution.py:18
  213.9 31.2 %collective-permute-start.13 = (bf16[4,1,512,64]{2,3,1,0:T(8,128)(2,1)}, bf16[4,1,512,64]{2,3,1,0:T(8,128)(2,1)}, u32[]{:S(2)}, u32[]{:S(2)}) collective-permute-start(bf16[4,1,512,64]{2,3,1,0:T(8,128)(2,1)} %get-tuple-element.34), channel_id=1, source_target_pairs={{4,0},{8,4},{12,8},{16,12},{20,16},{24,20},{28,24},{32,28},{36,32}... | collective-permute-start | bytes 786440 | tf_op jit(solution)/shard_map/ppermute | solution.py:19
  229.5 8.0 copy-start.14
  229.5 8.0 copy-start.17
  230.3 10.5 %copy-start.4 = (bf16[4,2,512,128]{3,2,1,0:T(8,128)(2,1)}, bf16[4,2,512,128]{3,2,1,0:T(8,128)(2,1)S(1)}, u32[]{:S(2)}) copy-start(bf16[4,2,512,128]{3,2,1,0:T(8,128)(2,1)S(1)} %fusion.57) | copy-start | bytes 3145732
  230.3 10.5 %copy-start.21 = (f32[8,2,512,64]{3,0,2,1:T(8,128)S(1)}, f32[8,2,512,64]{3,0,2,1:T(8,128)}, u32[]{:S(2)}) copy-start(f32[8,2,512,64]{3,0,2,1:T(8,128)} %get-tuple-element.42) | copy-start | bytes 6291460
  231.4 31.5 %collective-permute-start.8 = (bf16[4,1,512,128]{3,2,1,0:T(8,128)(2,1)}, bf16[4,1,512,128]{3,2,1,0:T(8,128)(2,1)}, u32[]{:S(2)}, u32[]{:S(2)}) collective-permute-start(bf16[4,1,512,128]{3,2,1,0:T(8,128)(2,1)} %get-tuple-element.27), channel_id=1, source_target_pairs={{0,4},{4,8},{8,12},{12,16},{16,20},{20,24},{24,28},{28,32},{32,36}... | collective-permute-start | bytes 1572872 | tf_op jit(solution)/shard_map/ppermute | solution.py:18
  236.1 26.9 %collective-permute-start.9 = (bf16[4,1,512,128]{3,2,1,0:T(8,128)(2,1)}, bf16[4,1,512,128]{3,2,1,0:T(8,128)(2,1)}, u32[]{:S(2)}, u32[]{:S(2)}) collective-permute-start(bf16[4,1,512,128]{3,2,1,0:T(8,128)(2,1)} %get-tuple-element.28), channel_id=1, source_target_pairs={{4,0},{8,4},{12,8},{16,12},{20,16},{24,20},{28,24},{32,28},{36,32}... | collective-permute-start | bytes 1572872 | tf_op jit(solution)/shard_map/ppermute | solution.py:19
  267.2 1.1 copy-start.27
  267.2 1.1 copy-start.35
  279.8 10.8 %copy-start.7 = (bf16[6,4,1,8,65,64]{5,3,4,1,0,2:T(8,128)(2,1)S(1)}, bf16[6,4,1,8,65,64]{5,3,4,1,0,2:T(8,128)(2,1)}, u32[]{:S(2)}) copy-start(bf16[6,4,1,8,65,64]{5,3,4,1,0,2:T(8,128)(2,1)} %copy.697) | copy-start | bytes 4792324
  279.8 10.8 %copy-start.23 = (bf16[6,4,1,7,2,64]{5,3,4,1,0,2:T(8,128)(2,1)S(1)}, bf16[6,4,1,7,2,64]{5,3,4,1,0,2:T(8,128)(2,1)}, u32[]{:S(2)}) copy-start(bf16[6,4,1,7,2,64]{5,3,4,1,0,2:T(8,128)(2,1)} %slice.356) | copy-start | bytes 129028
  279.8 10.8 %copy-start.29 = (bf16[3,3,3,3,64]{4,3,2,1,0:T(4,128)(2,1)S(1)}, bf16[3,3,3,3,64]{4,3,2,1,0:T(4,128)(2,1)}, u32[]{:S(2)}) copy-start(bf16[3,3,3,3,64]{4,3,2,1,0:T(4,128)(2,1)} %param.14) | copy-start | bytes 31108
  283.8 78.8 %collective-permute-start.10 = (bf16[4,1,512,64]{2,3,1,0:T(8,128)(2,1)}, bf16[4,1,512,64]{2,3,1,0:T(8,128)(2,1)}, u32[]{:S(2)}, u32[]{:S(2)}) collective-permute-start(bf16[4,1,512,64]{2,3,1,0:T(8,128)(2,1)} %get-tuple-element.35), channel_id=1, source_target_pairs={{0,4},{4,8},{8,12},{12,16},{16,20},{20,24},{24,28},{28,32},{32,36}... | collective-permute-start | bytes 786440 | tf_op jit(solution)/shard_map/ppermute | solution.py:18
  289.1 73.6 %collective-permute-start.11 = (bf16[4,1,512,64]{2,3,1,0:T(8,128)(2,1)}, bf16[4,1,512,64]{2,3,1,0:T(8,128)(2,1)}, u32[]{:S(2)}, u32[]{:S(2)}) collective-permute-start(bf16[4,1,512,64]{2,3,1,0:T(8,128)(2,1)} %get-tuple-element.36), channel_id=1, source_target_pairs={{4,0},{8,4},{12,8},{16,12},{20,16},{24,20},{28,24},{32,28},{36,32}... | collective-permute-start | bytes 786440 | tf_op jit(solution)/shard_map/ppermute | solution.py:19
  370.2 2.4 copy-start.1
  375.3 15.0 %slice-start = ((f32[4,2,1,520,3]{3,4,1,0,2:T(4,128)}), f32[4,2,1,512,3]{3,4,1,0,2:T(4,128)S(1)}, s32[]{:S(2)}) async-start(f32[4,2,1,520,3]{3,4,1,0,2:T(4,128)} %reshape.174), calls=%async_computation.1 | async-start | bytes 131072 | tf_op jit(solution)/shard_map/conv_general_dilated | solution.py:26
  390.3 3.3 copy-start.8
  395.0 1.3 copy-start.18
  396.9 1.2 copy-start.15
  400.9 196.8 %copy-start.31 = (bf16[3,3,3,128,3]{3,4,2,1,0:T(4,128)(2,1)S(1)}, bf16[3,3,3,128,3]{3,4,2,1,0:T(4,128)(2,1)}, u32[]{:S(2)}) copy-start(bf16[3,3,3,128,3]{3,4,2,1,0:T(4,128)(2,1)} %param.10) | copy-start | bytes 62212
  400.9 196.9 %copy-start.34 = (pred[8,65]{0,1:T(8,128)(4,1)S(1)}, pred[8,65]{0,1:T(8,128)(4,1)}, u32[]{:S(2)}) copy-start(pred[8,65]{0,1:T(8,128)(4,1)} %constant.78) | copy-start | bytes 1564
  587.1 3.2 collective-permute-start.14
  588.4 5.6 collective-permute-start.15
  603.6 1.6 copy-start.3
  605.2 2.3 copy-start.6
  611.0 1.5 copy-start.12
  612.6 1.9 copy-start.5
  614.4 1.5 copy-start.10
  620.4 8.6 collective-permute-start.16
  622.1 11.1 %collective-permute-start.17 = (bf16[4,1,512,128]{3,2,1,0:T(8,128)(2,1)S(1)}, bf16[4,1,512,128]{3,2,1,0:T(8,128)(2,1)S(1)}, u32[]{:S(2)}, u32[]{:S(2)}) collective-permute-start(bf16[4,1,512,128]{3,2,1,0:T(8,128)(2,1)S(1)} %get-tuple-element.26), channel_id=1, source_target_pairs={{4,0},{8,4},{12,8},{16,12},{20,16},{24,20},{28,24},{32,28},{36,32}... | collective-permute-start | bytes 1572872 | tf_op jit(solution)/shard_map/ppermute | solution.py:19
  624.5 0.9 copy-start.22
Sparse Core Ops, SparseCore 0:
  625.5 345.0 all-reduce.9
where the time goes:
time: 993 us; the launch traced here: 980 us
  waiting for transfers between devices  363 us (37%)
  matrix products  213 us (21%)
  blocking collectives  185 us (19%)
  local copies, waits for them, and re-layouts  116 us (12%)
  starting transfers between devices  51.2 us (5%)
  other arithmetic  37 us (4%)
  between operations  15.1 us (2%)
    psum x1, waiting for transfers between devices, per_device(): lax.psum(local_dec.astype(jnp.bfloat16), 'band').astype(jnp.float32)  321 us
    conv_general_dilated x10, matrix products, conv_valid(): lax.conv_general_dilated(field, kernel, (1,) * spatial, 'VALID', dimensio...  186 us
    psum x1, blocking collectives, per_device(): lax.psum(local_rgb.astype(jnp.bfloat16), 'band').astype(jnp.float32)  185 us
    conv_general_dilated x36, local copies, waits for them, and re-layouts, conv_valid(): lax.conv_general_dilated(field, kernel, (1,) * spatial, 'VALID', dimensio...  60 us
    ppermute x9, starting transfers between devices, with_halo(): before = lax.ppermute(last, axis, up)  39.2 us
    dot_general x54, matrix products, kernel_grad(): jnp.einsum('fhwi,fhwo->io', window, grad_out, preferred_element_type=jnp....  25.2 us
    unnamed x81, local copies, waits for them, and re-layouts  23.3 us
    ppermute x9, waiting for transfers between devices, with_halo(): before = lax.ppermute(last, axis, up)  22.1 us
  transfers between devices with their start and end apart: 19, of which 10 were waited for; matrix products, arithmetic and copies ran while one was open for 14% of the time, Pallas kernels for 0%

commit v1 on v0

v1 whole, which is shorter than its diff:
```python
import jax
import jax.numpy as jnp
from jax import lax
from jax.experimental import pallas as pl
from jax.experimental.pallas import tpu as pltpu
from jax.sharding import PartitionSpec as P

F32 = jnp.float32
BF16 = jnp.bfloat16
HALO = 4


def sigmoid(value):
    return 0.5 * jnp.tanh(0.5 * value) + 0.5


def slope_of(value, gate):
    return gate * (1.0 + value * (1.0 - gate))


def dot(left, right, contract=((1,), (0,))):
    return lax.dot_general(left, right, (contract, ((), ())), preferred_element_type=F32)


def call(kernel, outs, *args, scratch=(), macs=0):
    moved = sum(a.size * a.dtype.itemsize for a in args)
    moved += sum(o.size * o.dtype.itemsize for o in outs)
    return pl.pallas_call(
        kernel,
        out_shape=outs,
        in_specs=[pl.BlockSpec(memory_space=pltpu.VMEM)] * len(args),
        out_specs=[pl.BlockSpec(memory_space=pltpu.VMEM)] * len(outs),
        scratch_shapes=list(scratch),
        compiler_params=pltpu.CompilerParams(vmem_limit_bytes=48 * 1024 * 1024),
        cost_estimate=pl.CostEstimate(flops=2 * macs, bytes_accessed=moved, transcendentals=0),
    )(*args)


def shape(dims, dtype):
    return jax.ShapeDtypeStruct(dims, dtype)


def before(value):
    row = lax.broadcasted_iota(jnp.int32, value.shape, 0)
    return jnp.where(row >= 1, pltpu.roll(value, 1, 0), 0.0)


def after(value):
    size = value.shape[0]
    row = lax.broadcasted_iota(jnp.int32, value.shape, 0)
    return jnp.where(row < size - 1, pltpu.roll(value, size - 1, 0), 0.0)


def weights_kernel(dec, rgb, own, edge, own_t, edge_t, colour, scr):
    edge[...] = jnp.zeros_like(edge)
    edge_t[...] = jnp.zeros_like(edge_t)
    for a in range(3):
        for e in range(3):
            tap = [dec[(a * 3 + b) * 3 + e] for b in range(3)]
            for j in range(2):
                for r in range(2):
                    one, two = (a * 256 + j * 128, e * 256 + r * 128)
                    own[one : one + 128, two : two + 128] = tap[j - r + 1]
                    one, two = (e * 256 + j * 128, a * 256 + r * 128)
                    own_t[one : one + 128, two : two + 128] = tap[j - r + 1]
                one, two = (a * 256 + j * 128, e * 256 + j * 128)
                edge[one : one + 128, two : two + 128] = tap[2 * j]
                edge_t[two : two + 128, one : one + 128] = tap[2 - 2 * j]
    scr[...] = jnp.zeros_like(scr)
    for f in range(4):
        for r in range(2):
            lanes = slice((f * 2 + r) * 128, (f * 2 + r + 1) * 128)
            for a in range(3):
                to = f - a + 1
                if not 0 <= to < 4:
                    continue
                for e in range(3):
                    at = e * 128 + to * 12 + r * 3
                    scr[at : at + 9, lanes] = rgb[a * 3 + e]
    colour[...] = scr[...].astype(BF16)


def frames_of(f, step):
    return [(a, f + step * (a - 1)) for a in range(3) if 0 <= f + step * (a - 1) < 4]


def conv_rows(first, second, kernel, f):
    taps = frames_of(f, 1)
    left = jnp.concatenate([half[g] for _, g in taps for half in (first, second)], axis=1)
    wide = dot(left, kernel[taps[0][0] * 256 : (taps[-1][0] + 1) * 256, :])
    return before(wide[:, :256]) + wide[:, 256:512] + after(wide[:, 512:])


def conv_rows_t(first, second, kernel, f):
    taps = frames_of(f, -1)
    left = jnp.concatenate([half[g] for _, g in taps for half in (first, second)], axis=1)
    lanes = slice(taps[0][0] * 256, (taps[-1][0] + 1) * 256)
    wide = dot(left, kernel[:, lanes], ((1,), (1,)))
    return after(wide[:, :256]) + wide[:, 256:512] + before(wide[:, 512:])


def dec_own_kernel(zero, one, kernel, out):
    for f in range(4):
        out[f] = conv_rows(zero, one, kernel, f)


def dec_edge_kernel(above, below, kernel, own, colour, target, act, slope, parts, t_scr, p_scr):
    cols = act.shape[0]
    for f in range(4):
        pre = own[f] + conv_rows(above, below, kernel, f)
        gate = sigmoid(pre)
        act[:, f * 256 : (f + 1) * 256] = (pre * gate).astype(BF16)
        slope[f] = slope_of(pre, gate)
    wide = dot(act[...], colour[...], ((1,), (1,)))
    part = before(wide[:, :128]) + wide[:, 128:256] + after(wide[:, 256:])
    t_scr[...] = jnp.zeros_like(t_scr)
    t_scr[48:72, :] = target[...].astype(F32)
    p_scr[0:8, :] = jnp.zeros((8, 128), F32)
    p_scr[cols : cols + 8, :] = jnp.zeros((8, 128), F32)
    p_scr[HALO : HALO + cols, :] = part + t_scr[...].T
    blocks, width, _ = parts.shape
    for d in range(blocks):
        start = d * (width - 2 * HALO)
        parts[d] = p_scr[start : start + width, :]


def branch_kernel(parts, mask_ref, w1, w2, w2_t, w1_t, head, out, tap_scr, e_scr, im_scr, acc, g_scr):
    blocks, wide, _ = parts.shape
    lanes = blocks * wide
    lane = lax.broadcasted_iota(jnp.int32, (1, lanes), 1)
    mask = mask_ref[0:1, :]
    lo, hi = (lane >= wide, lane < lanes - wide)

    def down(value):
        return jnp.where(lo, pltpu.roll(value, wide, 1), 0.0)

    def up(value):
        return jnp.where(hi, pltpu.roll(value, lanes - wide, 1), 0.0)

    def left(value):
        return pltpu.roll(value, 1, 1)

    def right(value):
        return pltpu.roll(value, lanes - 1, 1)

    def rounded(value):
        return value.astype(BF16).astype(F32)

    turned = parts[...].reshape(lanes, 128).T
    g_scr[...] = turned
    e_scr[...] = jnp.zeros_like(e_scr)
    tap_scr[0:64, :] = jnp.zeros((64, lanes), BF16)
    tap_scr[320:384, :] = jnp.zeros((64, lanes), BF16)

    def place(at, even, odd):
        for k, value in enumerate((even, odd)):
            e_scr[k, 0:3, :] = left(value)
            e_scr[k, 3:6, :] = value
            e_scr[k, 6:9, :] = right(value)
        even, odd = (e_scr[0], e_scr[1])
        tap_scr[at : at + 16, :] = down(odd).astype(BF16)
        tap_scr[at + 16 : at + 32, :] = even.astype(BF16)
        tap_scr[at + 32 : at + 48, :] = odd.astype(BF16)
        tap_scr[at + 48 : at + 64, :] = up(even).astype(BF16)

    for f in range(4):
        at = f * 12
        even = g_scr[at + 3 : at + 6, :] + down(g_scr[at + 9 : at + 12, :])
        odd = g_scr[at + 6 : at + 9, :] + up(g_scr[at : at + 3, :])
        place(64 + f * 64, rounded(even * mask), rounded(odd * mask))
        at = 48 + f * 6
        place(384 + f * 64, g_scr[at : at + 3, :] * mask, g_scr[at + 3 : at + 6, :] * mask)
    acc[...] = jnp.zeros_like(acc)

    def second(feat):
        for e, moved in enumerate((left(feat), feat, right(feat))):
            at = e * 256
            im_scr[at : at + 64, :] = down(moved[64:]).astype(BF16)
            im_scr[at + 64 : at + 192, :] = moved.astype(BF16)
            im_scr[at + 192 : at + 256, :] = up(moved[:64]).astype(BF16)
        return dot(w2[...], im_scr[...])

    def one_frame(f, carry):
        at = pl.multiple_of(f * 64, 64)
        pre = dot(w1[0:128, 64:128], tap_scr[pl.ds(at + 384, 64), :])
        pre_two = second(rounded(pre * sigmoid(pre) * mask))
        wanted = pre_two * sigmoid(pre_two)
        both = dot(w1[...], tap_scr[pl.ds(at, 192), :])
        pre_vone, crit = (both[:128], both[128:])
        gate = sigmoid(pre_vone)
        slope_one = slope_of(pre_vone, gate) * mask
        pre_two = second(rounded(pre_vone * gate * mask))
        gate = sigmoid(pre_two)
        gap = pre_two * gate - wanted
        grad_two = (0.25 * gap * slope_of(pre_two, gate) * mask).astype(BF16)
        spread = dot(w2_t[...], grad_two)
        rows = []
        for rr in range(4):
            at_r = rr * 64
            rows.append(
                right(spread[at_r : at_r + 64])
                + spread[256 + at_r : 320 + at_r]
                + left(spread[512 + at_r : 576 + at_r])
            )
        back = jnp.concatenate([rows[1] + down(rows[3]), rows[2] + up(rows[0])], axis=0)
        grad_one = (back * slope_one).astype(BF16)
        gate = sigmoid(crit)
        scored = crit * gate * head[...]
        slope_c = slope_of(crit, gate) * head[...] * mask
        grads = []
        for r in range(2):
            logits = jnp.sum(scored[r * 64 : (r + 1) * 64], axis=0, keepdims=True)
            grads.append(-sigmoid(-logits) * slope_c[r * 64 : (r + 1) * 64])
        grad_crit = jnp.concatenate(grads, axis=0).astype(BF16)
        spread = dot(w1_t[...], jnp.concatenate([grad_one, grad_crit], axis=0))
        for a in range(3):
            acc[f + a] += spread[a * 64 : (a + 1) * 64]
        return carry

    lax.fori_loop(0, 4, one_frame, 0)
    g_scr[...] = jnp.zeros_like(g_scr)
    for f in range(4):
        field = acc[f + 1]
        e_scr[0] = field[16:32] + down(field[48:64])
        e_scr[1] = field[32:48] + up(field[0:16])
        even, odd = [
            rounded(right(e_scr[k, 0:3, :]) + e_scr[k, 3:6, :] + left(e_scr[k, 6:9, :]))
            for k in range(2)
        ]
        at = f * 12
        for k, value in enumerate((down(odd), even, odd, up(even))):
            g_scr[at + 3 * k : at + 3 * k + 3, :] = pltpu.roll(value, lanes - HALO, 1)
    back = g_scr[...].T.reshape(blocks, wide, 128)
    out[...] = back[:, : wide - 2 * HALO].astype(BF16)


def pre_kernel(grad_in, colour, slope, act, zero, one, moved, rgb_out, gram):
    cols = act.shape[0]
    grad = grad_in[...].reshape(cols, 128).astype(F32)
    taps = jnp.concatenate([after(grad), grad, before(grad)], axis=1).astype(BF16)
    grad_act = dot(taps, colour[...])
    lane = lax.broadcasted_iota(jnp.int32, (1, cols), 1)
    for f in range(4):
        pre = (grad_act[:, f * 256 : (f + 1) * 256] * slope[f]).astype(BF16)
        zero[f] = pre[:, :128]
        one[f] = pre[:, 128:]
        turned = pre.astype(F32).T
        later = jnp.where(lane < cols - 1, pltpu.roll(turned, cols - 1, 1), 0.0)
        sooner = jnp.where(lane >= 1, pltpu.roll(turned, 1, 1), 0.0)
        for e, value in enumerate((later, turned, sooner)):
            moved[e * 256 : (e + 1) * 256, f * cols : (f + 1) * cols] = value.astype(BF16)
    gram[...] = dot(taps.astype(F32).T.astype(BF16), act[...])
    for a in range(3):
        for e in range(3):
            total = jnp.zeros((9, 128), F32)
            for f in range(4):
                to = f - a + 1
                if not 0 <= to < 4:
                    continue
                for r in range(2):
                    at = e * 128 + to * 12 + r * 3
                    total += gram[at : at + 9, (f * 2 + r) * 128 : (f * 2 + r + 1) * 128]
            for b in range(3):
                at = ((a * 3 + b) * 3 + e) * 3
                rgb_out[at : at + 3, :] = total[(2 - b) * 3 : (2 - b) * 3 + 3]


def dec_grad_kernel(moved, zero, one, above, below, rgb_grad, out, field):
    cols = zero.shape[1]
    for f in range(4):
        for k, part in enumerate((above, zero, one, below)):
            field[f * cols : (f + 1) * cols, k * 128 : (k + 1) * 128] = part[f]
    for a in range(3):
        lo, hi = (max(0, 1 - a), min(4, 5 - a))
        first, last = (lo * cols, hi * cols)
        skip = (a - 1) * cols
        for e in range(3):
            gram = dot(
                moved[e * 256 : (e + 1) * 256, first:last],
                field[first + skip : last + skip, :],
            )
            for b in range(3):
                total = gram[:128, b * 128 : b * 128 + 128] + gram[128:, b * 128 + 128 : b * 128 + 256]
                at = ((a * 3 + b) * 3 + e) * 128
                out[at : at + 128, :] = total.T.astype(BF16)
    out[27 * 128 :, :] = rgb_grad[...].astype(BF16)


def lat_own_kernel(zero, one, kernel, out):
    for f in range(4):
        wide = conv_rows_t(zero, one, kernel, f)
        out[f, 0] = wide[:, :128]
        out[f, 1] = wide[:, 128:]


def lat_edge_kernel(above, below, kernel, own, out):
    for f in range(4):
        wide = conv_rows_t(above, below, kernel, f)
        out[f, 0] = own[f, 0] + wide[:, :128]
        out[f, 1] = own[f, 1] + wide[:, 128:]


def branch_weights(vgg_first, vgg_second, critic):
    def paired(taps):
        none = jnp.zeros_like(taps[..., :1, :, :])
        return jnp.stack(
            [jnp.concatenate([taps, none], -3), jnp.concatenate([none, taps], -3)], axis=-4
        )

    def nine(taps):
        flat = taps.reshape(taps.shape[:-3] + (9, taps.shape[-1]))
        edges = [(0, 0)] * (flat.ndim - 2) + [(0, 7), (0, 0)]
        return jnp.pad(flat, edges)

    first = paired(nine(vgg_first))
    none = jnp.zeros_like(first)
    first = jnp.stack([none, first, none])
    crit = paired(nine(critic))
    w1_t = jnp.stack([first, crit])
    w1_t = w1_t.transpose(1, 3, 4, 0, 2, 5).reshape(192, 256)
    w2_t = paired(vgg_second.transpose(1, 0, 2, 3))
    w2_t = w2_t.transpose(0, 2, 3, 1, 4).reshape(768, 256)
    return (w1_t.T, w2_t.T, w2_t, w1_t)


def per_device(
    latent, dec_kernel, rgb_kernel, target, vgg_first, vgg_second, critic_kernel, critic_head
):
    size = lax.axis_size("band")
    me = lax.axis_index("band")
    cols = latent.shape[2]
    width = cols // size
    wide = width + 2 * HALO
    up = [(i, i + 1) for i in range(size - 1)]
    down = [(i + 1, i) for i in range(size - 1)]

    def neighbours(zero, one):
        return (lax.ppermute(one, "band", up), lax.ppermute(zero, "band", down))

    zero, one = (latent[:, 0], latent[:, 1])
    above, below = neighbours(zero, one)
    rgb = rgb_kernel.transpose(0, 2, 1, 4, 3)[:, :, ::-1].reshape(9, 9, 128).astype(F32)
    square = shape((768, 768), BF16)
    own_w, edge_w, own_wt, edge_wt, colour = call(
        weights_kernel,
        [square, square, square, square, shape((384, 1024), BF16)],
        dec_kernel.reshape(27, 128, 128),
        rgb,
        scratch=[pltpu.VMEM((384, 1024), F32)],
    )
    w1, w2, w2_t, w1_t = branch_weights(vgg_first, vgg_second, critic_kernel)
    head = jnp.concatenate([critic_head, critic_head]).reshape(128, 1)
    place = jnp.arange(size * wide) % wide + me * width - HALO
    mask = jnp.where((place >= 0) & (place < cols), 1.0, 0.0).astype(F32)
    mask = jnp.broadcast_to(mask, (8, size * wide))

    big = 4 * cols * 768 * 640
    (pre_own,) = call(dec_own_kernel, [shape((4, cols, 256), F32)], zero, one, own_w, macs=big)
    act, slope, parts = call(
        dec_edge_kernel,
        [
            shape((cols, 1024), BF16),
            shape((4, cols, 256), F32),
            shape((size, wide, 128), F32),
        ],
        above,
        below,
        edge_w,
        pre_own,
        colour,
        target.transpose(0, 1, 3, 2).reshape(24, cols),
        scratch=[pltpu.VMEM((128, cols), F32), pltpu.VMEM((cols + 8, 128), F32)],
        macs=big,
    )
    parts = lax.all_to_all(parts, "band", 0, 0)
    lanes = size * wide
    (grad_frames,) = call(
        branch_kernel,
        [shape((size, width, 128), BF16)],
        parts,
        mask,
        w1,
        w2,
        w2_t,
        w1_t,
        head,
        scratch=[
            pltpu.VMEM((640, lanes), BF16),
            pltpu.VMEM((2, 16, lanes), F32),
            pltpu.VMEM((768, lanes), BF16),
            pltpu.VMEM((6, 64, lanes), F32),
            pltpu.VMEM((128, lanes), F32),
        ],
        macs=4 * 768 * 768 * 700,
    )
    grad_frames = lax.all_to_all(grad_frames, "band", 0, 0)
    half = shape((4, cols, 128), BF16)
    grad_zero, grad_one, moved, rgb_grad = call(
        pre_kernel,
        [half, half, shape((768, 4 * cols), BF16), shape((128, 128), F32)],
        grad_frames,
        colour,
        slope,
        act,
        scratch=[pltpu.VMEM((384, 1024), F32)],
        macs=2 * cols * 384 * 1024,
    )
    grad_above, grad_below = neighbours(grad_zero, grad_one)
    (local,) = call(
        dec_grad_kernel,
        [shape((28 * 128, 128), BF16)],
        moved,
        zero,
        one,
        above,
        below,
        rgb_grad,
        scratch=[pltpu.VMEM((4 * cols, 512), BF16)],
        macs=2 * big,
    )
    (lat_own,) = call(
        lat_own_kernel, [shape((4, 2, cols, 128), F32)], grad_zero, grad_one, own_wt, macs=big
    )
    (grad_latent,) = call(
        lat_edge_kernel,
        [shape((4, 2, cols, 128), F32)],
        grad_above,
        grad_below,
        edge_wt,
        lat_own,
        macs=big,
    )
    pieces = lax.all_to_all(local.reshape(size, -1, 128), "band", 0, 0)
    mine = jnp.sum(pieces.astype(F32), axis=0).astype(BF16)
    whole = lax.all_to_all(jnp.broadcast_to(mine, (size,) + mine.shape), "band", 0, 0)
    whole = whole.reshape(28 * 128, 128)
    pixels = 4 * latent.shape[1] * size * cols
    factor = float(pixels) ** (-0.5)
    grad_dec = whole[: 27 * 128].astype(F32).reshape(3, 3, 3, 128, 128) * factor
    grad_rgb = whole[27 * 128 : 27 * 128 + 81].astype(F32).reshape(3, 3, 3, 3, 128) * factor
    return (grad_latent, grad_dec, grad_rgb.transpose(0, 1, 2, 4, 3))


def solution(mesh):
    placed = (
        P("clip", "band", None, None),
        P(),
        P(),
        P("clip", "band", None, None),
        P(),
        P(),
        P(),
        P(),
    )
    return jax.shard_map(
        per_device,
        mesh=mesh,
        in_specs=placed,
        out_specs=(
            P("clip", "band", None, None),
            P("clip", None, None, None, None),
            P("clip", None, None, None, None),
        ),
        check_vma=False,
    )
```

time: 993 us -> 148 us (0.15); the launches traced: 980 us -> 145 us
  waiting for transfers between devices: 363 us -> 28.4 us
  matrix products: 213 us -> 0 us
  blocking collectives: 185 us -> 31 us
  local copies, waits for them, and re-layouts: 116 us -> 14.4 us
  Pallas kernels: 0 us -> 39.3 us
  other arithmetic: 37 us -> 2.89 us
  starting transfers between devices: 51.2 us -> 28.4 us
  between operations: 15.1 us -> 1.01 us
    psum x1 -> x0, waiting for transfers between devices: 321 us -> none  [per_device(): lax.psum(local_dec.astype(jnp.bfloat16), 'band').astype(jnp.float32)]
    conv_general_dilated x10 -> x0, matrix products: 186 us -> none  [conv_valid(): lax.conv_general_dilated(field, kernel, (1,) * spatial, 'VALID', dimensio...]
    psum x1 -> x0, blocking collectives: 185 us -> none  [per_device(): lax.psum(local_rgb.astype(jnp.bfloat16), 'band').astype(jnp.float32)]
    conv_general_dilated x36 -> x0, local copies, waits for them, and re-layouts: 60 us -> none  [conv_valid(): lax.conv_general_dilated(field, kernel, (1,) * spatial, 'VALID', dimensio...]
    ppermute x18 -> x4, starting transfers between devices: 51.1 us -> 11 us  [neighbours(): return (lax.ppermute(one, 'band', up), lax.ppermute(zero, 'band', down))]
    pallas_call x0 -> x8, Pallas kernels: none -> 39.3 us  [call(): pl.pallas_call(kernel, out_shape=outs, in_specs=[pl.BlockSpec(memory_spac...]
    all_to_all x0 -> x2, blocking collectives: none -> 31 us  [the longest x1 17.1 us: per_device(): pieces = lax.all_to_all(local.reshape(size, -1, 128), 'band', 0, 0)]
    dot_general x55 -> x0, matrix products: 27.5 us -> none  [the longest x54 25.2 us: kernel_grad(): jnp.einsum('fhwi,fhwo->io', window, grad_out, preferred_element_type=jnp....]
  transfers between devices with their start and end apart: 19 -> 6, of which waited for: 10 -> 5; matrix products, arithmetic and copies ran while one was open for 14% -> 3% of each run, Pallas kernels for 0% -> 7%
where the time goes in v1:
time: 148 us; the launch traced here: 145 us
  Pallas kernels  39.3 us (27%)
  blocking collectives  31 us (21%)
  starting transfers between devices  28.4 us (19%)
  waiting for transfers between devices  28.4 us (19%)
  local copies, waits for them, and re-layouts  14.4 us (10%)
  other arithmetic  2.89 us (2%)
    pallas_call x8, Pallas kernels, call(): pl.pallas_call(kernel, out_shape=outs, in_specs=[pl.BlockSpec(memory_spac...  39.3 us
    ppermute x4, waiting for transfers between devices, neighbours(): return (lax.ppermute(one, 'band', up), lax.ppermute(zero, 'band', down))  21 us
    all_to_all x1, blocking collectives, per_device(): pieces = lax.all_to_all(local.reshape(size, -1, 128), 'band', 0, 0)  17.1 us
    all_to_all x1, blocking collectives, per_device(): grad_frames = lax.all_to_all(grad_frames, 'band', 0, 0)  13.9 us
    all_to_all x1, starting transfers between devices, per_device(): parts = lax.all_to_all(parts, 'band', 0, 0)  13 us
    ppermute x4, starting transfers between devices, neighbours(): return (lax.ppermute(one, 'band', up), lax.ppermute(zero, 'band', down))  11 us
    unnamed x41, local copies, waits for them, and re-layouts  7.79 us
    all_to_all x1, waiting for transfers between devices, per_device(): parts = lax.all_to_all(parts, 'band', 0, 0)  7.34 us
  transfers between devices with their start and end apart: 6, of which 5 were waited for; matrix products, arithmetic and copies ran while one was open for 3% of the time, Pallas kernels for 7%

profile of v1, /device:TPU:0, one launch (start us, length us, event | category | flops | bytes accessed | tf_op | source)
XLA Modules:
  0.0 145.4 jit_solution(16355535552630569879)
XLA Ops:
  0.6 0.0 copy-start.15
  0.6 0.0 copy-start.16
  0.7 0.0 copy-start.17
  0.7 0.0 copy-start.14
  0.7 0.0 copy-start.1
  0.7 0.0 copy-start.13
  0.7 1.4 slice_bitcast_fusion
  2.1 4.7 %collective-permute-start = (bf16[4,512,128]{2,1,0:T(8,128)(2,1)S(1)}, bf16[4,512,128]{2,1,0:T(8,128)(2,1)}, u32[]{:S(2)}, u32[]{:S(2)}) collective-permute-start(bf16[4,512,128]{2,1,0:T(8,128)(2,1)S(1)} %get-tuple-element.28.one), channel_id=1, source_target_pairs={{0,4},{4,8},{8,12},{12,16},{16,20},{20,24},{24,28},{28,32},{32,36}... | collective-permute-start | bytes 1572872 | tf_op jit(solution)/shard_map/ppermute | solution.py:338
  6.8 1.3 collective-permute-start.1
  8.1 0.0 copy-done.15
  8.1 0.0 copy-done.16
  8.2 0.0 copy-done.17
  8.3 0.0 copy-done.14
  8.3 0.1 pad_bitcast_fusion.3
  8.4 0.0 copy-done.1
  8.4 1.6 %shard_map.103 = (bf16[768,768]{1,0:T(8,128)(2,1)S(1)}, bf16[768,768]{1,0:T(8,128)(2,1)S(1)}, bf16[768,768]{1,0:T(8,128)(2,1)S(1)}, bf16[768,768]{1,0:T(8,128)(2,1)}, bf16[384,1024]{1,0:T(8,128)(2,1)S(1)}) custom-call(bf16[27,128,128]{2,1,0:T(8,128)(2,1)S(1)} %bitcast.57, f32[9,9,128]{2,1,0:T(8,128)S(1)} %reshape.51.rgb), custom_call_target="tpu_custom_call" | custom-call | bytes 6431232 | tf_op jit(solution)/shard_map/pallas_call | solution.py:28
  10.0 1.0 copy-done.6
  11.1 0.2 maximum_bitcast_fusion.2
  11.3 0.0 copy-done.13
  11.3 0.8 pad_bitcast_fusion.1
  12.1 2.2 %shard_map.104.own = f32[4,512,256]{2,1,0:T(8,128)S(1)} custom-call(bf16[4,512,128]{2,1,0:T(8,128)(2,1)S(1)} %get-tuple-element.27.zero, bf16[4,512,128]{2,1,0:T(8,128)(2,1)S(1)} %get-tuple-element.28.one, bf16[768,768]{1,0:T(8,128)(2,1)S(1)} %get-tuple-element.16.kernel), custom_call_target="tpu_custom_call" | custom-call | flops 2013265920 | bytes 4325376 | tf_op jit(solution)/shard_map/pallas_call | solution.py:28
  14.3 0.0 copy-start.12
  14.3 1.3 copy-done.12
  15.6 1.5 %collective-permute-done.above = bf16[4,512,128]{2,1,0:T(8,128)(2,1)} collective-permute-done((bf16[4,512,128]{2,1,0:T(8,128)(2,1)S(1)}, bf16[4,512,128]{2,1,0:T(8,128)(2,1)}, u32[]{:S(2)}, u32[]{:S(2)}) %collective-permute-start) | collective-permute-done | bytes 524320 | tf_op jit(solution)/shard_map/ppermute | solution.py:338
  17.1 5.0 %collective-permute-done.1.below = bf16[4,512,128]{2,1,0:T(8,128)(2,1)} collective-permute-done((bf16[4,512,128]{2,1,0:T(8,128)(2,1)S(1)}, bf16[4,512,128]{2,1,0:T(8,128)(2,1)}, u32[]{:S(2)}, u32[]{:S(2)}) %collective-permute-start.1) | collective-permute-done | bytes 524320 | tf_op jit(solution)/shard_map/ppermute | solution.py:338
  22.1 6.4 %shard_map.105 = (bf16[512,1024]{1,0:T(8,128)(2,1)S(1)}, f32[4,512,256]{2,1,0:T(8,128)}, f32[32,24,128]{2,1,0:T(8,128)}) custom-call(bf16[4,512,128]{2,1,0:T(8,128)(2,1)} %collective-permute-done.above, bf16[4,512,128]{2,1,0:T(8,128)(2,1)} %collective-permute-done.1.below, bf16[768,768]{1,0:T(8,128)(2,1)S(1)} %get-tuple-element.15.kernel, ...), custom_call_target="tpu_custom_call" | custom-call | flops 2013265920 | bytes 8675328 | tf_op jit(solution)/shard_map/pallas_call | solution.py:28
  28.6 13.0 %all-to-all-start = ((f32[32,24,128]{2,1,0:T(8,128)}), f32[32,24,128]{2,1,0:T(8,128)}, u32[]{:S(2)}, u32[]{:S(2)}) async-start(f32[32,24,128]{2,1,0:T(8,128)} %get-tuple-element.18), calls=%async_computation | async-start | bytes 786432 | tf_op jit(solution)/shard_map/all_to_all | solution.py:375
  41.6 0.2 maximum_bitcast_fusion.1
  41.8 0.2 copy.31
  42.0 0.0 copy-start.18
  42.0 0.2 reshape.46.w1_t
  42.2 0.1 copy.33.w1
  42.3 1.0 maximum_bitcast_fusion
  43.3 0.4 copy.32
  43.7 0.1 copy.45
  43.7 0.9 copy.34.w2
  44.7 0.0 copy-done.18
  44.7 0.1 maximum_bitcast_fusion.5
  44.7 0.7 copy.35.head
  45.5 7.3 %all-to-all-done.parts = f32[32,24,128]{2,1,0:T(8,128)} async-done(((f32[32,24,128]{2,1,0:T(8,128)}), f32[32,24,128]{2,1,0:T(8,128)}, u32[]{:S(2)}, u32[]{:S(2)}) %all-to-all-start) | async-done | bytes 393248 | tf_op jit(solution)/shard_map/all_to_all | solution.py:375
  52.8 1.0 copy-done.2
  53.8 0.8 copy-done.3
  54.7 14.5 %shard_map.106 = bf16[32,16,128]{2,1,0:T(8,128)(2,1)S(1)} custom-call(f32[32,24,128]{2,1,0:T(8,128)} %all-to-all-done.parts, f32[8,768]{1,0:T(8,128)S(1)} %broadcast_in_dim.19.mask_ref, bf16[256,192]{1,0:T(8,128)(2,1)S(1)} %copy.33.w1, bf16[256,768]{1,0:T(8,128)(2,1)S(1)} %copy-done.2, bf16[768,256]{1,0:T(8,128)(2,1)S(1)} %bitcast.55, ...), custom_call_target="tpu_custom_call" | custom-call | flops 3303014400 | bytes 1532416 | tf_op jit(solution)/shard_map/pallas_call | solution.py:28
  69.1 13.9 %all_to_all.20.grad_in = bf16[32,16,128]{2,1,0:T(8,128)(2,1)S(1)} all-to-all(bf16[32,16,128]{2,1,0:T(8,128)(2,1)S(1)} %shard_map.106), channel_id=1, replica_groups=mesh['band'=32,'clip'=4] {'band'}, dimensions={0} | all-to-all | bytes 262144 | tf_op jit(solution)/shard_map/all_to_all | solution.py:396
  83.0 0.0 copy-done
  83.0 3.2 %shard_map.107 = (bf16[4,512,128]{2,1,0:T(8,128)(2,1)S(1)}, bf16[4,512,128]{2,1,0:T(8,128)(2,1)S(1)}, bf16[768,2048]{1,0:T(8,128)(2,1)}, f32[128,128]{1,0:T(8,128)S(1)}) custom-call(bf16[32,16,128]{2,1,0:T(8,128)(2,1)S(1)} %all_to_all.20.grad_in, bf16[384,1024]{1,0:T(8,128)(2,1)S(1)} %get-tuple-element.17.colour, f32[4,512,256]{2,1,0:T(8,128)S(1)} %copy-done, ...), custom_call_target="tpu_custom_call" | custom-call | flops 805306368 | bytes 8323072 | tf_op jit(solution)/shard_map/pallas_call | solution.py:28
  86.2 0.8 copy-done.8
  87.0 0.8 copy-done.10
  87.8 1.9 %copy-done.4 = bf16[768,2048]{1,0:T(8,128)(2,1)S(1)} copy-done((bf16[768,2048]{1,0:T(8,128)(2,1)S(1)}, bf16[768,2048]{1,0:T(8,128)(2,1)}, u32[]{:S(2)}) %copy-start.4) | copy-done | bytes 3145752
  89.7 5.6 %shard_map.110 = bf16[3584,128]{1,0:T(8,128)(2,1)S(1)} custom-call(bf16[768,2048]{1,0:T(8,128)(2,1)S(1)} %copy-done.4, bf16[4,512,128]{2,1,0:T(8,128)(2,1)S(1)} %get-tuple-element.27.zero, bf16[4,512,128]{2,1,0:T(8,128)(2,1)S(1)} %get-tuple-element.28.one, bf16[4,512,128]{2,1,0:T(8,128)(2,1)} %collective-permute-done.above, ...), custom_call_target="tpu_custom_call" | custom-call | flops 4026531840 | bytes 6225920 | tf_op jit(solution)/shard_map/pallas_call | solution.py:28
  95.3 17.1 %all_to_all.21 = bf16[32,112,128]{2,1,0:T(8,128)(2,1)S(1)} all-to-all(bf16[32,112,128]{2,1,0:T(8,128)(2,1)S(1)} %bitcast.56), channel_id=1, replica_groups=mesh['band'=32,'clip'=4] {'band'}, dimensions={0} | all-to-all | bytes 1835008 | tf_op jit(solution)/shard_map/all_to_all | solution.py:433
  112.4 0.1 reduce_sum.12
  112.6 1.1 broadcast_in_dim.20
  113.6 4.4 %all-to-all-start.3 = ((bf16[32,112,128]{2,1,0:T(8,128)(2,1)}), bf16[32,112,128]{2,1,0:T(8,128)(2,1)S(1)}, u32[]{:S(2)}, u32[]{:S(2)}) async-start(bf16[32,112,128]{2,1,0:T(8,128)(2,1)} %broadcast_in_dim.20), calls=%async_computation.3 | async-start | bytes 1835008 | tf_op jit(solution)/shard_map/all_to_all | solution.py:435
  118.0 3.7 %collective-permute-start.2 = (bf16[4,512,128]{2,1,0:T(8,128)(2,1)S(1)}, bf16[4,512,128]{2,1,0:T(8,128)(2,1)S(1)}, u32[]{:S(2)}, u32[]{:S(2)}) collective-permute-start(bf16[4,512,128]{2,1,0:T(8,128)(2,1)S(1)} %copy-done.11), channel_id=1, source_target_pairs={{0,4},{4,8},{8,12},{12,16},{16,20},{20,24},{24,28},{28,32},{32,36}... | collective-permute-start | bytes 1572872 | tf_op jit(solution)/shard_map/ppermute | solution.py:338
  121.7 1.3 collective-permute-start.3
  123.1 0.0 copy-start.5
  123.1 2.2 %shard_map.108.own = f32[4,2,512,128]{3,2,1,0:T(8,128)S(1)} custom-call(bf16[4,512,128]{2,1,0:T(8,128)(2,1)S(1)} %copy-done.9, bf16[4,512,128]{2,1,0:T(8,128)(2,1)S(1)} %copy-done.11, bf16[768,768]{1,0:T(8,128)(2,1)S(1)} %copy-done.7), custom_call_target="tpu_custom_call" | custom-call | flops 2013265920 | bytes 4325376 | tf_op jit(solution)/shard_map/pallas_call | solution.py:28
  125.3 11.6 %collective-permute-done.2.above = bf16[4,512,128]{2,1,0:T(8,128)(2,1)S(1)} collective-permute-done((bf16[4,512,128]{2,1,0:T(8,128)(2,1)S(1)}, bf16[4,512,128]{2,1,0:T(8,128)(2,1)S(1)}, u32[]{:S(2)}, u32[]{:S(2)}) %collective-permute-start.2) | collective-permute-done | bytes 524320 | tf_op jit(solution)/shard_map/ppermute | solution.py:338
  136.9 2.9 %collective-permute-done.3.below = bf16[4,512,128]{2,1,0:T(8,128)(2,1)S(1)} collective-permute-done((bf16[4,512,128]{2,1,0:T(8,128)(2,1)S(1)}, bf16[4,512,128]{2,1,0:T(8,128)(2,1)S(1)}, u32[]{:S(2)}, u32[]{:S(2)}) %collective-permute-start.3) | collective-permute-done | bytes 524320 | tf_op jit(solution)/shard_map/ppermute | solution.py:338
  139.8 3.6 %shard_map.109 = f32[4,2,512,128]{3,2,1,0:T(8,128)} custom-call(bf16[4,512,128]{2,1,0:T(8,128)(2,1)S(1)} %collective-permute-done.2.above, bf16[4,512,128]{2,1,0:T(8,128)(2,1)S(1)} %collective-permute-done.3.below, bf16[768,768]{1,0:T(8,128)(2,1)S(1)} %copy-done.5, f32[4,2,512,128]{3,2,1,0:T(8,128)S(1)} %shard_map.108.own), custom_call_target="tpu_custom_call" | custom-call | flops 2013265920 | bytes 6422528 | tf_op jit(solution)/shard_map/pallas_call | solution.py:28
  143.4 0.0 all-to-all-done.3
  143.4 1.3 convert_multiply_fusion
  144.7 0.6 mul.27
  (29 shorter events, 0.3 us)
Async XLA Ops:
  0.6 7.4 %copy-start.15 = (bf16[3,3,3,128,3]{3,4,2,1,0:T(4,128)(2,1)S(1)}, bf16[3,3,3,128,3]{3,4,2,1,0:T(4,128)(2,1)}, u32[]{:S(2)}) copy-start(bf16[3,3,3,128,3]{3,4,2,1,0:T(4,128)(2,1)} %param.10) | copy-start | bytes 62212
  0.6 7.5 %copy-start.16 = (bf16[4,2,512,3]{2,1,3,0:T(2,128)(2,1)S(1)}, bf16[4,2,512,3]{2,1,3,0:T(2,128)(2,1)}, u32[]{:S(2)}) copy-start(bf16[4,2,512,3]{2,1,3,0:T(2,128)(2,1)} %param.11) | copy-start | bytes 73732
  0.7 7.5 %copy-start.17 = (bf16[3,3,3,64]{3,2,1,0:T(4,128)(2,1)S(1)}, bf16[3,3,3,64]{3,2,1,0:T(4,128)(2,1)}, u32[]{:S(2)}) copy-start(bf16[3,3,3,64]{3,2,1,0:T(4,128)(2,1)} %param.12) | copy-start | bytes 10372
  0.7 7.6 %copy-start.14 = (bf16[3,3,3,3,64]{4,3,2,1,0:T(4,128)(2,1)S(1)}, bf16[3,3,3,3,64]{4,3,2,1,0:T(4,128)(2,1)}, u32[]{:S(2)}) copy-start(bf16[3,3,3,3,64]{4,3,2,1,0:T(4,128)(2,1)} %param.14) | copy-start | bytes 31108
  0.7 7.7 %copy-start.1 = (bf16[3,3,3,128,128]{4,3,2,1,0:T(8,128)(2,1)S(1)}, bf16[3,3,3,128,128]{4,3,2,1,0:T(8,128)(2,1)}, u32[]{:S(2)}) copy-start(bf16[3,3,3,128,128]{4,3,2,1,0:T(8,128)(2,1)} %param.9) | copy-start | bytes 2654212
  0.7 10.6 %copy-start.13 = (bf16[3,3,64,128]{3,2,1,0:T(8,128)(2,1)S(1)}, bf16[3,3,64,128]{3,2,1,0:T(8,128)(2,1)}, u32[]{:S(2)}) copy-start(bf16[3,3,64,128]{3,2,1,0:T(8,128)(2,1)} %param.13) | copy-start | bytes 442372
  2.1 15.1 %collective-permute-start = (bf16[4,512,128]{2,1,0:T(8,128)(2,1)S(1)}, bf16[4,512,128]{2,1,0:T(8,128)(2,1)}, u32[]{:S(2)}, u32[]{:S(2)}) collective-permute-start(bf16[4,512,128]{2,1,0:T(8,128)(2,1)S(1)} %get-tuple-element.28.one), channel_id=1, source_target_pairs={{0,4},{4,8},{8,12},{12,16},{16,20},{20,24},{24,28},{28,32},{32,36}... | collective-permute-start | bytes 1572872 | tf_op jit(solution)/shard_map/ppermute | solution.py:338
  6.8 15.4 %collective-permute-start.1 = (bf16[4,512,128]{2,1,0:T(8,128)(2,1)S(1)}, bf16[4,512,128]{2,1,0:T(8,128)(2,1)}, u32[]{:S(2)}, u32[]{:S(2)}) collective-permute-start(bf16[4,512,128]{2,1,0:T(8,128)(2,1)S(1)} %get-tuple-element.27.zero), channel_id=1, source_target_pairs={{4,0},{8,4},{12,8},{16,12},{20,16},{24,20},{28,24},{32,28},{36,32}... | collective-permute-start | bytes 1572872 | tf_op jit(solution)/shard_map/ppermute | solution.py:338
  10.0 1.0 copy-start.6
  14.3 1.3 copy-start.12
  28.6 24.3 %all-to-all-start = ((f32[32,24,128]{2,1,0:T(8,128)}), f32[32,24,128]{2,1,0:T(8,128)}, u32[]{:S(2)}, u32[]{:S(2)}) async-start(f32[32,24,128]{2,1,0:T(8,128)} %get-tuple-element.18), calls=%async_computation | async-start | bytes 786432 | tf_op jit(solution)/shard_map/all_to_all | solution.py:375
  42.0 2.7 %copy-start.18 = (f32[64]{0:T(128)S(1)}, f32[64]{0:T(128)}, u32[]{:S(2)}) copy-start(f32[64]{0:T(128)} %param.15) | copy-start | bytes 772
  52.8 1.0 copy-start.2
  53.8 0.8 copy-start.3
  54.7 28.4 %copy-start = (f32[4,512,256]{2,1,0:T(8,128)S(1)}, f32[4,512,256]{2,1,0:T(8,128)}, u32[]{:S(2)}) copy-start(f32[4,512,256]{2,1,0:T(8,128)} %get-tuple-element.19.slope) | copy-start | bytes 6291460
  86.2 0.8 copy-start.8
  87.0 0.8 copy-start.10
  87.8 1.9 %copy-start.4 = (bf16[768,2048]{1,0:T(8,128)(2,1)S(1)}, bf16[768,2048]{1,0:T(8,128)(2,1)}, u32[]{:S(2)}) copy-start(bf16[768,2048]{1,0:T(8,128)(2,1)} %get-tuple-element.25.moved) | copy-start | bytes 9437188
  112.4 5.6 %copy-start.11 = (bf16[4,512,128]{2,1,0:T(8,128)(2,1)S(1)}, bf16[4,512,128]{2,1,0:T(8,128)(2,1)}, u32[]{:S(2)}) copy-start(bf16[4,512,128]{2,1,0:T(8,128)(2,1)} %copy-done.10) | copy-start | bytes 1572868
  112.4 9.3 %copy-start.9 = (bf16[4,512,128]{2,1,0:T(8,128)(2,1)S(1)}, bf16[4,512,128]{2,1,0:T(8,128)(2,1)}, u32[]{:S(2)}) copy-start(bf16[4,512,128]{2,1,0:T(8,128)(2,1)} %copy-done.8) | copy-start | bytes 1572868
  112.4 10.6 %copy-start.7 = (bf16[768,768]{1,0:T(8,128)(2,1)S(1)}, bf16[768,768]{1,0:T(8,128)(2,1)}, u32[]{:S(2)}) copy-start(bf16[768,768]{1,0:T(8,128)(2,1)} %copy-done.6) | copy-start | bytes 3538948
  113.6 29.8 %all-to-all-start.3 = ((bf16[32,112,128]{2,1,0:T(8,128)(2,1)}), bf16[32,112,128]{2,1,0:T(8,128)(2,1)S(1)}, u32[]{:S(2)}, u32[]{:S(2)}) async-start(bf16[32,112,128]{2,1,0:T(8,128)(2,1)} %broadcast_in_dim.20), calls=%async_computation.3 | async-start | bytes 1835008 | tf_op jit(solution)/shard_map/all_to_all | solution.py:435
  118.0 18.9 %collective-permute-start.2 = (bf16[4,512,128]{2,1,0:T(8,128)(2,1)S(1)}, bf16[4,512,128]{2,1,0:T(8,128)(2,1)S(1)}, u32[]{:S(2)}, u32[]{:S(2)}) collective-permute-start(bf16[4,512,128]{2,1,0:T(8,128)(2,1)S(1)} %copy-done.11), channel_id=1, source_target_pairs={{0,4},{4,8},{8,12},{12,16},{16,20},{20,24},{24,28},{28,32},{32,36}... | collective-permute-start | bytes 1572872 | tf_op jit(solution)/shard_map/ppermute | solution.py:338
  121.7 18.1 %collective-permute-start.3 = (bf16[4,512,128]{2,1,0:T(8,128)(2,1)S(1)}, bf16[4,512,128]{2,1,0:T(8,128)(2,1)S(1)}, u32[]{:S(2)}, u32[]{:S(2)}) collective-permute-start(bf16[4,512,128]{2,1,0:T(8,128)(2,1)S(1)} %copy-done.9), channel_id=1, source_target_pairs={{4,0},{8,4},{12,8},{16,12},{20,16},{24,20},{28,24},{32,28},{36,32}... | collective-permute-start | bytes 1572872 | tf_op jit(solution)/shard_map/ppermute | solution.py:338
  123.1 16.8 %copy-start.5 = (bf16[768,768]{1,0:T(8,128)(2,1)S(1)}, bf16[768,768]{1,0:T(8,128)(2,1)}, u32[]{:S(2)}) copy-start(bf16[768,768]{1,0:T(8,128)(2,1)} %get-tuple-element.23.kernel) | copy-start | bytes 3538948

commit v2 on v0

v2 whole, which is shorter than its diff:
```python
import jax
import jax.numpy as jnp
from jax import lax
from jax.experimental import pallas as pl
from jax.experimental.pallas import tpu as pltpu
from jax.sharding import PartitionSpec as P

F32 = jnp.float32
BF16 = jnp.bfloat16
HBM = pltpu.HBM
EDGE_MIB = 56
PREPARE_MIB = 56
HALO = 4


def sigmoid(value):
    return 0.5 * jnp.tanh(0.5 * value) + 0.5


def slope_of(value, gate):
    return gate * (1.0 + value * (1.0 - gate))


def dot(left, right, contract=((1,), (0,))):
    return lax.dot_general(left, right, (contract, ((), ())), preferred_element_type=F32)


def call(kernel, outs, *args, scratch=(), macs=0, limit=60):
    args = [a if isinstance(a, tuple) else (a, pltpu.VMEM) for a in args]
    outs = [o if isinstance(o, tuple) else (o, pltpu.VMEM) for o in outs]
    moved = sum(a.size * a.dtype.itemsize for a, _ in args + outs)
    return pl.pallas_call(
        kernel,
        out_shape=[o for o, _ in outs],
        in_specs=[pl.BlockSpec(memory_space=m) for _, m in args],
        out_specs=[pl.BlockSpec(memory_space=m) for _, m in outs],
        scratch_shapes=list(scratch),
        compiler_params=pltpu.CompilerParams(vmem_limit_bytes=limit * 1024 * 1024),
        cost_estimate=pl.CostEstimate(flops=2 * macs, bytes_accessed=moved, transcendentals=0),
    )(*[a for a, _ in args])


def start(source, target, sem):
    copy = pltpu.make_async_copy(source, target, sem)
    copy.start()
    return copy


def shape(dims, dtype):
    return jax.ShapeDtypeStruct(dims, dtype)


def before(value):
    row = lax.broadcasted_iota(jnp.int32, value.shape, 0)
    return jnp.where(row >= 1, pltpu.roll(value, 1, 0), 0.0)


def after(value):
    size = value.shape[0]
    row = lax.broadcasted_iota(jnp.int32, value.shape, 0)
    return jnp.where(row < size - 1, pltpu.roll(value, size - 1, 0), 0.0)


def colour_rows(rgb, scr, rows):
    scr[...] = jnp.zeros_like(scr)
    for f in range(4):
        for k, j in enumerate(rows):
            lanes = slice((f * 2 + k) * 128, (f * 2 + k + 1) * 128)
            for a in range(3):
                to = f - a + 1
                if not 0 <= to < 4:
                    continue
                for e in range(3):
                    at = e * 128 + to * 24 + (j + 1) * 3
                    scr[at : at + 9, lanes] = rgb[a * 3 + e]


def frames_of(f, step):
    return [(a, f + step * (a - 1)) for a in range(3) if 0 <= f + step * (a - 1) < 4]


def wide_taps(field, taps, cols):
    return jnp.concatenate([field[g * cols : (g + 1) * cols, :] for _, g in taps], axis=1)


def conv_rows(field, kernel, f, cols):
    taps = frames_of(f, 1)
    kernel = kernel[taps[0][0] * 256 : (taps[-1][0] + 1) * 256, :]
    wide = dot(wide_taps(field, taps, cols), kernel)
    return before(wide[:, :256]) + wide[:, 256:512] + after(wide[:, 512:])


def conv_rows_t(field, kernel, f, cols):
    taps = frames_of(f, -1)
    lanes = slice(taps[0][0] * 256, (taps[-1][0] + 1) * 256)
    wide = dot(wide_taps(field, taps, cols), kernel[:, lanes], ((1,), (1,)))
    return after(wide[:, :256]) + wide[:, 256:512] + before(wide[:, 512:])


def blocks_of(dec, edge, place):
    for a in range(3):
        for e in range(3):
            tap = [dec[(a * 3 + b) * 3 + e] for b in range(3)]
            for j in range(2):
                if edge:
                    place(a * 256 + j * 128, e * 256 + j * 128, tap, 2 * j)
                else:
                    for r in range(2):
                        place(a * 256 + j * 128, e * 256 + r * 128, tap, j - r + 1)


def prepare_kernel(latent, dec, rgb, edge, pre, colour, own, field, scr):
    cols = latent.shape[2]

    def put_own(one, two, tap, b):
        own[one : one + 128, two : two + 128] = tap[b]

    def put_edge(one, two, tap, b):
        edge[one : one + 128, two : two + 128] = tap[b]

    edge[...] = jnp.zeros_like(edge)
    blocks_of(dec, False, put_own)
    blocks_of(dec, True, put_edge)
    for f in range(4):
        for r in range(2):
            field[f * cols : (f + 1) * cols, r * 128 : (r + 1) * 128] = latent[f, r]
    for f in range(4):
        pre[f] = conv_rows(field, own, f, cols)
    colour_rows(rgb, scr, (0, 1))
    colour[...] = scr[...].astype(BF16)


def edge_kernel(
    odd_ref, first, second, kernel, own, colour, target,
    act, send_first, send_second, field, parts_out,
    act_s, slope_s, field_s, t_scr, p_scr, parts, sems,
):
    odd = odd_ref[0]
    cols = first.shape[1]
    t_scr[...] = jnp.zeros_like(t_scr)
    for f in range(4):
        t_scr[f * 24 + 18 : f * 24 + 24, :] = target[f * 6 : f * 6 + 6, :].astype(F32)
    p_scr[0:8, :] = jnp.zeros((8, 128), F32)
    p_scr[cols : cols + 8, :] = jnp.zeros((8, 128), F32)
    for f in range(4):
        rows = slice(f * cols, (f + 1) * cols)
        field_s[rows, :128] = jnp.where(odd == 1, first[f], second[f])
        field_s[rows, 128:] = jnp.where(odd == 1, second[f], first[f])
    copies = [
        start(field_s.at[pl.ds(f * cols, cols)], field.at[f], sems.at[f]) for f in range(4)
    ]
    for f in range(4):
        pre = own[f] + conv_rows(field_s, kernel, f, cols)
        gate = sigmoid(pre)
        act_s[:, f * 256 : (f + 1) * 256] = (pre * gate).astype(BF16)
        slope = slope_of(pre, gate).astype(BF16)
        slope_s[0, f] = slope[:, :128]
        slope_s[1, f] = slope[:, 128:]
    copies.append(start(slope_s.at[1 - odd], send_first, sems.at[4]))
    copies.append(start(slope_s.at[odd], send_second, sems.at[5]))
    copies.append(start(act_s, act, sems.at[6]))
    wide = dot(act_s[...], colour[...], ((1,), (1,)))
    part = before(wide[:, :128]) + wide[:, 128:256] + after(wide[:, 256:])
    p_scr[HALO : HALO + cols, :] = part + t_scr[...].T
    blocks, width, _ = parts.shape
    for d in range(blocks):
        at = d * (width - 2 * HALO)
        parts[d] = p_scr[at : at + width, :]
    copies.append(start(parts, parts_out, sems.at[7]))
    for copy in copies:
        copy.wait()


def branch_scratch(bands, wide):
    return [
        pltpu.VMEM((bands * wide, 128), F32),
        pltpu.VMEM((wide + 1, 8, 128), F32),
        pltpu.VMEM((768, 256), BF16),
        pltpu.VMEM((144, 256), BF16),
        pltpu.VMEM((256, 144), BF16),
        pltpu.VMEM((48, 768), BF16),
        pltpu.VMEM((256, 768), BF16),
        pltpu.VMEM((256, 768), BF16),
        pltpu.VMEM((wide, 24, 128), F32),
        pltpu.VMEM((wide, 16, 128), F32),
        pltpu.VMEM((4, wide + 2, 16, 128), BF16),
        pltpu.VMEM((2, wide, 256, 128), BF16),
        pltpu.VMEM((wide, 128, 128), F32),
        pltpu.VMEM((wide, 256, 128), BF16),
        pltpu.VMEM((wide, 256, 128), BF16),
        pltpu.VMEM((bands * (wide - 2 * HALO), 128), F32),
        pltpu.SemaphoreType.DMA((4,)),
    ]


def branch_kernel(
    parts_in, consts_in, w2_in, w1_in,
    out,
    parts, consts, w2_t, w1_t, w1, w1_z, w2, w2_b,
    rows, taps, colours, feats, slopes, grads_two, grads, turned, sems,
):
    copies = [
        start(source, target, sems.at[k])
        for k, (source, target) in enumerate(
            [(parts_in, parts), (consts_in, consts), (w2_in, w2_t), (w1_in, w1_t)]
        )
    ]
    wide = rows.shape[0]
    bands = parts.shape[0] // wide
    own = wide - 2 * HALO
    lane = lax.broadcasted_iota(jnp.int32, (1, 128), 1)
    frame, band = (lane // bands, lane % bands)

    def rolled(value, by):
        by = by % 128
        return value if by == 0 else pltpu.roll(value, by, value.ndim - 1)

    def down(value):
        return jnp.where(band >= 1, rolled(value, 1), 0.0)

    def up(value):
        return jnp.where(band < bands - 1, rolled(value, -1), 0.0)

    def earlier(value):
        return jnp.where(frame >= 1, rolled(value, bands), 0.0)

    def later(value):
        return jnp.where(frame < 3, rolled(value, -bands), 0.0)

    def rounded(value):
        return value.astype(BF16).astype(F32)

    def tile(value, n):
        return value[:, n * 128 : (n + 1) * 128]

    def stacked(get, first, step):
        return jnp.concatenate(
            [
                jnp.concatenate([get(first + n + step * (e - 1)) for e in range(3)], axis=0)
                for n in range(4)
            ],
            axis=1,
        )

    def masks(first):
        return jnp.concatenate([consts[first + n][0:1] for n in range(4)], axis=1)

    taps[...] = jnp.zeros_like(taps)
    colours[...] = jnp.zeros_like(colours)
    grads_two[1] = jnp.zeros((256, 128), BF16)
    grads_two[wide - 2] = jnp.zeros((256, 128), BF16)
    for copy in copies:
        copy.wait()
    w1[...] = w1_t[...].astype(F32).T.astype(BF16)
    w2[...] = w2_t[...].astype(F32).T.astype(BF16)
    for e in range(3):
        w2_b[:, e * 256 : (e + 1) * 256] = w2_t[e * 256 : (e + 1) * 256, :]
        for a in range(3):
            at = (a * 3 + e) * 16
            w1_z[a * 16 : (a + 1) * 16, e * 256 : (e + 1) * 256] = w1_t[at : at + 16, :]
    head = consts[wide].T[:, 0:1]

    for k in range(wide // 4):
        block = jnp.concatenate(
            [parts[pl.ds(4 * k + m, bands, stride=wide), :] for m in range(4)], axis=0
        ).T
        for m in range(4):
            value = jnp.zeros((24, 128), F32)
            for f in range(4):
                piece = rolled(block[f * 24 : (f + 1) * 24], (f - m) * bands)
                value = jnp.where(frame == f, piece, value)
            rows[4 * k + m] = value

    mask = consts[0:wide, 0:1, :]

    def place(even, odd):
        taps[:, 0:3, :] = down(odd)
        taps[:, 3:6, :] = even
        taps[:, 6:9, :] = odd
        taps[:, 9:12, :] = up(even)
        return taps[...]

    colours[0, 1 : wide + 1] = place(rows[:, 18:21, :] * mask, rows[:, 21:24, :] * mask).astype(BF16)
    even = rounded((rows[:, 6:9, :] + down(rows[:, 12:15, :])) * mask)
    odd = rounded((rows[:, 9:12, :] + up(rows[:, 3:6, :])) * mask)
    field = place(even, odd)
    for a, value in enumerate((earlier(field), field, later(field))):
        colours[1 + a, 1 : wide + 1] = value.astype(BF16)

    def keep_feats(kind, first, feat):
        for n in range(4):
            value = tile(feat, n)
            feats[kind, first + n, 0:64] = down(value[64:]).astype(BF16)
            feats[kind, first + n, 64:192] = value.astype(BF16)
            feats[kind, first + n, 192:256] = up(value[:64]).astype(BF16)

    def first_layer(t, carry):
        c = t * 4
        mask = masks(c)
        pre = dot(w1[0:128, 48:96], stacked(lambda at: colours[0, at], c + 1, 1))
        keep_feats(0, c, rounded(pre * sigmoid(pre) * mask))
        field = [stacked(lambda at: colours[1 + a, at], c + 1, 1) for a in range(3)]
        both = dot(w1[...], jnp.concatenate(field, axis=0))
        pre, crit = (both[:128], both[128:])
        gate = sigmoid(pre)
        keep_feats(1, c, rounded(pre * gate * mask))
        slope = slope_of(pre, gate) * mask
        gate = sigmoid(crit)
        scored = crit * gate * head
        slope_c = slope_of(crit, gate) * head * mask
        logits = [jnp.sum(scored[r * 64 : r * 64 + 64], axis=0, keepdims=True) for r in range(2)]
        grad = [-sigmoid(-logits[r]) * slope_c[r * 64 : r * 64 + 64] for r in range(2)]
        grad = jnp.concatenate(grad, axis=0).astype(BF16)
        for n in range(4):
            slopes[c + n] = tile(slope, n)
            grads[c + n, 128:256] = tile(grad, n)
        return carry

    lax.fori_loop(0, wide // 4, first_layer, 0, unroll=True)

    def second_layer(t, carry):
        c = t * 4 + 2
        pre = dot(w2[...], stacked(lambda at: feats[0, at], c, 1))
        wanted = pre * sigmoid(pre)
        pre = dot(w2[...], stacked(lambda at: feats[1, at], c, 1))
        gate = sigmoid(pre)
        gap = pre * gate - wanted
        grad = (0.25 * gap * slope_of(pre, gate) * masks(c)).astype(BF16)
        for n in range(4):
            grads_two[c + n] = tile(grad, n)
        return carry

    lax.fori_loop(0, (wide - 4) // 4, second_layer, 0, unroll=True)

    def second_back(t, carry):
        c = t * 4 + 2
        spread = dot(w2_b[...], stacked(lambda at: grads_two[at], c, -1))
        for n in range(4):
            value = tile(spread, n)
            even = value[64:128] + down(value[192:256])
            odd = value[128:192] + up(value[0:64])
            grad = jnp.concatenate([even, odd], axis=0) * slopes[c + n]
            grads[c + n, 0:128] = grad.astype(BF16)
        return carry

    lax.fori_loop(0, (wide - 4) // 4, second_back, 0, unroll=True)

    def first_back(t, carry):
        c = t * 4 + HALO
        spread = dot(w1_z[...], stacked(lambda at: grads[at], c, -1))
        for n in range(4):
            value = tile(spread, n)
            taps[c + n] = later(value[0:16]) + value[16:32] + earlier(value[32:48])
        return carry

    lax.fori_loop(0, own // 4, first_back, 0, unroll=True)
    mid = slice(HALO, HALO + own)
    even = rounded(taps[mid, 3:6, :] + down(taps[mid, 9:12, :]))
    odd = rounded(taps[mid, 6:9, :] + up(taps[mid, 0:3, :]))
    for k, value in enumerate((down(even), down(odd), even, odd, up(even), up(odd))):
        rows[mid, 3 * k : 3 * k + 3, :] = value
    for k in range(own // 4):
        block = []
        for f in range(4):
            value = jnp.zeros((24, 128), F32)
            for m in range(4):
                piece = rolled(rows[HALO + 4 * k + m], (m - f) * bands)
                value = jnp.where(frame == m, piece, value)
            block.append(value)
        block = jnp.concatenate(block + [jnp.zeros((32, 128), F32)], axis=0).T
        for m in range(4):
            turned[pl.ds(4 * k + m, bands, stride=own), :] = block[m * bands : (m + 1) * bands]
    out[...] = turned[...].astype(BF16)


def taps_of(grad_in, cols):
    grad = grad_in[...].reshape(cols, 128).astype(F32)
    return jnp.concatenate([after(grad), grad, before(grad)], axis=1)


def dec_grad_kernel(
    odd_ref, grad_in, colour_in, first_in, second_in, act_in, latent, edge_in,
    local_out, grad_pre,
    local, colour, slope, act, field, pre_s, moved, gram, sems,
):
    cols = act.shape[0]
    odd = odd_ref[0]
    moves = [
        (colour_in, colour),
        (first_in, slope.at[1 - odd]),
        (second_in, slope.at[odd]),
        (act_in, act),
        (latent.at[:, 0], field.at[:, :, pl.ds(0, 128)]),
        (latent.at[:, 1], field.at[:, :, pl.ds(128, 128)]),
        (edge_in, field.at[:, :, pl.ds(256, 256)]),
    ]
    copies = [start(source, target, sems.at[k]) for k, (source, target) in enumerate(moves)]
    taps = taps_of(grad_in, cols)
    for copy in copies[:3]:
        copy.wait()
    grad_act = dot(taps.astype(BF16), colour[...])
    lane = lax.broadcasted_iota(jnp.int32, (1, cols), 1)
    for f in range(4):
        wide = grad_act[:, f * 256 : (f + 1) * 256]
        zero = (wide[:, :128] * slope[0, f].astype(F32)).astype(BF16)
        one = (wide[:, 128:] * slope[1, f].astype(F32)).astype(BF16)
        pre_s[f * cols : (f + 1) * cols, :128] = zero
        pre_s[f * cols : (f + 1) * cols, 128:] = one
        turned = jnp.concatenate([zero.astype(F32).T, one.astype(F32).T], axis=0)
        later = jnp.where(lane < cols - 1, pltpu.roll(turned, cols - 1, 1), 0.0)
        sooner = jnp.where(lane >= 1, pltpu.roll(turned, 1, 1), 0.0)
        for e, value in enumerate((later, turned, sooner)):
            moved[e * 256 : (e + 1) * 256, f * cols : (f + 1) * cols] = value.astype(BF16)
    outs = [start(pre_s, grad_pre, sems.at[7])]
    copies[3].wait()
    gram[...] = dot(taps.T.astype(BF16), act[...])
    rows = []
    for a in range(3):
        sums = []
        for e in range(3):
            total = jnp.zeros((9, 128), F32)
            for f in range(4):
                to = f - a + 1
                if not 0 <= to < 4:
                    continue
                for r in range(2):
                    at = e * 128 + to * 24 + (r + 1) * 3
                    total += gram[at : at + 9, (f * 2 + r) * 128 : (f * 2 + r + 1) * 128]
            sums.append(total)
        for b in range(3):
            for e in range(3):
                rows.append(sums[e][(2 - b) * 3 : (2 - b) * 3 + 3])
    gram[0:128, 0:128] = jnp.zeros((128, 128), F32)
    for k, value in enumerate(rows):
        gram[k * 3 : k * 3 + 3, 0:128] = value
    local[27 * 128 :, :] = gram[0:128, 0:128].astype(BF16)
    for copy in copies[4:]:
        copy.wait()
    rows_of = (2, 0, 1, 3)
    for a in range(3):
        lo, hi = (max(0, 1 - a), min(4, 5 - a))
        first, last = (lo * cols, hi * cols)
        source = field[lo + a - 1 : hi + a - 1].reshape((hi - lo) * cols, 512)
        for e in range(3):
            wide = dot(moved[e * 256 : (e + 1) * 256, first:last], source)
            for b in range(3):
                one, two = (rows_of[b] * 128, rows_of[b + 1] * 128)
                total = wide[:128, one : one + 128] + wide[128:, two : two + 128]
                at = ((a * 3 + b) * 3 + e) * 128
                local[at : at + 128, :] = total.T.astype(BF16)
        part = pl.ds(a * 9 * 128, 9 * 128 if a < 2 else 10 * 128)
        outs.append(start(local.at[part], local_out.at[part], sems.at[8 + a]))
    for copy in outs:
        copy.wait()


def latent_kernel(
    odd_ref, grad_in, dec, rgb, first, second, pre,
    out,
    own_t, edge_t, colour, edge_s, scr,
):
    cols = first.shape[1]
    odd = odd_ref[0]
    colour_rows(rgb, scr, (-1, 2))
    colour[...] = scr[...].astype(BF16)

    def put_own(one, two, tap, b):
        at, to = (two // 256 * 256 + one % 256, one // 256 * 256 + two % 256)
        own_t[at : at + 128, to : to + 128] = tap[b]

    def put_edge(one, two, tap, b):
        edge_t[two : two + 128, one : one + 128] = tap[2 - b]

    edge_t[...] = jnp.zeros_like(edge_t)
    blocks_of(dec, False, put_own)
    blocks_of(dec, True, put_edge)
    grad_act = dot(taps_of(grad_in, cols).astype(BF16), colour[...])
    for f in range(4):
        slopes = (
            jnp.where(odd == 1, first[f], second[f]),
            jnp.where(odd == 1, second[f], first[f]),
        )
        for k in range(2):
            at = (f * 2 + k) * 128
            value = grad_act[:, at : at + 128] * slopes[k].astype(F32)
            edge_s[f * cols : (f + 1) * cols, k * 128 : (k + 1) * 128] = value.astype(BF16)
    for f in range(4):
        wide = conv_rows_t(pre, own_t, f, cols) + conv_rows_t(edge_s, edge_t, f, cols)
        out[f, 0] = wide[:, :128]
        out[f, 1] = wide[:, 128:]


def branch_weights(vgg_first, vgg_second, critic):
    def paired(taps):
        none = jnp.zeros_like(taps[..., :1, :, :])
        return jnp.stack(
            [jnp.concatenate([taps, none], -3), jnp.concatenate([none, taps], -3)], axis=-4
        )

    first = paired(vgg_first.reshape(3, 9, 64)).reshape(1, 2, 4, 3, 3, 64)
    crit = paired(critic.reshape(3, 3, 9, 64)).reshape(3, 2, 4, 3, 3, 64)
    both = jnp.stack([jnp.pad(first, ((1, 1),) + ((0, 0),) * 5), crit])
    w1_t = both.transpose(1, 4, 3, 5, 0, 2, 6).reshape(9, 12, 256)
    w1_t = jnp.pad(w1_t, ((0, 0), (0, 4), (0, 0))).reshape(144, 256)
    w2_t = paired(vgg_second.transpose(1, 0, 2, 3))
    w2_t = w2_t.transpose(0, 2, 3, 1, 4).reshape(768, 256)
    return (w2_t, w1_t)


def per_device(
    latent, dec_kernel, rgb_kernel, target, vgg_first, vgg_second, critic_kernel, critic_head
):
    size = lax.axis_size("band")
    me = lax.axis_index("band")
    cols = latent.shape[2]
    width = cols // size
    wide = width + 2 * HALO
    pairs = [[(i, i + 1), (i + 1, i)] for i in range(size - 1)]
    first_pairs, second_pairs = (sum(pairs[0::2], []), sum(pairs[1::2], []))
    odd = me % 2
    odd_ref = (jnp.reshape(odd, (1,)).astype(jnp.int32), pltpu.SMEM)

    def row(index):
        return lax.dynamic_index_in_dim(latent, index, 1, keepdims=False)

    first = lax.ppermute(row(1 - odd), "band", first_pairs)
    second = lax.ppermute(row(odd), "band", second_pairs)
    rgb = rgb_kernel.transpose(0, 2, 1, 4, 3)[:, :, ::-1].reshape(9, 9, 128).astype(F32)
    big = 4 * cols * 768 * 640
    square = shape((768, 768), BF16)
    toeplitz = shape((384, 1024), BF16)
    half = shape((4, cols, 128), BF16)
    field = shape((4 * cols, 256), BF16)
    dma = pltpu.SemaphoreType.DMA
    dec = dec_kernel.reshape(27, 128, 128)
    edge_w, pre_own, colour = call(
        prepare_kernel,
        [square, shape((4, cols, 256), F32), toeplitz],
        latent,
        dec,
        rgb,
        scratch=[
            pltpu.VMEM((768, 768), BF16),
            pltpu.VMEM((4 * cols, 256), BF16),
            pltpu.VMEM((384, 1024), F32),
        ],
        macs=big,
        limit=PREPARE_MIB,
    )
    w2_t, w1_t = branch_weights(vgg_first, vgg_second, critic_kernel)
    place = jnp.arange(wide) + me * width - HALO
    mask = jnp.where((place >= 0) & (place < cols), 1.0, 0.0).astype(F32)
    consts = jnp.concatenate(
        [jnp.broadcast_to(mask[:, None], (wide, 128)), jnp.tile(critic_head, 2)[None]]
    )
    consts = jnp.broadcast_to(consts[:, None], (wide + 1, 8, 128))
    act, send_first, send_second, field_edge, parts = call(
        edge_kernel,
        [
            (shape((cols, 1024), BF16), HBM),
            (half, HBM),
            (half, HBM),
            (shape((4, cols, 256), BF16), HBM),
            (shape((size, wide, 128), F32), HBM),
        ],
        odd_ref,
        first,
        second,
        edge_w,
        pre_own,
        colour,
        target.transpose(0, 1, 3, 2).reshape(24, cols),
        scratch=[
            pltpu.VMEM((cols, 1024), BF16),
            pltpu.VMEM((2, 4, cols, 128), BF16),
            pltpu.VMEM((4 * cols, 256), BF16),
            pltpu.VMEM((128, cols), F32),
            pltpu.VMEM((cols + 8, 128), F32),
            pltpu.VMEM((size, wide, 128), F32),
            dma((8,)),
        ],
        macs=big,
        limit=EDGE_MIB,
    )
    parts = lax.all_to_all(parts, "band", 0, 0)
    parts, sent = lax.optimization_barrier((parts, send_first))
    first = lax.ppermute(sent, "band", first_pairs)
    (grad_frames,) = call(
        branch_kernel,
        [shape((size * width, 128), BF16)],
        (parts.reshape(size * wide, 128), HBM),
        (consts, HBM),
        (w2_t, HBM),
        (w1_t, HBM),
        scratch=branch_scratch(size, wide),
        macs=4 * 768 * 768 * 700,
    )
    grad_frames, first, sent = lax.optimization_barrier((grad_frames, first, send_second))
    second = lax.ppermute(sent, "band", second_pairs)
    grad_frames = lax.all_to_all(grad_frames.reshape(size, width, 128), "band", 0, 0)
    local, grad_pre = call(
        dec_grad_kernel,
        [(shape((28 * 128, 128), BF16), HBM), (field, HBM)],
        odd_ref,
        grad_frames,
        (colour, HBM),
        (send_first, HBM),
        (send_second, HBM),
        (act, HBM),
        (latent, HBM),
        (field_edge, HBM),
        scratch=[
            pltpu.VMEM((28 * 128, 128), BF16),
            pltpu.VMEM((384, 1024), BF16),
            pltpu.VMEM((2, 4, cols, 128), BF16),
            pltpu.VMEM((cols, 1024), BF16),
            pltpu.VMEM((4, cols, 512), BF16),
            pltpu.VMEM((4 * cols, 256), BF16),
            pltpu.VMEM((768, 4 * cols), BF16),
            pltpu.VMEM((384, 1024), F32),
            dma((11,)),
        ],
        macs=3 * big,
    )
    local, second = lax.optimization_barrier((local, second))
    pieces = lax.all_to_all(local.reshape(size, -1, 128), "band", 0, 0)
    mine = jnp.sum(pieces.astype(F32), axis=0).astype(BF16)
    whole = lax.all_to_all(jnp.broadcast_to(mine, (size,) + mine.shape), "band", 0, 0)
    (grad_latent,) = call(
        latent_kernel,
        [shape((4, 2, cols, 128), F32)],
        odd_ref,
        grad_frames,
        dec,
        rgb,
        first,
        second,
        grad_pre,
        scratch=[
            pltpu.VMEM((768, 768), BF16),
            pltpu.VMEM((768, 768), BF16),
            pltpu.VMEM((384, 1024), BF16),
            pltpu.VMEM((4 * cols, 256), BF16),
            pltpu.VMEM((384, 1024), F32),
        ],
        macs=2 * big,
    )
    whole = whole.reshape(28 * 128, 128)
    pixels = 4 * latent.shape[1] * size * cols
    factor = float(pixels) ** (-0.5)
    grad_dec = whole[: 27 * 128].astype(F32).reshape(3, 3, 3, 128, 128) * factor
    grad_rgb = whole[27 * 128 : 27 * 128 + 81].astype(F32).reshape(3, 3, 3, 3, 128) * factor
    return (grad_latent, grad_dec, grad_rgb.transpose(0, 1, 2, 4, 3))


def solution(mesh):
    placed = (
        P("clip", "band", None, None),
        P(),
        P(),
        P("clip", "band", None, None),
        P(),
        P(),
        P(),
        P(),
    )
    return jax.shard_map(
        per_device,
        mesh=mesh,
        in_specs=placed,
        out_specs=(
            P("clip", "band", None, None),
            P("clip", None, None, None, None),
            P("clip", None, None, None, None),
        ),
        check_vma=False,
    )
```

time: 993 us -> 128 us (0.13); the launches traced: 980 us -> 128 us
  waiting for transfers between devices: 363 us -> 28.3 us
  matrix products: 213 us -> 0 us
  blocking collectives: 185 us -> 19.3 us
  local copies, waits for them, and re-layouts: 116 us -> 8.95 us
  Pallas kernels: 0 us -> 39.3 us
  other arithmetic: 37 us -> 1.73 us
  starting transfers between devices: 51.2 us -> 29.4 us
  between operations: 15.1 us -> 0.95 us
    psum x1 -> x0, waiting for transfers between devices: 321 us -> none  [per_device(): lax.psum(local_dec.astype(jnp.bfloat16), 'band').astype(jnp.float32)]
    conv_general_dilated x10 -> x0, matrix products: 186 us -> none  [conv_valid(): lax.conv_general_dilated(field, kernel, (1,) * spatial, 'VALID', dimensio...]
    psum x1 -> x0, blocking collectives: 185 us -> none  [per_device(): lax.psum(local_rgb.astype(jnp.bfloat16), 'band').astype(jnp.float32)]
    conv_general_dilated x36 -> x0, local copies, waits for them, and re-layouts: 60 us -> none  [conv_valid(): lax.conv_general_dilated(field, kernel, (1,) * spatial, 'VALID', dimensio...]
    ppermute x18 -> x4, starting transfers between devices: 51.1 us -> 4.03 us  [the longest x1 2.08 us: per_device(): first = lax.ppermute(row(1 - odd), 'band', first_pairs)]
    pallas_call x0 -> x5, Pallas kernels: none -> 39.3 us  [call(): pl.pallas_call(kernel, out_shape=[o for o, _ in outs], in_specs=[pl.Block...]
    ppermute x18 -> x4, waiting for transfers between devices: 41.3 us -> 4.72 us  [the longest x1 3.76 us: per_device(): first = lax.ppermute(row(1 - odd), 'band', first_pairs)]
    dot_general x55 -> x0, matrix products: 27.5 us -> none  [the longest x54 25.2 us: kernel_grad(): jnp.einsum('fhwi,fhwo->io', window, grad_out, preferred_element_type=jnp....]
  transfers between devices with their start and end apart: 19 -> 7, of which waited for: 10 -> 5; matrix products, arithmetic and copies ran while one was open for 14% -> 4% of each run, Pallas kernels for 0% -> 26%
where the time goes in v2:
time: 128 us
  Pallas kernels  39.3 us (31%)
  starting transfers between devices  29.4 us (23%)
  waiting for transfers between devices  28.3 us (22%)
  blocking collectives  19.3 us (15%)
  local copies, waits for them, and re-layouts  8.95 us (7%)
  other arithmetic  1.73 us (1%)
    pallas_call x5, Pallas kernels, call(): pl.pallas_call(kernel, out_shape=[o for o, _ in outs], in_specs=[pl.Block...  39.3 us
    all_to_all x1, blocking collectives, per_device(): pieces = lax.all_to_all(local.reshape(size, -1, 128), 'band', 0, 0)  19.3 us
    all_to_all x1, starting transfers between devices, per_device(): parts = lax.all_to_all(parts, 'band', 0, 0)  17 us
    all_to_all x1, waiting for transfers between devices, per_device(): lax.all_to_all(grad_frames.reshape(size, width, 128), 'band', 0, 0)  9.54 us
    all_to_all x1, waiting for transfers between devices, per_device(): parts = lax.all_to_all(parts, 'band', 0, 0)  8.79 us
    all_to_all x1, waiting for transfers between devices, per_device(): lax.all_to_all(jnp.broadcast_to(mine, (size,) + mine.shape), 'band', 0, 0)  5.22 us
    all_to_all x1, starting transfers between devices, per_device(): lax.all_to_all(jnp.broadcast_to(mine, (size,) + mine.shape), 'band', 0, 0)  4.37 us
    all_to_all x1, starting transfers between devices, per_device(): lax.all_to_all(grad_frames.reshape(size, width, 128), 'band', 0, 0)  4.04 us
  transfers between devices with their start and end apart: 7, of which 5 were waited for; matrix products, arithmetic and copies ran while one was open for 4% of the time, Pallas kernels for 26%

profile of v2, /device:TPU:0, one launch (start us, length us, event | category | flops | bytes accessed | tf_op | source)
XLA Modules:
  0.0 127.9 jit_solution(6768419661224063103)
XLA Ops:
  0.6 0.0 copy-start.4
  0.6 0.0 copy-start.5
  0.7 0.0 copy-start.6
  0.7 0.0 copy-start.3
  0.7 1.3 %dynamic-slice_bitcast_fusion = (bf16[4,512,128]{2,1,0:T(8,128)(2,1)S(1)}, bf16[4,512,128]{2,1,0:T(8,128)(2,1)S(1)}) fusion(bf16[4,2,512,128]{3,2,1,0:T(8,128)(2,1)} %latent.3, s32[]{:T(128)S(6)} %select_n.24, s32[]{:T(128)S(6)} %select_n.23), kind=kLoop, calls=%fused_computation.1 | loop fusion | bytes 2097160 | tf_op jit(solution)/shard_map/jit(dynamic_index_in_dim)/squeeze | solution.py:524
  2.0 2.1 %collective-permute-start = (bf16[4,512,128]{2,1,0:T(8,128)(2,1)S(1)}, bf16[4,512,128]{2,1,0:T(8,128)(2,1)S(1)}, u32[]{:S(2)}, u32[]{:S(2)}) collective-permute-start(bf16[4,512,128]{2,1,0:T(8,128)(2,1)S(1)} %get-tuple-element.38), channel_id=1, source_target_pairs={{0,4},{4,0},{8,12},{12,8},{16,20},{20,16},{24,28},{28,24},{32,36},... | collective-permute-start | bytes 1572872 | tf_op jit(solution)/shard_map/ppermute | solution.py:526
  4.1 0.7 collective-permute-start.1
  4.8 0.0 copy-done.4
  4.8 0.7 reshape.83.rgb
  5.5 0.0 copy-done.5
  5.5 0.6 reshape.73.target
  6.1 0.0 copy-done.6
  6.1 0.0 copy-done.3
  6.3 6.0 %shard_map.103 = (bf16[768,768]{1,0:T(8,128)(2,1)}, f32[4,512,256]{2,1,0:T(8,128)}, bf16[384,1024]{1,0:T(8,128)(2,1)}) custom-call(bf16[4,2,512,128]{3,2,1,0:T(8,128)(2,1)} %latent.3, bf16[27,128,128]{2,1,0:T(8,128)(2,1)} %bitcast.60, f32[9,9,128]{2,1,0:T(8,128)} %reshape.83.rgb), custom_call_target="tpu_custom_call" | custom-call | flops 2013265920 | bytes 6038016 | tf_op jit(solution)/shard_map/pallas_call | solution.py:32
  12.2 3.8 %collective-permute-done.first = bf16[4,512,128]{2,1,0:T(8,128)(2,1)S(1)} collective-permute-done((bf16[4,512,128]{2,1,0:T(8,128)(2,1)S(1)}, bf16[4,512,128]{2,1,0:T(8,128)(2,1)S(1)}, u32[]{:S(2)}, u32[]{:S(2)}) %collective-permute-start) | collective-permute-done | bytes 524320 | tf_op jit(solution)/shard_map/ppermute | solution.py:526
  16.0 0.0 copy-start.10
  16.0 0.0 collective-permute-done.1.second
  16.0 0.0 copy-start.11
  16.0 0.8 copy-done.10
  16.8 0.2 copy-done.11
  17.0 0.0 copy-start.13
  17.0 0.0 copy-start.1
  17.0 6.7 %shard_map.104 = (bf16[512,1024]{1,0:T(8,128)(2,1)}, bf16[4,512,128]{2,1,0:T(8,128)(2,1)}, bf16[4,512,128]{2,1,0:T(8,128)(2,1)}, bf16[4,512,256]{2,1,0:T(8,128)(2,1)}, f32[32,24,128]{2,1,0:T(8,128)}) custom-call(s32[1]{0:T(128)} %bitcast.odd_ref, bf16[4,512,128]{2,1,0:T(8,128)(2,1)} %copy-done.10, bf16[4,512,128]{2,1,0:T(8,128)(2,1)} %copy-done.11, ...), custom_call_target="tpu_custom_call" | custom-call | flops 2013265920 | bytes 8675332 | tf_op jit(solution)/shard_map/pallas_call | solution.py:32
  23.6 17.0 %all-to-all-start = ((f32[32,24,128]{2,1,0:T(8,128)}), f32[32,24,128]{2,1,0:T(8,128)S(1)}, u32[]{:S(2)}, u32[]{:S(2)}) async-start(f32[32,24,128]{2,1,0:T(8,128)} %get-tuple-element.23), calls=%async_computation | async-start | bytes 786432 | tf_op jit(solution)/shard_map/all_to_all | solution.py:585
  40.6 0.1 maximum_bitcast_fusion.1
  40.7 0.0 copy-start.7
  40.7 0.1 copy.32
  40.8 0.1 reshape.78
  41.0 0.0 copy-done.13
  41.0 0.1 broadcast_in_dim_tile.3
  41.1 0.0 copy-done.1
  41.1 0.1 pad_bitcast_fusion.1
  41.2 0.4 copy.27
  41.6 0.8 copy.35
  42.4 0.6 pad.15
  43.1 8.8 %all-to-all-done = f32[32,24,128]{2,1,0:T(8,128)S(1)} async-done(((f32[32,24,128]{2,1,0:T(8,128)}), f32[32,24,128]{2,1,0:T(8,128)S(1)}, u32[]{:S(2)}, u32[]{:S(2)}) %all-to-all-start) | async-done | bytes 393248 | tf_op jit(solution)/shard_map/all_to_all | solution.py:585
  51.9 0.0 copy-start
  51.9 0.0 copy-done.7
  51.9 0.6 collective-permute-start.2
  52.4 0.1 pad_maximum_fusion
  52.5 0.7 broadcast_in_dim.29.consts_in
  53.2 0.0 copy-done
  53.2 0.0 copy-start.8
  53.2 8.9 %shard_map.105 = bf16[512,128]{1,0:T(8,128)(2,1)} custom-call(f32[768,128]{1,0:T(8,128)} %bitcast.46, f32[25,8,128]{2,1,0:T(8,128)} %broadcast_in_dim.29.consts_in, bf16[768,256]{1,0:T(8,128)(2,1)} %bitcast.47, bf16[144,256]{1,0:T(8,128)(2,1)} %bitcast.53), custom_call_target="tpu_custom_call" | custom-call | flops 3303014400 | bytes 1093632 | tf_op jit(solution)/shard_map/pallas_call | solution.py:32
  62.1 1.0 collective-permute-done.2.first
  63.0 0.0 copy-start.9
  63.0 4.0 %all-to-all-start.1 = ((bf16[32,16,128]{2,1,0:T(8,128)(2,1)}), bf16[32,16,128]{2,1,0:T(8,128)(2,1)S(1)}, u32[]{:S(2)}, u32[]{:S(2)}) async-start(bf16[32,16,128]{2,1,0:T(8,128)(2,1)} %bitcast.49), calls=%async_computation.1 | async-start | bytes 262144 | tf_op jit(solution)/shard_map/all_to_all | solution.py:600
  67.1 0.0 copy-done.8
  67.1 0.7 collective-permute-start.3
  67.8 9.5 %all-to-all-done.1.grad_in = bf16[32,16,128]{2,1,0:T(8,128)(2,1)S(1)} async-done(((bf16[32,16,128]{2,1,0:T(8,128)(2,1)}), bf16[32,16,128]{2,1,0:T(8,128)(2,1)S(1)}, u32[]{:S(2)}, u32[]{:S(2)}) %all-to-all-start.1) | async-done | bytes 131104 | tf_op jit(solution)/shard_map/all_to_all | solution.py:600
  77.3 0.7 copy-done.2
  78.0 9.6 %shard_map.106 = (bf16[3584,128]{1,0:T(8,128)(2,1)}, bf16[2048,256]{1,0:T(8,128)(2,1)}) custom-call(s32[1]{0:T(128)} %bitcast.odd_ref, bf16[32,16,128]{2,1,0:T(8,128)(2,1)} %copy-done.2, bf16[384,1024]{1,0:T(8,128)(2,1)} %get-tuple-element.22.colour.colour_in, bf16[4,512,128]{2,1,0:T(8,128)(2,1)} %get-tuple-element.26.first_in, ...), custom_call_target="tpu_custom_call" | custom-call | flops 6039797760 | bytes 7077892 | tf_op jit(solution)/shard_map/pallas_call | solution.py:32
  87.6 0.0 copy-done.9
  87.6 0.0 collective-permute-done.3.second
  87.6 0.0 copy-start.12
  87.6 19.3 %all_to_all.20 = bf16[32,112,128]{2,1,0:T(8,128)(2,1)S(1)} all-to-all(bf16[32,112,128]{2,1,0:T(8,128)(2,1)} %bitcast.45), channel_id=1, replica_groups=mesh['band'=32,'clip'=4] {'band'}, dimensions={0} | all-to-all | bytes 1835008 | tf_op jit(solution)/shard_map/all_to_all | solution.py:626
  106.9 0.1 reduce_sum.12
  107.0 1.1 broadcast_in_dim.30
  108.1 0.0 copy-done.12
  108.1 4.4 %all-to-all-start.3 = ((bf16[32,112,128]{2,1,0:T(8,128)(2,1)}), bf16[32,112,128]{2,1,0:T(8,128)(2,1)S(1)}, u32[]{:S(2)}, u32[]{:S(2)}) async-start(bf16[32,112,128]{2,1,0:T(8,128)(2,1)} %broadcast_in_dim.30), calls=%async_computation.3 | async-start | bytes 1835008 | tf_op jit(solution)/shard_map/all_to_all | solution.py:628
  112.5 8.2 %shard_map.107 = f32[4,2,512,128]{3,2,1,0:T(8,128)} custom-call(s32[1]{0:T(128)} %bitcast.odd_ref, bf16[32,16,128]{2,1,0:T(8,128)(2,1)} %copy-done.2, bf16[27,128,128]{2,1,0:T(8,128)(2,1)} %bitcast.61, f32[9,9,128]{2,1,0:T(8,128)} %reshape.83.rgb, bf16[4,512,128]{2,1,0:T(8,128)(2,1)} %copy-done.9, bf16[4,512,128]{2,1,0:T(8,128)(2,1)} %copy-done.12, ...), custom_call_target="tpu_custom_call" | custom-call | flops 4026531840 | bytes 5251588 | tf_op jit(solution)/shard_map/pallas_call | solution.py:32
  120.7 5.2 %all-to-all-done.3 = bf16[32,112,128]{2,1,0:T(8,128)(2,1)S(1)} async-done(((bf16[32,112,128]{2,1,0:T(8,128)(2,1)}), bf16[32,112,128]{2,1,0:T(8,128)(2,1)S(1)}, u32[]{:S(2)}, u32[]{:S(2)}) %all-to-all-start.3) | async-done | bytes 917536 | tf_op jit(solution)/shard_map/all_to_all | solution.py:628
  125.9 1.3 %convert_multiply_fusion = f32[3456,128]{1,0:T(8,128)} fusion(bf16[3584,128]{1,0:T(8,128)(2,1)S(1)} %bitcast.41), kind=kLoop, calls=%fused_computation | loop fusion | flops 884736 | bytes 2654208 | tf_op jit(solution)/shard_map/mul | solution.py:651
  127.2 0.6 mul.27
  (14 shorter events, 0.2 us)
Async XLA Ops:
  0.6 4.1 %copy-start.4 = (bf16[3,3,3,128,3]{3,4,2,1,0:T(4,128)(2,1)S(1)}, bf16[3,3,3,128,3]{3,4,2,1,0:T(4,128)(2,1)}, u32[]{:S(2)}) copy-start(bf16[3,3,3,128,3]{3,4,2,1,0:T(4,128)(2,1)} %param.10) | copy-start | bytes 62212
  0.6 4.8 %copy-start.5 = (bf16[4,2,512,3]{2,1,3,0:T(2,128)(2,1)S(1)}, bf16[4,2,512,3]{2,1,3,0:T(2,128)(2,1)}, u32[]{:S(2)}) copy-start(bf16[4,2,512,3]{2,1,3,0:T(2,128)(2,1)} %param.11) | copy-start | bytes 73732
  0.7 5.5 %copy-start.6 = (bf16[3,3,3,64]{3,2,1,0:T(4,128)(2,1)S(1)}, bf16[3,3,3,64]{3,2,1,0:T(4,128)(2,1)}, u32[]{:S(2)}) copy-start(bf16[3,3,3,64]{3,2,1,0:T(4,128)(2,1)} %param.12) | copy-start | bytes 10372
  0.7 5.5 %copy-start.3 = (bf16[3,3,3,3,64]{4,3,2,1,0:T(4,128)(2,1)S(1)}, bf16[3,3,3,3,64]{4,3,2,1,0:T(4,128)(2,1)}, u32[]{:S(2)}) copy-start(bf16[3,3,3,3,64]{4,3,2,1,0:T(4,128)(2,1)} %param.14) | copy-start | bytes 31108
  2.0 14.0 %collective-permute-start = (bf16[4,512,128]{2,1,0:T(8,128)(2,1)S(1)}, bf16[4,512,128]{2,1,0:T(8,128)(2,1)S(1)}, u32[]{:S(2)}, u32[]{:S(2)}) collective-permute-start(bf16[4,512,128]{2,1,0:T(8,128)(2,1)S(1)} %get-tuple-element.38), channel_id=1, source_target_pairs={{0,4},{4,0},{8,12},{12,8},{16,20},{20,16},{24,28},{28,24},{32,36},... | collective-permute-start | bytes 1572872 | tf_op jit(solution)/shard_map/ppermute | solution.py:526
  4.1 11.9 %collective-permute-start.1 = (bf16[4,512,128]{2,1,0:T(8,128)(2,1)S(1)}, bf16[4,512,128]{2,1,0:T(8,128)(2,1)S(1)}, u32[]{:S(2)}, u32[]{:S(2)}) collective-permute-start(bf16[4,512,128]{2,1,0:T(8,128)(2,1)S(1)} %get-tuple-element.37), channel_id=1, source_target_pairs={{4,8},{8,4},{12,16},{16,12},{20,24},{24,20},{28,32},{32,28},{36,40... | collective-permute-start | bytes 1572872 | tf_op jit(solution)/shard_map/ppermute | solution.py:527
  16.0 0.8 copy-start.10
  16.0 1.0 copy-start.11
  17.0 24.0 %copy-start.13 = (f32[64]{0:T(128)S(1)}, f32[64]{0:T(128)}, u32[]{:S(2)}) copy-start(f32[64]{0:T(128)} %param.15) | copy-start | bytes 772
  17.0 24.1 %copy-start.1 = (bf16[3,3,64,128]{3,2,1,0:T(8,128)(2,1)S(1)}, bf16[3,3,64,128]{3,2,1,0:T(8,128)(2,1)}, u32[]{:S(2)}) copy-start(bf16[3,3,64,128]{3,2,1,0:T(8,128)(2,1)} %param.13) | copy-start | bytes 442372
  23.6 28.2 %all-to-all-start = ((f32[32,24,128]{2,1,0:T(8,128)}), f32[32,24,128]{2,1,0:T(8,128)S(1)}, u32[]{:S(2)}, u32[]{:S(2)}) async-start(f32[32,24,128]{2,1,0:T(8,128)} %get-tuple-element.23), calls=%async_computation | async-start | bytes 786432 | tf_op jit(solution)/shard_map/all_to_all | solution.py:585
  40.7 11.1 %copy-start.7 = (bf16[4,512,128]{2,1,0:T(8,128)(2,1)S(1)}, bf16[4,512,128]{2,1,0:T(8,128)(2,1)}, u32[]{:S(2)}) copy-start(bf16[4,512,128]{2,1,0:T(8,128)(2,1)} %get-tuple-element.26.first_in) | copy-start | bytes 1572868
  51.9 1.3 %copy-start = (f32[32,24,128]{2,1,0:T(8,128)}, f32[32,24,128]{2,1,0:T(8,128)S(1)}, u32[]{:S(2)}) copy-start(f32[32,24,128]{2,1,0:T(8,128)S(1)} %all-to-all-done) | copy-start | bytes 1179652
  51.9 11.2 %collective-permute-start.2 = (bf16[4,512,128]{2,1,0:T(8,128)(2,1)S(1)}, bf16[4,512,128]{2,1,0:T(8,128)(2,1)S(1)}, u32[]{:S(2)}, u32[]{:S(2)}) collective-permute-start(bf16[4,512,128]{2,1,0:T(8,128)(2,1)S(1)} %copy-done.7), channel_id=1, source_target_pairs={{0,4},{4,0},{8,12},{12,8},{16,20},{20,16},{24,28},{28,24},{32,36},... | collective-permute-start | bytes 1572872 | tf_op jit(solution)/shard_map/ppermute | solution.py:587
  53.2 13.9 %copy-start.8 = (bf16[4,512,128]{2,1,0:T(8,128)(2,1)S(1)}, bf16[4,512,128]{2,1,0:T(8,128)(2,1)}, u32[]{:S(2)}) copy-start(bf16[4,512,128]{2,1,0:T(8,128)(2,1)} %get-tuple-element.33.second_in) | copy-start | bytes 1572868
  63.0 24.6 %copy-start.9 = (bf16[4,512,128]{2,1,0:T(8,128)(2,1)}, bf16[4,512,128]{2,1,0:T(8,128)(2,1)S(1)}, u32[]{:S(2)}) copy-start(bf16[4,512,128]{2,1,0:T(8,128)(2,1)S(1)} %collective-permute-done.2.first) | copy-start | bytes 1572868
  63.0 14.3 %all-to-all-start.1 = ((bf16[32,16,128]{2,1,0:T(8,128)(2,1)}), bf16[32,16,128]{2,1,0:T(8,128)(2,1)S(1)}, u32[]{:S(2)}, u32[]{:S(2)}) async-start(bf16[32,16,128]{2,1,0:T(8,128)(2,1)} %bitcast.49), calls=%async_computation.1 | async-start | bytes 262144 | tf_op jit(solution)/shard_map/all_to_all | solution.py:600
  67.1 20.5 %collective-permute-start.3 = (bf16[4,512,128]{2,1,0:T(8,128)(2,1)S(1)}, bf16[4,512,128]{2,1,0:T(8,128)(2,1)S(1)}, u32[]{:S(2)}, u32[]{:S(2)}) collective-permute-start(bf16[4,512,128]{2,1,0:T(8,128)(2,1)S(1)} %copy-done.8), channel_id=1, source_target_pairs={{4,8},{8,4},{12,16},{16,12},{20,24},{24,20},{28,32},{32,28},{36,40... | collective-permute-start | bytes 1572872 | tf_op jit(solution)/shard_map/ppermute | solution.py:599
  77.3 0.7 copy-start.2
  87.6 20.5 %copy-start.12 = (bf16[4,512,128]{2,1,0:T(8,128)(2,1)}, bf16[4,512,128]{2,1,0:T(8,128)(2,1)S(1)}, u32[]{:S(2)}) copy-start(bf16[4,512,128]{2,1,0:T(8,128)(2,1)S(1)} %collective-permute-done.3.second) | copy-start | bytes 1572868
  108.1 17.8 %all-to-all-start.3 = ((bf16[32,112,128]{2,1,0:T(8,128)(2,1)}), bf16[32,112,128]{2,1,0:T(8,128)(2,1)S(1)}, u32[]{:S(2)}, u32[]{:S(2)}) async-start(bf16[32,112,128]{2,1,0:T(8,128)(2,1)} %broadcast_in_dim.30), calls=%async_computation.3 | async-start | bytes 1835008 | tf_op jit(solution)/shard_map/all_to_all | solution.py:628

commit v3 on v2

--- a/solution.py
+++ b/solution.py
@@ -8,8 +8,10 @@
 F32 = jnp.float32
 BF16 = jnp.bfloat16
 HBM = pltpu.HBM
-EDGE_MIB = 56
-PREPARE_MIB = 56
+PREPARE_MIB = 24
+EDGE_MIB = 24
+ROWS = 80000
+SLOTS = 80
 HALO = 4
 
 
@@ -79,21 +81,24 @@
     return [(a, f + step * (a - 1)) for a in range(3) if 0 <= f + step * (a - 1) < 4]
 
 
-def wide_taps(field, taps, cols):
-    return jnp.concatenate([field[g * cols : (g + 1) * cols, :] for _, g in taps], axis=1)
-
-
-def conv_rows(field, kernel, f, cols):
+def wide_taps(field, taps):
+    return jnp.concatenate([field[g] for _, g in taps], axis=1)
+
+
+def conv_rows(field, kernel, f):
     taps = frames_of(f, 1)
     kernel = kernel[taps[0][0] * 256 : (taps[-1][0] + 1) * 256, :]
-    wide = dot(wide_taps(field, taps, cols), kernel)
+    wide = dot(wide_taps(field, taps), kernel)
     return before(wide[:, :256]) + wide[:, 256:512] + after(wide[:, 512:])
 
 
-def conv_rows_t(field, kernel, f, cols):
+def conv_rows_t(pairs, f):
     taps = frames_of(f, -1)
     lanes = slice(taps[0][0] * 256, (taps[-1][0] + 1) * 256)
-    wide = dot(wide_taps(field, taps, cols), kernel[:, lanes], ((1,), (1,)))
+    wide = sum(
+        dot(wide_taps(field, taps), kernel[:, lanes], ((1,), (1,)))
+        for field, kernel in pairs
+    )
     return after(wide[:, :256]) + wide[:, 256:512] + before(wide[:, 512:])
 
 
@@ -109,8 +114,24 @@
                         place(a * 256 + j * 128, e * 256 + r * 128, tap, j - r + 1)
 
 
-def prepare_kernel(latent, dec, rgb, edge, pre, colour, own, field, scr):
-    cols = latent.shape[2]
+def rows_kernel(odd_ref, latent, first, second, sems):
+    odd = odd_ref[0]
+    copies = [
+        start(latent.at[:, 1 - odd], first, sems.at[0]),
+        start(latent.at[:, odd], second, sems.at[1]),
+    ]
+    for copy in copies:
+        copy.wait()
+
+
+def prepare_kernel(
+    latent, dec, rgb, vgg_first, vgg_second, critic,
+    edge, pre, colour, branch,
+    own, field, scr, w1_f, w1, w2, sems,
+):
+    loads = [
+        start(latent.at[:, r], field.at[:, :, pl.ds(r * 128, 128)], sems.at[r]) for r in range(2)
+    ]
 
     def put_own(one, two, tap, b):
         own[one : one + 128, two : two + 128] = tap[b]
@@ -121,60 +142,89 @@
     edge[...] = jnp.zeros_like(edge)
     blocks_of(dec, False, put_own)
     blocks_of(dec, True, put_edge)
+    w1_f[...] = jnp.zeros_like(w1_f)
+    w2[...] = jnp.zeros_like(w2)
+    for p in range(2):
+        lanes = slice(p * 64, p * 64 + 64)
+        kinds = (lanes, slice(128 + p * 64, 192 + p * 64))
+        for b in range(3):
+            rr = p + b
+            for e in range(3):
+                at, tap = (e * 256 + rr * 64, (b * 3 + e) * 64)
+                w2[at : at + 64, p * 128 : p * 128 + 128] = vgg_second[tap : tap + 64, :]
+                at, tap = ((3 + e) * 16 + rr * 3, (b * 3 + e) * 3)
+                w1_f[at : at + 3, kinds[0]] = vgg_first[tap : tap + 3, lanes]
+                for a in range(3):
+                    at, tap = ((a * 3 + e) * 16 + rr * 3, ((a * 3 + b) * 3 + e) * 3)
+                    w1_f[at : at + 3, kinds[1]] = critic[tap : tap + 3, lanes]
+    w1[...] = w1_f[...].astype(BF16)
+    stores = [
+        start(w2, branch.at[pl.ds(0, 768)], sems.at[2]),
+        start(w1, branch.at[pl.ds(768, 144)], sems.at[3]),
+    ]
+    for load in loads:
+        load.wait()
     for f in range(4):
-        for r in range(2):
-            field[f * cols : (f + 1) * cols, r * 128 : (r + 1) * 128] = latent[f, r]
-    for f in range(4):
-        pre[f] = conv_rows(field, own, f, cols)
+        pre[f] = conv_rows(field, own, f)
     colour_rows(rgb, scr, (0, 1))
     colour[...] = scr[...].astype(BF16)
+    for store in stores:
+        store.wait()
 
 
 def edge_kernel(
     odd_ref, first, second, kernel, own, colour, target,
-    act, send_first, send_second, field, parts_out,
-    act_s, slope_s, field_s, t_scr, p_scr, parts, sems,
+    kept, parts,
+    act_s, slope_s, field_s, t_scr, p_scr, sems,
 ):
     odd = odd_ref[0]
     cols = first.shape[1]
+    copies = []
+
+    def keep(source, target):
+        copies.append(start(source, target, sems.at[len(copies)]))
+
+    for f in range(4):
+        field_s[f, :, :128] = jnp.where(odd == 1, first[f], second[f])
+        field_s[f, :, 128:] = jnp.where(odd == 1, second[f], first[f])
+    keep(first, kept.at[3 - odd])
+    keep(second, kept.at[2 + odd])
+    for f in range(4):
+        pre = own[f] + conv_rows(field_s, kernel, f)
+        gate = sigmoid(pre)
+        act = (pre * gate).astype(BF16)
+        slope = slope_of(pre, gate).astype(BF16)
+        for r in range(2):
+            act_s[r, f] = act[:, r * 128 : (r + 1) * 128]
+            slope_s[r, f] = slope[:, r * 128 : (r + 1) * 128]
+        keep(slope_s.at[1 - odd, f], kept.at[0, f])
+        keep(slope_s.at[odd, f], kept.at[1, f])
+        keep(act_s.at[0, f], kept.at[4, f])
+        keep(act_s.at[1, f], kept.at[5, f])
+    wide = dot(wide_act(act_s), colour[...], ((1,), (1,)))
+    part = before(wide[:, :128]) + wide[:, 128:256] + after(wide[:, 256:])
     t_scr[...] = jnp.zeros_like(t_scr)
     for f in range(4):
         t_scr[f * 24 + 18 : f * 24 + 24, :] = target[f * 6 : f * 6 + 6, :].astype(F32)
     p_scr[0:8, :] = jnp.zeros((8, 128), F32)
     p_scr[cols : cols + 8, :] = jnp.zeros((8, 128), F32)
-    for f in range(4):
-        rows = slice(f * cols, (f + 1) * cols)
-        field_s[rows, :128] = jnp.where(odd == 1, first[f], second[f])
-        field_s[rows, 128:] = jnp.where(odd == 1, second[f], first[f])
-    copies = [
-        start(field_s.at[pl.ds(f * cols, cols)], field.at[f], sems.at[f]) for f in range(4)
-    ]
-    for f in range(4):
-        pre = own[f] + conv_rows(field_s, kernel, f, cols)
-        gate = sigmoid(pre)
-        act_s[:, f * 256 : (f + 1) * 256] = (pre * gate).astype(BF16)
-        slope = slope_of(pre, gate).astype(BF16)
-        slope_s[0, f] = slope[:, :128]
-        slope_s[1, f] = slope[:, 128:]
-    copies.append(start(slope_s.at[1 - odd], send_first, sems.at[4]))
-    copies.append(start(slope_s.at[odd], send_second, sems.at[5]))
-    copies.append(start(act_s, act, sems.at[6]))
-    wide = dot(act_s[...], colour[...], ((1,), (1,)))
-    part = before(wide[:, :128]) + wide[:, 128:256] + after(wide[:, 256:])
     p_scr[HALO : HALO + cols, :] = part + t_scr[...].T
     blocks, width, _ = parts.shape
     for d in range(blocks):
         at = d * (width - 2 * HALO)
         parts[d] = p_scr[at : at + width, :]
-    copies.append(start(parts, parts_out, sems.at[7]))
     for copy in copies:
         copy.wait()
+
+
+def wide_act(act):
+    return jnp.concatenate([act[r, f] for f in range(4) for r in range(2)], axis=1)
 
 
 def branch_scratch(bands, wide):
     return [
         pltpu.VMEM((bands * wide, 128), F32),
-        pltpu.VMEM((wide + 1, 8, 128), F32),
+        pltpu.VMEM((1, 64), F32),
         pltpu.VMEM((768, 256), BF16),
         pltpu.VMEM((144, 256), BF16),
         pltpu.VMEM((256, 144), BF16),
@@ -194,15 +244,20 @@
 
 
 def branch_kernel(
-    parts_in, consts_in, w2_in, w1_in,
+    me_ref, parts_in, branch_in, head_in,
     out,
-    parts, consts, w2_t, w1_t, w1, w1_z, w2, w2_b,
+    parts, head_row, w2_t, w1_t, w1, w1_z, w2, w2_b,
     rows, taps, colours, feats, slopes, grads_two, grads, turned, sems,
 ):
     copies = [
         start(source, target, sems.at[k])
         for k, (source, target) in enumerate(
-            [(parts_in, parts), (consts_in, consts), (w2_in, w2_t), (w1_in, w1_t)]
+            [
+                (parts_in, parts),
+                (branch_in.at[pl.ds(0, 768)], w2_t),
+                (branch_in.at[pl.ds(768, 144)], w1_t),
+                (head_in, head_row),
+            ]
         )
     ]
     wide = rows.shape[0]
@@ -242,8 +297,13 @@
             axis=1,
         )
 
+    def inside(column):
+        place = column + me_ref[0] * own - HALO
+        kept = jnp.logical_and(place >= 0, place < own * bands)
+        return jnp.full((1, 128), jnp.where(kept, 1.0, 0.0), F32)
+
     def masks(first):
-        return jnp.concatenate([consts[first + n][0:1] for n in range(4)], axis=1)
+        return jnp.concatenate([inside(first + n) for n in range(4)], axis=1)
 
     taps[...] = jnp.zeros_like(taps)
     colours[...] = jnp.zeros_like(colours)
@@ -258,7 +318,8 @@
         for a in range(3):
             at = (a * 3 + e) * 16
             w1_z[a * 16 : (a + 1) * 16, e * 256 : (e + 1) * 256] = w1_t[at : at + 16, :]
-    head = consts[wide].T[:, 0:1]
+    head = jnp.broadcast_to(head_row[...], (8, 64)).T[:, 0:1]
+    head = jnp.concatenate([head, head], axis=0)
 
     for k in range(wide // 4):
         block = jnp.concatenate(
@@ -271,7 +332,7 @@
                 value = jnp.where(frame == f, piece, value)
             rows[4 * k + m] = value
 
-    mask = consts[0:wide, 0:1, :]
+    mask = jnp.stack([inside(column) for column in range(wide)])
 
     def place(even, odd):
         taps[:, 0:3, :] = down(odd)
@@ -379,20 +440,21 @@
 
 
 def dec_grad_kernel(
-    odd_ref, grad_in, colour_in, first_in, second_in, act_in, latent, edge_in,
-    local_out, grad_pre,
+    odd_ref, grad_in, colour_in, kept, latent,
+    local_out, grad_pre, grad_kept,
     local, colour, slope, act, field, pre_s, moved, gram, sems,
 ):
-    cols = act.shape[0]
+    cols = act.shape[2]
     odd = odd_ref[0]
     moves = [
         (colour_in, colour),
-        (first_in, slope.at[1 - odd]),
-        (second_in, slope.at[odd]),
-        (act_in, act),
+        (kept.at[0], slope.at[1 - odd]),
+        (kept.at[1], slope.at[odd]),
+        (kept.at[pl.ds(4, 2)], act),
         (latent.at[:, 0], field.at[:, :, pl.ds(0, 128)]),
         (latent.at[:, 1], field.at[:, :, pl.ds(128, 128)]),
-        (edge_in, field.at[:, :, pl.ds(256, 256)]),
+        (kept.at[2], field.at[:, :, pl.ds(256, 128)]),
+        (kept.at[3], field.at[:, :, pl.ds(384, 128)]),
     ]
     copies = [start(source, target, sems.at[k]) for k, (source, target) in enumerate(moves)]
     taps = taps_of(grad_in, cols)
@@ -404,16 +466,17 @@
         wide = grad_act[:, f * 256 : (f + 1) * 256]
         zero = (wide[:, :128] * slope[0, f].astype(F32)).astype(BF16)
         one = (wide[:, 128:] * slope[1, f].astype(F32)).astype(BF16)
-        pre_s[f * cols : (f + 1) * cols, :128] = zero
-        pre_s[f * cols : (f + 1) * cols, 128:] = one
+        pre_s[f, :, :128] = zero
+        pre_s[f, :, 128:] = one
         turned = jnp.concatenate([zero.astype(F32).T, one.astype(F32).T], axis=0)
         later = jnp.where(lane < cols - 1, pltpu.roll(turned, cols - 1, 1), 0.0)
         sooner = jnp.where(lane >= 1, pltpu.roll(turned, 1, 1), 0.0)
         for e, value in enumerate((later, turned, sooner)):
             moved[e * 256 : (e + 1) * 256, f * cols : (f + 1) * cols] = value.astype(BF16)
-    outs = [start(pre_s, grad_pre, sems.at[7])]
+    outs = [start(pre_s, grad_pre, sems.at[8])]
+    outs.append(start(grad_in, grad_kept, sems.at[7]))
     copies[3].wait()
-    gram[...] = dot(taps.T.astype(BF16), act[...])
+    gram[...] = dot(taps.T.astype(BF16), wide_act(act))
     rows = []
     for a in range(3):
         sums = []
@@ -434,6 +497,8 @@
     for k, value in enumerate(rows):
         gram[k * 3 : k * 3 + 3, 0:128] = value
     local[27 * 128 :, :] = gram[0:128, 0:128].astype(BF16)
+    last = pl.ds(27 * 128, 128)
+    outs.append(start(local.at[last], local_out.at[last], sems.at[36]))
     for copy in copies[4:]:
         copy.wait()
     rows_of = (2, 0, 1, 3)
@@ -448,8 +513,8 @@
                 total = wide[:128, one : one + 128] + wide[128:, two : two + 128]
                 at = ((a * 3 + b) * 3 + e) * 128
                 local[at : at + 128, :] = total.T.astype(BF16)
-        part = pl.ds(a * 9 * 128, 9 * 128 if a < 2 else 10 * 128)
-        outs.append(start(local.at[part], local_out.at[part], sems.at[8 + a]))
+                part = pl.ds(at, 128)
+                outs.append(start(local.at[part], local_out.at[part], sems.at[9 + at // 128]))
     for copy in outs:
         copy.wait()
 
@@ -457,10 +522,11 @@
 def latent_kernel(
     odd_ref, grad_in, dec, rgb, first, second, pre,
     out,
-    own_t, edge_t, colour, edge_s, scr,
+    own_t, edge_t, colour, edge_s, scr, out_s, sems,
 ):
     cols = first.shape[1]
     odd = odd_ref[0]
+    copies = []
     colour_rows(rgb, scr, (-1, 2))
     colour[...] = scr[...].astype(BF16)
 
@@ -483,28 +549,14 @@
         for k in range(2):
             at = (f * 2 + k) * 128
             value = grad_act[:, at : at + 128] * slopes[k].astype(F32)
-            edge_s[f * cols : (f + 1) * cols, k * 128 : (k + 1) * 128] = value.astype(BF16)
+            edge_s[f, :, k * 128 : (k + 1) * 128] = value.astype(BF16)
     for f in range(4):
-        wide = conv_rows_t(pre, own_t, f, cols) + conv_rows_t(edge_s, edge_t, f, cols)
-        out[f, 0] = wide[:, :128]
-        out[f, 1] = wide[:, 128:]
-
-
-def branch_weights(vgg_first, vgg_second, critic):
-    def paired(taps):
-        none = jnp.zeros_like(taps[..., :1, :, :])
-        return jnp.stack(
-            [jnp.concatenate([taps, none], -3), jnp.concatenate([none, taps], -3)], axis=-4
-        )
-
-    first = paired(vgg_first.reshape(3, 9, 64)).reshape(1, 2, 4, 3, 3, 64)
-    crit = paired(critic.reshape(3, 3, 9, 64)).reshape(3, 2, 4, 3, 3, 64)
-    both = jnp.stack([jnp.pad(first, ((1, 1),) + ((0, 0),) * 5), crit])
-    w1_t = both.transpose(1, 4, 3, 5, 0, 2, 6).reshape(9, 12, 256)
-    w1_t = jnp.pad(w1_t, ((0, 0), (0, 4), (0, 0))).reshape(144, 256)
-    w2_t = paired(vgg_second.transpose(1, 0, 2, 3))
-    w2_t = w2_t.transpose(0, 2, 3, 1, 4).reshape(768, 256)
-    return (w2_t, w1_t)
+        wide = conv_rows_t([(pre, own_t), (edge_s, edge_t)], f)
+        out_s[f, 0] = wide[:, :128]
+        out_s[f, 1] = wide[:, 128:]
+        copies.append(start(out_s.at[f], out.at[f], sems.at[f]))
+    for copy in copies:
+        copy.wait()
 
 
 def per_device(
@@ -520,49 +572,48 @@
     odd = me % 2
     odd_ref = (jnp.reshape(odd, (1,)).astype(jnp.int32), pltpu.SMEM)
 
-    def row(index):
-        return lax.dynamic_index_in_dim(latent, index, 1, keepdims=False)
-
-    first = lax.ppermute(row(1 - odd), "band", first_pairs)
-    second = lax.ppermute(row(odd), "band", second_pairs)
+    half = shape((4, cols, 128), BF16)
+    sent_first, sent_second = call(
+        rows_kernel,
+        [half, half],
+        odd_ref,
+        (latent, HBM),
+        scratch=[pltpu.SemaphoreType.DMA((2,))],
+        limit=16,
+    )
+    first = lax.ppermute(sent_first, "band", first_pairs)
+    second = lax.ppermute(sent_second, "band", second_pairs)
     rgb = rgb_kernel.transpose(0, 2, 1, 4, 3)[:, :, ::-1].reshape(9, 9, 128).astype(F32)
     big = 4 * cols * 768 * 640
     square = shape((768, 768), BF16)
     toeplitz = shape((384, 1024), BF16)
-    half = shape((4, cols, 128), BF16)
-    field = shape((4 * cols, 256), BF16)
+    field = shape((4, cols, 256), BF16)
     dma = pltpu.SemaphoreType.DMA
     dec = dec_kernel.reshape(27, 128, 128)
-    edge_w, pre_own, colour = call(
+    edge_w, pre_own, colour, branch = call(
         prepare_kernel,
-        [square, shape((4, cols, 256), F32), toeplitz],
-        latent,
+        [square, shape((4, cols, 256), F32), toeplitz, (shape((ROWS, 256), BF16), HBM)],
+        (latent, HBM),
         dec,
         rgb,
+        jnp.tile(vgg_first.reshape(27, 64).astype(F32), (1, 2)),
+        vgg_second.reshape(576, 128),
+        jnp.tile(critic_kernel.reshape(81, 64).astype(F32), (1, 2)),
         scratch=[
             pltpu.VMEM((768, 768), BF16),
-            pltpu.VMEM((4 * cols, 256), BF16),
+            pltpu.VMEM((4, cols, 256), BF16),
             pltpu.VMEM((384, 1024), F32),
+            pltpu.VMEM((144, 256), F32),
+            pltpu.VMEM((144, 256), BF16),
+            pltpu.VMEM((768, 256), BF16),
+            dma((4,)),
         ],
         macs=big,
         limit=PREPARE_MIB,
     )
-    w2_t, w1_t = branch_weights(vgg_first, vgg_second, critic_kernel)
-    place = jnp.arange(wide) + me * width - HALO
-    mask = jnp.where((place >= 0) & (place < cols), 1.0, 0.0).astype(F32)
-    consts = jnp.concatenate(
-        [jnp.broadcast_to(mask[:, None], (wide, 128)), jnp.tile(critic_head, 2)[None]]
-    )
-    consts = jnp.broadcast_to(consts[:, None], (wide + 1, 8, 128))
-    act, send_first, send_second, field_edge, parts = call(
+    kept, parts = call(
         edge_kernel,
-        [
-            (shape((cols, 1024), BF16), HBM),
-            (half, HBM),
-            (half, HBM),
-            (shape((4, cols, 256), BF16), HBM),
-            (shape((size, wide, 128), F32), HBM),
-        ],
+        [(shape((SLOTS, 4, cols, 128), BF16), HBM), shape((size, wide, 128), F32)],
         odd_ref,
         first,
         second,
@@ -571,66 +622,62 @@
         colour,
         target.transpose(0, 1, 3, 2).reshape(24, cols),
         scratch=[
-            pltpu.VMEM((cols, 1024), BF16),
             pltpu.VMEM((2, 4, cols, 128), BF16),
-            pltpu.VMEM((4 * cols, 256), BF16),
+            pltpu.VMEM((2, 4, cols, 128), BF16),
+            pltpu.VMEM((4, cols, 256), BF16),
             pltpu.VMEM((128, cols), F32),
             pltpu.VMEM((cols + 8, 128), F32),
-            pltpu.VMEM((size, wide, 128), F32),
-            dma((8,)),
+            dma((18,)),
         ],
         macs=big,
         limit=EDGE_MIB,
     )
     parts = lax.all_to_all(parts, "band", 0, 0)
-    parts, sent = lax.optimization_barrier((parts, send_first))
+    parts, sent = lax.optimization_barrier((parts, kept[0]))
     first = lax.ppermute(sent, "band", first_pairs)
     (grad_frames,) = call(
         branch_kernel,
         [shape((size * width, 128), BF16)],
+        (jnp.reshape(me, (1,)).astype(jnp.int32), pltpu.SMEM),
         (parts.reshape(size * wide, 128), HBM),
-        (consts, HBM),
-        (w2_t, HBM),
-        (w1_t, HBM),
+        (branch, HBM),
+        (critic_head.reshape(1, 64), HBM),
         scratch=branch_scratch(size, wide),
         macs=4 * 768 * 768 * 700,
     )
-    grad_frames, first, sent = lax.optimization_barrier((grad_frames, first, send_second))
+    grad_frames, sent = lax.optimization_barrier((grad_frames, kept[1]))
     second = lax.ppermute(sent, "band", second_pairs)
     grad_frames = lax.all_to_all(grad_frames.reshape(size, width, 128), "band", 0, 0)
-    local, grad_pre = call(
+    local, grad_pre, grad_kept = call(
         dec_grad_kernel,
-        [(shape((28 * 128, 128), BF16), HBM), (field, HBM)],
+        [(shape((28 * 128, 128), BF16), HBM), (field, HBM), (shape((size, width, 128), BF16), HBM)],
         odd_ref,
         grad_frames,
         (colour, HBM),
-        (send_first, HBM),
-        (send_second, HBM),
-        (act, HBM),
+        (kept, HBM),
         (latent, HBM),
-        (field_edge, HBM),
         scratch=[
             pltpu.VMEM((28 * 128, 128), BF16),
             pltpu.VMEM((384, 1024), BF16),
             pltpu.VMEM((2, 4, cols, 128), BF16),
-            pltpu.VMEM((cols, 1024), BF16),
+            pltpu.VMEM((2, 4, cols, 128), BF16),
             pltpu.VMEM((4, cols, 512), BF16),
-            pltpu.VMEM((4 * cols, 256), BF16),
+            pltpu.VMEM((4, cols, 256), BF16),
             pltpu.VMEM((768, 4 * cols), BF16),
             pltpu.VMEM((384, 1024), F32),
-            dma((11,)),
+            dma((37,)),
         ],
         macs=3 * big,
     )
-    local, second = lax.optimization_barrier((local, second))
+    local, first, second = lax.optimization_barrier((local, first, second))
     pieces = lax.all_to_all(local.reshape(size, -1, 128), "band", 0, 0)
     mine = jnp.sum(pieces.astype(F32), axis=0).astype(BF16)
     whole = lax.all_to_all(jnp.broadcast_to(mine, (size,) + mine.shape), "band", 0, 0)
     (grad_latent,) = call(
         latent_kernel,
-        [shape((4, 2, cols, 128), F32)],
+        [(shape((4, 2, cols, 128), F32), HBM)],
         odd_ref,
-        grad_frames,
+        grad_kept,
         dec,
         rgb,
         first,
@@ -640,8 +687,10 @@
             pltpu.VMEM((768, 768), BF16),
             pltpu.VMEM((768, 768), BF16),
             pltpu.VMEM((384, 1024), BF16),
-            pltpu.VMEM((4 * cols, 256), BF16),
+            pltpu.VMEM((4, cols, 256), BF16),
             pltpu.VMEM((384, 1024), F32),
+            pltpu.VMEM((4, 2, cols, 128), F32),
+            dma((4,)),
         ],
         macs=2 * big,
     )

time: 128 us -> 125 us (0.977)
  waiting for transfers between devices: 28.3 us -> 21.8 us
  Pallas kernels: 39.3 us -> 34 us
  starting transfers between devices: 29.4 us -> 33.8 us
  local copies, waits for them, and re-layouts: 8.95 us -> 11.5 us
    pallas_call x5 -> x6, Pallas kernels: 39.3 us -> 34 us  [call(): pl.pallas_call(kernel, out_shape=[o for o, _ in outs], in_specs=[pl.Block...]
    all_to_all x1, waiting for transfers between devices: 9.54 us -> 4.79 us  [per_device(): lax.all_to_all(grad_frames.reshape(size, width, 128), 'band', 0, 0)]
    ppermute x1, starting transfers between devices: 0.57 us -> 4.76 us  [per_device(): first = lax.ppermute(sent, 'band', first_pairs)]
    unnamed x31 -> x20, local copies, waits for them, and re-layouts: 2.49 us -> 5.95 us
    ppermute x2, waiting for transfers between devices: 3.76 us -> 1.49 us  [the longest x1 1.49 us: per_device(): first = lax.ppermute(sent_first, 'band', first_pairs)]
    convert_element_type x0 -> x3, local copies, waits for them, and re-layouts: none -> 1.56 us  [the longest x2 0.84 us: per_device(): critic_kernel.reshape(81, 64).astype(F32)]
  transfers between devices with their start and end apart: 7 -> 7, of which waited for: 5 -> 4; matrix products, arithmetic and copies ran while one was open for 4% -> 4% of each run, Pallas kernels for 26% -> 17%
where the time goes in v3:
time: 125 us; the launch traced here: 124 us
  Pallas kernels  34 us (27%)
  starting transfers between devices  33.8 us (27%)
  waiting for transfers between devices  21.8 us (17%)
  blocking collectives  19.5 us (16%)
  local copies, waits for them, and re-layouts  11.5 us (9%)
  other arithmetic  2.25 us (2%)
    pallas_call x6, Pallas kernels, call(): pl.pallas_call(kernel, out_shape=[o for o, _ in outs], in_specs=[pl.Block...  34 us
    all_to_all x1, blocking collectives, per_device(): pieces = lax.all_to_all(local.reshape(size, -1, 128), 'band', 0, 0)  19.5 us
    all_to_all x1, starting transfers between devices, per_device(): parts = lax.all_to_all(parts, 'band', 0, 0)  17.3 us
    all_to_all x1, waiting for transfers between devices, per_device(): parts = lax.all_to_all(parts, 'band', 0, 0)  9.78 us
    unnamed x20, local copies, waits for them, and re-layouts  5.95 us
    all_to_all x1, waiting for transfers between devices, per_device(): lax.all_to_all(jnp.broadcast_to(mine, (size,) + mine.shape), 'band', 0, 0)  5.73 us
    all_to_all x1, waiting for transfers between devices, per_device(): lax.all_to_all(grad_frames.reshape(size, width, 128), 'band', 0, 0)  4.79 us
    ppermute x1, starting transfers between devices, per_device(): first = lax.ppermute(sent, 'band', first_pairs)  4.76 us
  transfers between devices with their start and end apart: 7, of which 4 were waited for; matrix products, arithmetic and copies ran while one was open for 4% of the time, Pallas kernels for 17%

profile of v3, /device:TPU:0, one launch (start us, length us, event | category | flops | bytes accessed | tf_op | source)
XLA Modules:
  0.0 123.6 jit_solution(13615311610345753915)
XLA Ops:
  0.6 0.0 copy-start
  0.7 1.2 copy-done
  1.9 0.1 shard_map.103
  2.0 2.1 %collective-permute-start = (bf16[4,512,128]{2,1,0:T(8,128)(2,1)S(1)}, bf16[4,512,128]{2,1,0:T(8,128)(2,1)S(1)}, u32[]{:S(2)}, u32[]{:S(2)}) collective-permute-start(bf16[4,512,128]{2,1,0:T(8,128)(2,1)S(1)} %get-tuple-element.21), channel_id=1, source_target_pairs={{0,4},{4,0},{8,12},{12,8},{16,20},{20,16},{24,28},{28,24},{32,36},... | collective-permute-start | bytes 1572872 | tf_op jit(solution)/shard_map/ppermute | solution.py:584
  4.0 0.7 collective-permute-start.1
  4.7 0.7 reshape.78
  5.5 0.1 tile.9.vgg_first
  5.6 0.8 copy.16
  6.3 0.8 reshape.79
  7.1 0.1 copy.14
  7.2 0.1 copy.15.critic
  7.3 0.8 reverse_convert_fusion
  8.1 0.0 copy-start.3
  8.1 0.0 copy-start.1
  8.1 1.2 %copy-done.1 = bf16[4,2,512,128]{3,2,1,0:T(8,128)(2,1)S(1)} copy-done((bf16[4,2,512,128]{3,2,1,0:T(8,128)(2,1)S(1)}, bf16[4,2,512,128]{3,2,1,0:T(8,128)(2,1)}, u32[]{:S(2)}) %copy-start.1) | copy-done | bytes 1048600
  9.4 0.0 copy-start.4
  9.4 1.2 copy-done.4
  10.5 0.0 copy-start.5
  10.5 0.9 copy-done.5
  11.4 3.0 %shard_map.104 = (bf16[768,768]{1,0:T(8,128)(2,1)S(1)}, f32[4,512,256]{2,1,0:T(8,128)S(1)}, bf16[384,1024]{1,0:T(8,128)(2,1)S(1)}, bf16[80000,256]{1,0:T(8,128)(2,1)}) custom-call(bf16[4,2,512,128]{3,2,1,0:T(8,128)(2,1)S(1)} %copy-done.1, bf16[27,128,128]{2,1,0:T(8,128)(2,1)S(1)} %bitcast.19, f32[9,9,128]{2,1,0:T(8,128)S(1)} %reshape.77.rgb, ...), custom_call_target="tpu_custom_call" | custom-call | flops 2013265920 | bytes 47200768 | tf_op jit(solution)/shard_map/pallas_call | solution.py:34
  14.5 0.0 copy-done.3
  14.5 0.0 copy-start.2
  14.5 1.5 %collective-permute-done.first = bf16[4,512,128]{2,1,0:T(8,128)(2,1)S(1)} collective-permute-done((bf16[4,512,128]{2,1,0:T(8,128)(2,1)S(1)}, bf16[4,512,128]{2,1,0:T(8,128)(2,1)S(1)}, u32[]{:S(2)}, u32[]{:S(2)}) %collective-permute-start) | collective-permute-done | bytes 524320 | tf_op jit(solution)/shard_map/ppermute | solution.py:584
  16.0 0.0 collective-permute-done.1.second
  16.0 4.8 %shard_map.105 = (bf16[80,4,512,128]{3,2,1,0:T(8,128)(2,1)}, f32[32,24,128]{2,1,0:T(8,128)}) custom-call(s32[1]{0:T(128)} %bitcast.odd_ref, bf16[4,512,128]{2,1,0:T(8,128)(2,1)S(1)} %collective-permute-done.first, bf16[4,512,128]{2,1,0:T(8,128)(2,1)S(1)} %collective-permute-done.1.second, bf16[768,768]{1,0:T(8,128)(2,1)S(1)} %get-tuple-element.23.kernel, ...), custom_call_target="tpu_custom_call" | custom-call | flops 2013265920 | bytes 47472644 | tf_op jit(solution)/shard_map/pallas_call | solution.py:34
  20.8 0.0 copy-done.2
  20.8 17.3 %all-to-all-start = ((f32[32,24,128]{2,1,0:T(8,128)}), f32[32,24,128]{2,1,0:T(8,128)S(1)}, u32[]{:S(2)}, u32[]{:S(2)}) async-start(f32[32,24,128]{2,1,0:T(8,128)} %get-tuple-element.26), calls=%async_computation | async-start | bytes 786432 | tf_op jit(solution)/shard_map/all_to_all | solution.py:635
  38.1 1.3 %slice_bitcast_fusion = (bf16[4,512,128]{2,1,0:T(8,128)(2,1)S(1)}, bf16[4,512,128]{2,1,0:T(8,128)(2,1)S(1)}) fusion(bf16[80,4,512,128]{3,2,1,0:T(8,128)(2,1)} %get-tuple-element.27.kept), kind=kLoop, calls=%fused_computation.1 | loop fusion | bytes 2097152 | tf_op jit(solution)/shard_map/squeeze | solution.py:648
  39.4 9.8 %all-to-all-done = f32[32,24,128]{2,1,0:T(8,128)S(1)} async-done(((f32[32,24,128]{2,1,0:T(8,128)}), f32[32,24,128]{2,1,0:T(8,128)S(1)}, u32[]{:S(2)}, u32[]{:S(2)}) %all-to-all-start) | async-done | bytes 393248 | tf_op jit(solution)/shard_map/all_to_all | solution.py:635
  49.2 0.0 copy-start.6
  49.2 0.7 copy-done.6
  49.9 8.6 %shard_map.106 = bf16[512,128]{1,0:T(8,128)(2,1)} custom-call(s32[1]{0:T(128)} %bitcast.1.me_ref, f32[768,128]{1,0:T(8,128)} %bitcast.24, bf16[80000,256]{1,0:T(8,128)(2,1)} %get-tuple-element.29.branch_in, f32[1,64]{1,0:T(1,128)} %bitcast.31), custom_call_target="tpu_custom_call" | custom-call | flops 3303014400 | bytes 41484548 | tf_op jit(solution)/shard_map/pallas_call | solution.py:34
  58.6 3.9 %all-to-all-start.1 = ((bf16[32,16,128]{2,1,0:T(8,128)(2,1)}), bf16[32,16,128]{2,1,0:T(8,128)(2,1)S(1)}, u32[]{:S(2)}, u32[]{:S(2)}) async-start(bf16[32,16,128]{2,1,0:T(8,128)(2,1)} %bitcast.26), calls=%async_computation.1 | async-start | bytes 262144 | tf_op jit(solution)/shard_map/all_to_all | solution.py:650
  62.5 0.7 collective-permute-start.3
  63.2 4.8 %collective-permute-start.2 = (bf16[4,512,128]{2,1,0:T(8,128)(2,1)S(1)}, bf16[4,512,128]{2,1,0:T(8,128)(2,1)S(1)}, u32[]{:S(2)}, u32[]{:S(2)}) collective-permute-start(bf16[4,512,128]{2,1,0:T(8,128)(2,1)S(1)} %get-tuple-element.33), channel_id=1, source_target_pairs={{0,4},{4,0},{8,12},{12,8},{16,20},{20,16},{24,28},{28,24},{32,36},... | collective-permute-start | bytes 1572872 | tf_op jit(solution)/shard_map/ppermute | solution.py:637
  67.9 4.8 %all-to-all-done.1.grad_in = bf16[32,16,128]{2,1,0:T(8,128)(2,1)S(1)} async-done(((bf16[32,16,128]{2,1,0:T(8,128)(2,1)}), bf16[32,16,128]{2,1,0:T(8,128)(2,1)S(1)}, u32[]{:S(2)}, u32[]{:S(2)}) %all-to-all-start.1) | async-done | bytes 131104 | tf_op jit(solution)/shard_map/all_to_all | solution.py:650
  72.7 0.0 copy-start.7
  72.7 0.6 copy-done.7
  73.4 9.7 %shard_map.107 = (bf16[3584,128]{1,0:T(8,128)(2,1)}, bf16[4,512,256]{2,1,0:T(8,128)(2,1)}, bf16[32,16,128]{2,1,0:T(8,128)(2,1)}) custom-call(s32[1]{0:T(128)} %bitcast.odd_ref, bf16[32,16,128]{2,1,0:T(8,128)(2,1)} %copy-done.7, bf16[384,1024]{1,0:T(8,128)(2,1)} %copy-done.2, bf16[80,4,512,128]{3,2,1,0:T(8,128)(2,1)} %get-tuple-element.27.kept, ...), custom_call_target="tpu_custom_call" | custom-call | flops 6039797760 | bytes 46006276 | tf_op jit(solution)/shard_map/pallas_call | solution.py:34
  83.1 0.0 collective-permute-done.3.second
  83.1 0.0 copy-start.8
  83.1 0.0 collective-permute-done.2.first
  83.2 0.0 copy-start.9
  83.2 19.5 %all_to_all.20 = bf16[32,112,128]{2,1,0:T(8,128)(2,1)S(1)} all-to-all(bf16[32,112,128]{2,1,0:T(8,128)(2,1)} %bitcast.25), channel_id=1, replica_groups=mesh['band'=32,'clip'=4] {'band'}, dimensions={0} | all-to-all | bytes 1835008 | tf_op jit(solution)/shard_map/all_to_all | solution.py:673
  102.6 0.1 reduce_sum.12
  102.8 1.1 broadcast_in_dim.3
  103.8 0.0 copy-done.8
  103.8 0.0 copy-done.9
  103.8 4.4 %all-to-all-start.3 = ((bf16[32,112,128]{2,1,0:T(8,128)(2,1)}), bf16[32,112,128]{2,1,0:T(8,128)(2,1)S(1)}, u32[]{:S(2)}, u32[]{:S(2)}) async-start(bf16[32,112,128]{2,1,0:T(8,128)(2,1)} %broadcast_in_dim.3), calls=%async_computation.3 | async-start | bytes 1835008 | tf_op jit(solution)/shard_map/all_to_all | solution.py:675
  108.3 7.7 %shard_map.108 = f32[4,2,512,128]{3,2,1,0:T(8,128)} custom-call(s32[1]{0:T(128)} %bitcast.odd_ref, bf16[32,16,128]{2,1,0:T(8,128)(2,1)} %get-tuple-element.31.grad_in, bf16[27,128,128]{2,1,0:T(8,128)(2,1)} %bitcast.18, f32[9,9,128]{2,1,0:T(8,128)} %copy-done.3, bf16[4,512,128]{2,1,0:T(8,128)(2,1)} %copy-done.9, bf16[4,512,128]{2,1,0:T(8,128)(2,1)} %copy-done.8, ...), custom_call_target="tpu_custom_call" | custom-call | flops 4026531840 | bytes 5251588 | tf_op jit(solution)/shard_map/pallas_call | solution.py:34
  115.9 5.7 %all-to-all-done.3 = bf16[32,112,128]{2,1,0:T(8,128)(2,1)S(1)} async-done(((bf16[32,112,128]{2,1,0:T(8,128)(2,1)}), bf16[32,112,128]{2,1,0:T(8,128)(2,1)S(1)}, u32[]{:S(2)}, u32[]{:S(2)}) %all-to-all-start.3) | async-done | bytes 917536 | tf_op jit(solution)/shard_map/all_to_all | solution.py:675
  121.7 1.3 %convert_multiply_fusion = f32[3456,128]{1,0:T(8,128)} fusion(bf16[3584,128]{1,0:T(8,128)(2,1)S(1)} %bitcast.22), kind=kLoop, calls=%fused_computation | loop fusion | flops 884736 | bytes 2654208 | tf_op jit(solution)/shard_map/mul | solution.py:700
  123.0 0.6 mul.23
  (6 shorter events, 0.1 us)
Async XLA Ops:
  0.6 1.2 copy-start
  2.0 14.0 %collective-permute-start = (bf16[4,512,128]{2,1,0:T(8,128)(2,1)S(1)}, bf16[4,512,128]{2,1,0:T(8,128)(2,1)S(1)}, u32[]{:S(2)}, u32[]{:S(2)}) collective-permute-start(bf16[4,512,128]{2,1,0:T(8,128)(2,1)S(1)} %get-tuple-element.21), channel_id=1, source_target_pairs={{0,4},{4,0},{8,12},{12,8},{16,20},{20,16},{24,28},{28,24},{32,36},... | collective-permute-start | bytes 1572872 | tf_op jit(solution)/shard_map/ppermute | solution.py:584
  4.0 11.9 %collective-permute-start.1 = (bf16[4,512,128]{2,1,0:T(8,128)(2,1)S(1)}, bf16[4,512,128]{2,1,0:T(8,128)(2,1)S(1)}, u32[]{:S(2)}, u32[]{:S(2)}) collective-permute-start(bf16[4,512,128]{2,1,0:T(8,128)(2,1)S(1)} %get-tuple-element.22), channel_id=1, source_target_pairs={{4,8},{8,4},{12,16},{16,12},{20,24},{24,20},{28,32},{32,28},{36,40... | collective-permute-start | bytes 1572872 | tf_op jit(solution)/shard_map/ppermute | solution.py:585
  8.1 6.4 %copy-start.3 = (f32[9,9,128]{2,1,0:T(8,128)}, f32[9,9,128]{2,1,0:T(8,128)S(1)}, u32[]{:S(2)}) copy-start(f32[9,9,128]{2,1,0:T(8,128)S(1)} %reshape.77.rgb) | copy-start | bytes 124420
  8.1 1.3 %copy-start.1 = (bf16[4,2,512,128]{3,2,1,0:T(8,128)(2,1)S(1)}, bf16[4,2,512,128]{3,2,1,0:T(8,128)(2,1)}, u32[]{:S(2)}) copy-start(bf16[4,2,512,128]{3,2,1,0:T(8,128)(2,1)} %latent.5) | copy-start | bytes 3145732
  9.4 1.2 copy-start.4
  10.5 0.9 copy-start.5
  14.5 6.3 %copy-start.2 = (bf16[384,1024]{1,0:T(8,128)(2,1)}, bf16[384,1024]{1,0:T(8,128)(2,1)S(1)}, u32[]{:S(2)}) copy-start(bf16[384,1024]{1,0:T(8,128)(2,1)S(1)} %get-tuple-element.25.colour.colour_in) | copy-start | bytes 2359300
  20.8 28.4 %all-to-all-start = ((f32[32,24,128]{2,1,0:T(8,128)}), f32[32,24,128]{2,1,0:T(8,128)S(1)}, u32[]{:S(2)}, u32[]{:S(2)}) async-start(f32[32,24,128]{2,1,0:T(8,128)} %get-tuple-element.26), calls=%async_computation | async-start | bytes 786432 | tf_op jit(solution)/shard_map/all_to_all | solution.py:635
  49.2 0.7 copy-start.6
  58.6 14.1 %all-to-all-start.1 = ((bf16[32,16,128]{2,1,0:T(8,128)(2,1)}), bf16[32,16,128]{2,1,0:T(8,128)(2,1)S(1)}, u32[]{:S(2)}, u32[]{:S(2)}) async-start(bf16[32,16,128]{2,1,0:T(8,128)(2,1)} %bitcast.26), calls=%async_computation.1 | async-start | bytes 262144 | tf_op jit(solution)/shard_map/all_to_all | solution.py:650
  62.5 20.7 %collective-permute-start.3 = (bf16[4,512,128]{2,1,0:T(8,128)(2,1)S(1)}, bf16[4,512,128]{2,1,0:T(8,128)(2,1)S(1)}, u32[]{:S(2)}, u32[]{:S(2)}) collective-permute-start(bf16[4,512,128]{2,1,0:T(8,128)(2,1)S(1)} %get-tuple-element.34), channel_id=1, source_target_pairs={{4,8},{8,4},{12,16},{16,12},{20,24},{24,20},{28,32},{32,28},{36,40... | collective-permute-start | bytes 1572872 | tf_op jit(solution)/shard_map/ppermute | solution.py:649
  63.2 20.0 %collective-permute-start.2 = (bf16[4,512,128]{2,1,0:T(8,128)(2,1)S(1)}, bf16[4,512,128]{2,1,0:T(8,128)(2,1)S(1)}, u32[]{:S(2)}, u32[]{:S(2)}) collective-permute-start(bf16[4,512,128]{2,1,0:T(8,128)(2,1)S(1)} %get-tuple-element.33), channel_id=1, source_target_pairs={{0,4},{4,0},{8,12},{12,8},{16,20},{20,16},{24,28},{28,24},{32,36},... | collective-permute-start | bytes 1572872 | tf_op jit(solution)/shard_map/ppermute | solution.py:637
  72.7 0.6 copy-start.7
  83.1 20.7 %copy-start.8 = (bf16[4,512,128]{2,1,0:T(8,128)(2,1)}, bf16[4,512,128]{2,1,0:T(8,128)(2,1)S(1)}, u32[]{:S(2)}) copy-start(bf16[4,512,128]{2,1,0:T(8,128)(2,1)S(1)} %collective-permute-done.3.second) | copy-start | bytes 1572868
  83.2 20.7 %copy-start.9 = (bf16[4,512,128]{2,1,0:T(8,128)(2,1)}, bf16[4,512,128]{2,1,0:T(8,128)(2,1)S(1)}, u32[]{:S(2)}) copy-start(bf16[4,512,128]{2,1,0:T(8,128)(2,1)S(1)} %collective-permute-done.2.first) | copy-start | bytes 1572868
  103.8 17.8 %all-to-all-start.3 = ((bf16[32,112,128]{2,1,0:T(8,128)(2,1)}), bf16[32,112,128]{2,1,0:T(8,128)(2,1)S(1)}, u32[]{:S(2)}, u32[]{:S(2)}) async-start(bf16[32,112,128]{2,1,0:T(8,128)(2,1)} %broadcast_in_dim.3), calls=%async_computation.3 | async-start | bytes 1835008 | tf_op jit(solution)/shard_map/all_to_all | solution.py:675

commit v4 on v3

--- a/solution.py
+++ b/solution.py
@@ -1,3 +1,5 @@
+import functools
+
 import jax
 import jax.numpy as jnp
 from jax import lax
@@ -27,7 +29,7 @@
     return lax.dot_general(left, right, (contract, ((), ())), preferred_element_type=F32)
 
 
-def call(kernel, outs, *args, scratch=(), macs=0, limit=60):
+def call(kernel, outs, *args, scratch=(), macs=0, limit=60, aliases=None):
     args = [a if isinstance(a, tuple) else (a, pltpu.VMEM) for a in args]
     outs = [o if isinstance(o, tuple) else (o, pltpu.VMEM) for o in outs]
     moved = sum(a.size * a.dtype.itemsize for a, _ in args + outs)
@@ -37,6 +39,7 @@
         in_specs=[pl.BlockSpec(memory_space=m) for _, m in args],
         out_specs=[pl.BlockSpec(memory_space=m) for _, m in outs],
         scratch_shapes=list(scratch),
+        input_output_aliases=aliases or {},
         compiler_params=pltpu.CompilerParams(vmem_limit_bytes=limit * 1024 * 1024),
         cost_estimate=pl.CostEstimate(flops=2 * macs, bytes_accessed=moved, transcendentals=0),
     )(*[a for a, _ in args])
@@ -207,12 +210,12 @@
     for f in range(4):
         t_scr[f * 24 + 18 : f * 24 + 24, :] = target[f * 6 : f * 6 + 6, :].astype(F32)
     p_scr[0:8, :] = jnp.zeros((8, 128), F32)
-    p_scr[cols : cols + 8, :] = jnp.zeros((8, 128), F32)
+    p_scr[cols : cols + 16, :] = jnp.zeros((16, 128), F32)
     p_scr[HALO : HALO + cols, :] = part + t_scr[...].T
-    blocks, width, _ = parts.shape
+    blocks, length, _ = parts.shape
     for d in range(blocks):
-        at = d * (width - 2 * HALO)
-        parts[d] = p_scr[at : at + width, :]
+        at = d * (cols // blocks)
+        parts[d] = p_scr[at : at + length, :].astype(BF16)
     for copy in copies:
         copy.wait()
 
@@ -223,7 +226,7 @@
 
 def branch_scratch(bands, wide):
     return [
-        pltpu.VMEM((bands * wide, 128), F32),
+        pltpu.VMEM((bands * 2 * (wide - 2 * HALO), 128), F32),
         pltpu.VMEM((1, 64), F32),
         pltpu.VMEM((768, 256), BF16),
         pltpu.VMEM((144, 256), BF16),
@@ -239,7 +242,7 @@
         pltpu.VMEM((wide, 256, 128), BF16),
         pltpu.VMEM((wide, 256, 128), BF16),
         pltpu.VMEM((bands * (wide - 2 * HALO), 128), F32),
-        pltpu.SemaphoreType.DMA((4,)),
+        pltpu.SemaphoreType.DMA((3,)),
     ]
 
 
@@ -253,7 +256,6 @@
         start(source, target, sems.at[k])
         for k, (source, target) in enumerate(
             [
-                (parts_in, parts),
                 (branch_in.at[pl.ds(0, 768)], w2_t),
                 (branch_in.at[pl.ds(768, 144)], w1_t),
                 (head_in, head_row),
@@ -261,8 +263,9 @@
         )
     ]
     wide = rows.shape[0]
-    bands = parts.shape[0] // wide
     own = wide - 2 * HALO
+    bands = parts.shape[0] // (2 * own)
+    parts[...] = parts_in[...].astype(F32)
     lane = lax.broadcasted_iota(jnp.int32, (1, 128), 1)
     frame, band = (lane // bands, lane % bands)
 
@@ -309,6 +312,33 @@
     colours[...] = jnp.zeros_like(colours)
     grads_two[1] = jnp.zeros((256, 128), BF16)
     grads_two[wide - 2] = jnp.zeros((256, 128), BF16)
+    for k in range(wide // 4):
+        block = jnp.concatenate(
+            [parts[pl.ds(4 * k + m, bands, stride=2 * own), :] for m in range(4)], axis=0
+        ).T
+        for m in range(4):
+            value = jnp.zeros((24, 128), F32)
+            for f in range(4):
+                piece = rolled(block[f * 24 : (f + 1) * 24], (f - m) * bands)
+                value = jnp.where(frame == f, piece, value)
+            rows[4 * k + m] = value
+
+    mask = jnp.stack([inside(column) for column in range(wide)])
+
+    def place(even, odd):
+        taps[:, 0:3, :] = down(odd)
+        taps[:, 3:6, :] = even
+        taps[:, 6:9, :] = odd
+        taps[:, 9:12, :] = up(even)
+        return taps[...]
+
+    colours[0, 1 : wide + 1] = place(rows[:, 18:21, :] * mask, rows[:, 21:24, :] * mask).astype(BF16)
+    even = rounded((rows[:, 6:9, :] + down(rows[:, 12:15, :])) * mask)
+    odd = rounded((rows[:, 9:12, :] + up(rows[:, 3:6, :])) * mask)
+    field = place(even, odd)
+    for a, value in enumerate((earlier(field), field, later(field))):
+        colours[1 + a, 1 : wide + 1] = value.astype(BF16)
+
     for copy in copies:
         copy.wait()
     w1[...] = w1_t[...].astype(F32).T.astype(BF16)
@@ -320,33 +350,6 @@
             w1_z[a * 16 : (a + 1) * 16, e * 256 : (e + 1) * 256] = w1_t[at : at + 16, :]
     head = jnp.broadcast_to(head_row[...], (8, 64)).T[:, 0:1]
     head = jnp.concatenate([head, head], axis=0)
-
-    for k in range(wide // 4):
-        block = jnp.concatenate(
-            [parts[pl.ds(4 * k + m, bands, stride=wide), :] for m in range(4)], axis=0
-        ).T
-        for m in range(4):
-            value = jnp.zeros((24, 128), F32)
-            for f in range(4):
-                piece = rolled(block[f * 24 : (f + 1) * 24], (f - m) * bands)
-                value = jnp.where(frame == f, piece, value)
-            rows[4 * k + m] = value
-
-    mask = jnp.stack([inside(column) for column in range(wide)])
-
-    def place(even, odd):
-        taps[:, 0:3, :] = down(odd)
-        taps[:, 3:6, :] = even
-        taps[:, 6:9, :] = odd
-        taps[:, 9:12, :] = up(even)
-        return taps[...]
-
-    colours[0, 1 : wide + 1] = place(rows[:, 18:21, :] * mask, rows[:, 21:24, :] * mask).astype(BF16)
-    even = rounded((rows[:, 6:9, :] + down(rows[:, 12:15, :])) * mask)
-    odd = rounded((rows[:, 9:12, :] + up(rows[:, 3:6, :])) * mask)
-    field = place(even, odd)
-    for a, value in enumerate((earlier(field), field, later(field))):
-        colours[1 + a, 1 : wide + 1] = value.astype(BF16)
 
     def keep_feats(kind, first, feat):
         for n in range(4):
@@ -519,11 +522,9 @@
         copy.wait()
 
 
-def latent_kernel(
-    odd_ref, grad_in, dec, rgb, first, second, pre,
-    out,
-    own_t, edge_t, colour, edge_s, scr, out_s, sems,
-):
+def latent_kernel(frames, odd_ref, grad_in, dec, rgb, first, second, pre, *rest):
+    out, own_t, edge_t, colour, edge_s, scr, out_s, sems = rest[-8:]
+    needed = range(max(0, frames[0] - 1), min(4, frames[-1] + 2))
     cols = first.shape[1]
     odd = odd_ref[0]
     copies = []
@@ -541,7 +542,7 @@
     blocks_of(dec, False, put_own)
     blocks_of(dec, True, put_edge)
     grad_act = dot(taps_of(grad_in, cols).astype(BF16), colour[...])
-    for f in range(4):
+    for f in needed:
         slopes = (
             jnp.where(odd == 1, first[f], second[f]),
             jnp.where(odd == 1, second[f], first[f]),
@@ -550,11 +551,11 @@
             at = (f * 2 + k) * 128
             value = grad_act[:, at : at + 128] * slopes[k].astype(F32)
             edge_s[f, :, k * 128 : (k + 1) * 128] = value.astype(BF16)
-    for f in range(4):
+    for n, f in enumerate(frames):
         wide = conv_rows_t([(pre, own_t), (edge_s, edge_t)], f)
-        out_s[f, 0] = wide[:, :128]
-        out_s[f, 1] = wide[:, 128:]
-        copies.append(start(out_s.at[f], out.at[f], sems.at[f]))
+        out_s[n, 0] = wide[:, :128]
+        out_s[n, 1] = wide[:, 128:]
+        copies.append(start(out_s.at[n], out.at[f], sems.at[n]))
     for copy in copies:
         copy.wait()
 
@@ -613,7 +614,7 @@
     )
     kept, parts = call(
         edge_kernel,
-        [(shape((SLOTS, 4, cols, 128), BF16), HBM), shape((size, wide, 128), F32)],
+        [(shape((SLOTS, 4, cols, 128), BF16), HBM), shape((size, 2 * width, 128), BF16)],
         odd_ref,
         first,
         second,
@@ -626,7 +627,7 @@
             pltpu.VMEM((2, 4, cols, 128), BF16),
             pltpu.VMEM((4, cols, 256), BF16),
             pltpu.VMEM((128, cols), F32),
-            pltpu.VMEM((cols + 8, 128), F32),
+            pltpu.VMEM((cols + 16, 128), F32),
             dma((18,)),
         ],
         macs=big,
@@ -639,11 +640,12 @@
         branch_kernel,
         [shape((size * width, 128), BF16)],
         (jnp.reshape(me, (1,)).astype(jnp.int32), pltpu.SMEM),
-        (parts.reshape(size * wide, 128), HBM),
+        parts.reshape(size * 2 * width, 128),
         (branch, HBM),
         (critic_head.reshape(1, 64), HBM),
         scratch=branch_scratch(size, wide),
         macs=4 * 768 * 768 * 700,
+        limit=40,
     )
     grad_frames, sent = lax.optimization_barrier((grad_frames, kept[1]))
     second = lax.ppermute(sent, "band", second_pairs)
@@ -670,30 +672,38 @@
         macs=3 * big,
     )
     local, first, second = lax.optimization_barrier((local, first, second))
+    def latent_part(frames, *earlier):
+        (grad_latent,) = call(
+            functools.partial(latent_kernel, frames),
+            [(shape((4, 2, cols, 128), F32), HBM)],
+            odd_ref,
+            grad_kept,
+            dec,
+            rgb,
+            first,
+            second,
+            grad_pre,
+            *[(part, HBM) for part in earlier],
+            scratch=[
+                pltpu.VMEM((768, 768), BF16),
+                pltpu.VMEM((768, 768), BF16),
+                pltpu.VMEM((384, 1024), BF16),
+                pltpu.VMEM((4, cols, 256), BF16),
+                pltpu.VMEM((384, 1024), F32),
+                pltpu.VMEM((2, 2, cols, 128), F32),
+                dma((2,)),
+            ],
+            macs=big,
+            aliases={7: 0} if earlier else None,
+        )
+        return grad_latent
+
     pieces = lax.all_to_all(local.reshape(size, -1, 128), "band", 0, 0)
+    half_done = latent_part((0, 1))
     mine = jnp.sum(pieces.astype(F32), axis=0).astype(BF16)
+    mine, half_done = lax.optimization_barrier((mine, half_done))
     whole = lax.all_to_all(jnp.broadcast_to(mine, (size,) + mine.shape), "band", 0, 0)
-    (grad_latent,) = call(
-        latent_kernel,
-        [(shape((4, 2, cols, 128), F32), HBM)],
-        odd_ref,
-        grad_kept,
-        dec,
-        rgb,
-        first,
-        second,
-        grad_pre,
-        scratch=[
-            pltpu.VMEM((768, 768), BF16),
-            pltpu.VMEM((768, 768), BF16),
-            pltpu.VMEM((384, 1024), BF16),
-            pltpu.VMEM((4, cols, 256), BF16),
-            pltpu.VMEM((384, 1024), F32),
-            pltpu.VMEM((4, 2, cols, 128), F32),
-            dma((4,)),
-        ],
-        macs=2 * big,
-    )
+    grad_latent = latent_part((2, 3), half_done)
     whole = whole.reshape(28 * 128, 128)
     pixels = 4 * latent.shape[1] * size * cols
     factor = float(pixels) ** (-0.5)

time: 125 us -> 122 us (0.976)
  blocking collectives: 19.5 us -> 0 us
  waiting for transfers between devices: 21.8 us -> 30.8 us
  starting transfers between devices: 33.8 us -> 39.6 us
  Pallas kernels: 34 us -> 36.8 us
    all_to_all x1 -> x0, blocking collectives: 19.5 us -> none  [per_device(): pieces = lax.all_to_all(local.reshape(size, -1, 128), 'band', 0, 0)]
    all_to_all x0 -> x1, waiting for transfers between devices: none -> 7.88 us  [per_device(): pieces = lax.all_to_all(local.reshape(size, -1, 128), 'band', 0, 0)]
    all_to_all x0 -> x1, starting transfers between devices: none -> 5.98 us  [per_device(): pieces = lax.all_to_all(local.reshape(size, -1, 128), 'band', 0, 0)]
    pallas_call x6 -> x7, Pallas kernels: 34 us -> 36.8 us  [call(): pl.pallas_call(kernel, out_shape=[o for o, _ in outs], in_specs=[pl.Block...]
    all_to_all x1, waiting for transfers between devices: 5.73 us -> 7.25 us  [per_device(): lax.all_to_all(jnp.broadcast_to(mine, (size,) + mine.shape), 'band', 0, 0)]
  transfers between devices with their start and end apart: 7 -> 8, of which waited for: 4 -> 5; matrix products, arithmetic and copies ran while one was open for 4% -> 4% of each run, Pallas kernels for 17% -> 20%
where the time goes in v4:
time: 122 us; the launch traced here: 121 us
  starting transfers between devices  39.6 us (32%)
  Pallas kernels  36.8 us (30%)
  waiting for transfers between devices  30.8 us (25%)
  local copies, waits for them, and re-layouts  10.8 us (9%)
  other arithmetic  2.25 us (2%)
    pallas_call x7, Pallas kernels, call(): pl.pallas_call(kernel, out_shape=[o for o, _ in outs], in_specs=[pl.Block...  36.8 us
    all_to_all x1, starting transfers between devices, per_device(): parts = lax.all_to_all(parts, 'band', 0, 0)  17.3 us
    all_to_all x1, waiting for transfers between devices, per_device(): parts = lax.all_to_all(parts, 'band', 0, 0)  9.27 us
    all_to_all x1, waiting for transfers between devices, per_device(): pieces = lax.all_to_all(local.reshape(size, -1, 128), 'band', 0, 0)  7.88 us
    all_to_all x1, waiting for transfers between devices, per_device(): lax.all_to_all(jnp.broadcast_to(mine, (size,) + mine.shape), 'band', 0, 0)  7.25 us
    all_to_all x1, starting transfers between devices, per_device(): pieces = lax.all_to_all(local.reshape(size, -1, 128), 'band', 0, 0)  5.98 us
    unnamed x20, local copies, waits for them, and re-layouts  5.22 us
    all_to_all x1, waiting for transfers between devices, per_device(): lax.all_to_all(grad_frames.reshape(size, width, 128), 'band', 0, 0)  4.89 us
  transfers between devices with their start and end apart: 8, of which 5 were waited for; matrix products, arithmetic and copies ran while one was open for 4% of the time, Pallas kernels for 20%

profile of v4, /device:TPU:0, one launch (start us, length us, event | category | flops | bytes accessed | tf_op | source)
XLA Modules:
  0.0 121.2 jit_solution(3930462441252352548)
XLA Ops:
  0.6 0.0 copy-start
  0.7 1.2 %copy-done = bf16[4,2,512,128]{3,2,1,0:T(8,128)(2,1)S(1)} copy-done((bf16[4,2,512,128]{3,2,1,0:T(8,128)(2,1)S(1)}, bf16[4,2,512,128]{3,2,1,0:T(8,128)(2,1)}, u32[]{:S(2)}) %copy-start) | copy-done | bytes 1048600
  1.9 0.1 shard_map.103
  2.0 2.1 %collective-permute-start = (bf16[4,512,128]{2,1,0:T(8,128)(2,1)S(1)}, bf16[4,512,128]{2,1,0:T(8,128)(2,1)S(1)}, u32[]{:S(2)}, u32[]{:S(2)}) collective-permute-start(bf16[4,512,128]{2,1,0:T(8,128)(2,1)S(1)} %get-tuple-element.23), channel_id=1, source_target_pairs={{0,4},{4,0},{8,12},{12,8},{16,20},{20,16},{24,28},{28,24},{32,36},... | collective-permute-start | bytes 1572872 | tf_op jit(solution)/shard_map/ppermute | solution.py:585
  4.0 0.7 collective-permute-start.1
  4.7 0.7 reshape.78
  5.5 0.1 tile.9.vgg_first
  5.6 0.8 copy.17
  6.3 0.8 reshape.79
  7.1 0.1 copy.15
  7.2 0.1 copy.16.critic
  7.3 0.8 reverse_convert_fusion
  8.1 0.0 copy-start.3
  8.1 0.0 copy-start.1
  8.1 1.2 %copy-done.1 = bf16[4,2,512,128]{3,2,1,0:T(8,128)(2,1)S(1)} copy-done((bf16[4,2,512,128]{3,2,1,0:T(8,128)(2,1)S(1)}, bf16[4,2,512,128]{3,2,1,0:T(8,128)(2,1)}, u32[]{:S(2)}) %copy-start.1) | copy-done | bytes 1048600
  9.4 0.0 copy-start.5
  9.4 1.2 copy-done.5
  10.5 0.0 copy-start.6
  10.5 0.9 copy-done.6
  11.4 3.0 %shard_map.104 = (bf16[768,768]{1,0:T(8,128)(2,1)S(1)}, f32[4,512,256]{2,1,0:T(8,128)S(1)}, bf16[384,1024]{1,0:T(8,128)(2,1)S(1)}, bf16[80000,256]{1,0:T(8,128)(2,1)}) custom-call(bf16[4,2,512,128]{3,2,1,0:T(8,128)(2,1)S(1)} %copy-done.1, bf16[27,128,128]{2,1,0:T(8,128)(2,1)S(1)} %bitcast.22, f32[9,9,128]{2,1,0:T(8,128)S(1)} %reshape.77.rgb, ...), custom_call_target="tpu_custom_call" | custom-call | flops 2013265920 | bytes 47200768 | tf_op jit(solution)/shard_map/pallas_call | solution.py:36
  14.5 0.0 copy-done.3
  14.5 0.0 copy-start.2
  14.5 1.5 %collective-permute-done.first = bf16[4,512,128]{2,1,0:T(8,128)(2,1)S(1)} collective-permute-done((bf16[4,512,128]{2,1,0:T(8,128)(2,1)S(1)}, bf16[4,512,128]{2,1,0:T(8,128)(2,1)S(1)}, u32[]{:S(2)}, u32[]{:S(2)}) %collective-permute-start) | collective-permute-done | bytes 524320 | tf_op jit(solution)/shard_map/ppermute | solution.py:585
  16.0 0.0 collective-permute-done.1.second
  16.0 4.7 %shard_map.105 = (bf16[80,4,512,128]{3,2,1,0:T(8,128)(2,1)}, bf16[32,32,128]{2,1,0:T(8,128)(2,1)}) custom-call(s32[1]{0:T(128)} %bitcast.odd_ref, bf16[4,512,128]{2,1,0:T(8,128)(2,1)S(1)} %collective-permute-done.first, bf16[4,512,128]{2,1,0:T(8,128)(2,1)S(1)} %collective-permute-done.1.second, bf16[768,768]{1,0:T(8,128)(2,1)S(1)} %get-tuple-element.25.kernel, ...), custom_call_target="tpu_custom_call" | custom-call | flops 2013265920 | bytes 47341572 | tf_op jit(solution)/shard_map/pallas_call | solution.py:36
  20.7 0.0 copy-done.2
  20.7 0.0 copy-start.4
  20.7 17.3 %all-to-all-start = ((bf16[32,32,128]{2,1,0:T(8,128)(2,1)}), bf16[32,32,128]{2,1,0:T(8,128)(2,1)S(1)}, u32[]{:S(2)}, u32[]{:S(2)}) async-start(bf16[32,32,128]{2,1,0:T(8,128)(2,1)} %get-tuple-element.28), calls=%async_computation | async-start | bytes 524288 | tf_op jit(solution)/shard_map/all_to_all | solution.py:636
  38.0 1.3 %slice_bitcast_fusion = (bf16[4,512,128]{2,1,0:T(8,128)(2,1)S(1)}, bf16[4,512,128]{2,1,0:T(8,128)(2,1)S(1)}) fusion(bf16[80,4,512,128]{3,2,1,0:T(8,128)(2,1)} %get-tuple-element.29.kept), kind=kLoop, calls=%fused_computation.1 | loop fusion | bytes 2097152 | tf_op jit(solution)/shard_map/squeeze | solution.py:650
  39.3 9.3 %all-to-all-done = bf16[32,32,128]{2,1,0:T(8,128)(2,1)S(1)} async-done(((bf16[32,32,128]{2,1,0:T(8,128)(2,1)}), bf16[32,32,128]{2,1,0:T(8,128)(2,1)S(1)}, u32[]{:S(2)}, u32[]{:S(2)}) %all-to-all-start) | async-done | bytes 262176 | tf_op jit(solution)/shard_map/all_to_all | solution.py:636
  48.6 0.0 copy-done.4
  48.6 7.6 %shard_map.106 = bf16[512,128]{1,0:T(8,128)(2,1)} custom-call(s32[1]{0:T(128)} %bitcast.1.me_ref, bf16[1024,128]{1,0:T(8,128)(2,1)S(1)} %bitcast.18, bf16[80000,256]{1,0:T(8,128)(2,1)} %get-tuple-element.31.branch_in, f32[1,64]{1,0:T(1,128)S(1)} %bitcast.19), custom_call_target="tpu_custom_call" | custom-call | flops 3303014400 | bytes 41353476 | tf_op jit(solution)/shard_map/pallas_call | solution.py:36
  56.2 3.9 %all-to-all-start.1 = ((bf16[32,16,128]{2,1,0:T(8,128)(2,1)}), bf16[32,16,128]{2,1,0:T(8,128)(2,1)S(1)}, u32[]{:S(2)}, u32[]{:S(2)}) async-start(bf16[32,16,128]{2,1,0:T(8,128)(2,1)} %bitcast.11), calls=%async_computation.1 | async-start | bytes 262144 | tf_op jit(solution)/shard_map/all_to_all | solution.py:652
  60.1 0.7 collective-permute-start.3
  60.8 4.7 %collective-permute-start.2 = (bf16[4,512,128]{2,1,0:T(8,128)(2,1)S(1)}, bf16[4,512,128]{2,1,0:T(8,128)(2,1)S(1)}, u32[]{:S(2)}, u32[]{:S(2)}) collective-permute-start(bf16[4,512,128]{2,1,0:T(8,128)(2,1)S(1)} %get-tuple-element.35), channel_id=1, source_target_pairs={{0,4},{4,0},{8,12},{12,8},{16,20},{20,16},{24,28},{28,24},{32,36},... | collective-permute-start | bytes 1572872 | tf_op jit(solution)/shard_map/ppermute | solution.py:638
  65.5 4.9 %all-to-all-done.1.grad_in = bf16[32,16,128]{2,1,0:T(8,128)(2,1)S(1)} async-done(((bf16[32,16,128]{2,1,0:T(8,128)(2,1)}), bf16[32,16,128]{2,1,0:T(8,128)(2,1)S(1)}, u32[]{:S(2)}, u32[]{:S(2)}) %all-to-all-start.1) | async-done | bytes 131104 | tf_op jit(solution)/shard_map/all_to_all | solution.py:652
  70.4 0.0 copy-start.7
  70.4 0.6 copy-done.7
  71.0 9.8 %shard_map.107 = (bf16[3584,128]{1,0:T(8,128)(2,1)}, bf16[4,512,256]{2,1,0:T(8,128)(2,1)}, bf16[32,16,128]{2,1,0:T(8,128)(2,1)}) custom-call(s32[1]{0:T(128)} %bitcast.odd_ref, bf16[32,16,128]{2,1,0:T(8,128)(2,1)} %copy-done.7, bf16[384,1024]{1,0:T(8,128)(2,1)} %copy-done.2, bf16[80,4,512,128]{3,2,1,0:T(8,128)(2,1)} %get-tuple-element.29.kept, ...), custom_call_target="tpu_custom_call" | custom-call | flops 6039797760 | bytes 46006276 | tf_op jit(solution)/shard_map/pallas_call | solution.py:36
  80.8 0.0 collective-permute-done.3.second
  80.8 0.0 copy-start.8
  80.8 0.0 collective-permute-done.2.first
  80.8 0.0 copy-start.9
  80.8 6.0 %all-to-all-start.2 = ((bf16[32,112,128]{2,1,0:T(8,128)(2,1)}), bf16[32,112,128]{2,1,0:T(8,128)(2,1)S(1)}, u32[]{:S(2)}, u32[]{:S(2)}) async-start(bf16[32,112,128]{2,1,0:T(8,128)(2,1)} %bitcast.27), calls=%async_computation.2 | async-start | bytes 1835008 | tf_op jit(solution)/shard_map/all_to_all | solution.py:701
  86.8 0.0 copy-done.8
  86.8 0.0 copy-done.9
  86.8 5.5 %shard_map.108.rest_0_ = f32[4,2,512,128]{3,2,1,0:T(8,128)} custom-call(s32[1]{0:T(128)} %bitcast.odd_ref, bf16[32,16,128]{2,1,0:T(8,128)(2,1)} %get-tuple-element.33.grad_in, bf16[27,128,128]{2,1,0:T(8,128)(2,1)} %bitcast.20, f32[9,9,128]{2,1,0:T(8,128)} %copy-done.3, bf16[4,512,128]{2,1,0:T(8,128)(2,1)} %copy-done.9, bf16[4,512,128]{2,1,0:T(8,128)(2,1)} %copy-done.8, ...), custom_call_target="tpu_custom_call" | custom-call | flops 2013265920 | bytes 5251588 | tf_op jit(solution)/shard_map/pallas_call | solution.py:36
  92.3 7.9 %all-to-all-done.2 = bf16[32,112,128]{2,1,0:T(8,128)(2,1)S(1)} async-done(((bf16[32,112,128]{2,1,0:T(8,128)(2,1)}), bf16[32,112,128]{2,1,0:T(8,128)(2,1)S(1)}, u32[]{:S(2)}, u32[]{:S(2)}) %all-to-all-start.2) | async-done | bytes 917536 | tf_op jit(solution)/shard_map/all_to_all | solution.py:701
  100.2 0.1 reduce_sum.12
  100.4 1.1 broadcast_in_dim.3
  101.4 4.4 %all-to-all-start.3 = ((bf16[32,112,128]{2,1,0:T(8,128)(2,1)}), bf16[32,112,128]{2,1,0:T(8,128)(2,1)S(1)}, u32[]{:S(2)}, u32[]{:S(2)}) async-start(bf16[32,112,128]{2,1,0:T(8,128)(2,1)} %broadcast_in_dim.3), calls=%async_computation.3 | async-start | bytes 1835008 | tf_op jit(solution)/shard_map/all_to_all | solution.py:705
  105.8 6.1 %shard_map.109 = f32[4,2,512,128]{3,2,1,0:T(8,128)} custom-call(s32[1]{0:T(128)} %bitcast.odd_ref, bf16[32,16,128]{2,1,0:T(8,128)(2,1)} %get-tuple-element.33.grad_in, bf16[27,128,128]{2,1,0:T(8,128)(2,1)} %bitcast.21, f32[9,9,128]{2,1,0:T(8,128)} %copy-done.3, bf16[4,512,128]{2,1,0:T(8,128)(2,1)} %copy-done.9, ...), custom_call_target="tpu_custom_call", output_to_operand_aliasing={{}: (7, {})} | custom-call | flops 2013265920 | bytes 7348740 | tf_op jit(solution)/shard_map/pallas_call | solution.py:36
  111.9 7.2 %all-to-all-done.3 = bf16[32,112,128]{2,1,0:T(8,128)(2,1)S(1)} async-done(((bf16[32,112,128]{2,1,0:T(8,128)(2,1)}), bf16[32,112,128]{2,1,0:T(8,128)(2,1)S(1)}, u32[]{:S(2)}, u32[]{:S(2)}) %all-to-all-start.3) | async-done | bytes 917536 | tf_op jit(solution)/shard_map/all_to_all | solution.py:705
  119.2 1.3 %convert_multiply_fusion = f32[3456,128]{1,0:T(8,128)} fusion(bf16[3584,128]{1,0:T(8,128)(2,1)S(1)} %bitcast.25), kind=kLoop, calls=%fused_computation | loop fusion | flops 884736 | bytes 2654208 | tf_op jit(solution)/shard_map/mul | solution.py:710
  120.5 0.6 mul.23
  (6 shorter events, 0.1 us)
Async XLA Ops:
  0.6 1.2 %copy-start = (bf16[4,2,512,128]{3,2,1,0:T(8,128)(2,1)S(1)}, bf16[4,2,512,128]{3,2,1,0:T(8,128)(2,1)}, u32[]{:S(2)}) copy-start(bf16[4,2,512,128]{3,2,1,0:T(8,128)(2,1)} %latent.5) | copy-start | bytes 3145732
  2.0 14.0 %collective-permute-start = (bf16[4,512,128]{2,1,0:T(8,128)(2,1)S(1)}, bf16[4,512,128]{2,1,0:T(8,128)(2,1)S(1)}, u32[]{:S(2)}, u32[]{:S(2)}) collective-permute-start(bf16[4,512,128]{2,1,0:T(8,128)(2,1)S(1)} %get-tuple-element.23), channel_id=1, source_target_pairs={{0,4},{4,0},{8,12},{12,8},{16,20},{20,16},{24,28},{28,24},{32,36},... | collective-permute-start | bytes 1572872 | tf_op jit(solution)/shard_map/ppermute | solution.py:585
  4.0 11.9 %collective-permute-start.1 = (bf16[4,512,128]{2,1,0:T(8,128)(2,1)S(1)}, bf16[4,512,128]{2,1,0:T(8,128)(2,1)S(1)}, u32[]{:S(2)}, u32[]{:S(2)}) collective-permute-start(bf16[4,512,128]{2,1,0:T(8,128)(2,1)S(1)} %get-tuple-element.24), channel_id=1, source_target_pairs={{4,8},{8,4},{12,16},{16,12},{20,24},{24,20},{28,32},{32,28},{36,40... | collective-permute-start | bytes 1572872 | tf_op jit(solution)/shard_map/ppermute | solution.py:586
  8.1 6.4 %copy-start.3 = (f32[9,9,128]{2,1,0:T(8,128)}, f32[9,9,128]{2,1,0:T(8,128)S(1)}, u32[]{:S(2)}) copy-start(f32[9,9,128]{2,1,0:T(8,128)S(1)} %reshape.77.rgb) | copy-start | bytes 124420
  8.1 1.3 %copy-start.1 = (bf16[4,2,512,128]{3,2,1,0:T(8,128)(2,1)S(1)}, bf16[4,2,512,128]{3,2,1,0:T(8,128)(2,1)}, u32[]{:S(2)}) copy-start(bf16[4,2,512,128]{3,2,1,0:T(8,128)(2,1)} %latent.5) | copy-start | bytes 3145732
  9.4 1.2 copy-start.5
  10.5 0.9 copy-start.6
  14.5 6.2 %copy-start.2 = (bf16[384,1024]{1,0:T(8,128)(2,1)}, bf16[384,1024]{1,0:T(8,128)(2,1)S(1)}, u32[]{:S(2)}) copy-start(bf16[384,1024]{1,0:T(8,128)(2,1)S(1)} %get-tuple-element.27.colour.colour_in) | copy-start | bytes 2359300
  20.7 27.9 %copy-start.4 = (f32[64]{0:T(128)S(1)}, f32[64]{0:T(128)}, u32[]{:S(2)}) copy-start(f32[64]{0:T(128)} %param.15) | copy-start | bytes 772
  20.7 27.9 %all-to-all-start = ((bf16[32,32,128]{2,1,0:T(8,128)(2,1)}), bf16[32,32,128]{2,1,0:T(8,128)(2,1)S(1)}, u32[]{:S(2)}, u32[]{:S(2)}) async-start(bf16[32,32,128]{2,1,0:T(8,128)(2,1)} %get-tuple-element.28), calls=%async_computation | async-start | bytes 524288 | tf_op jit(solution)/shard_map/all_to_all | solution.py:636
  56.2 14.1 %all-to-all-start.1 = ((bf16[32,16,128]{2,1,0:T(8,128)(2,1)}), bf16[32,16,128]{2,1,0:T(8,128)(2,1)S(1)}, u32[]{:S(2)}, u32[]{:S(2)}) async-start(bf16[32,16,128]{2,1,0:T(8,128)(2,1)} %bitcast.11), calls=%async_computation.1 | async-start | bytes 262144 | tf_op jit(solution)/shard_map/all_to_all | solution.py:652
  60.1 20.7 %collective-permute-start.3 = (bf16[4,512,128]{2,1,0:T(8,128)(2,1)S(1)}, bf16[4,512,128]{2,1,0:T(8,128)(2,1)S(1)}, u32[]{:S(2)}, u32[]{:S(2)}) collective-permute-start(bf16[4,512,128]{2,1,0:T(8,128)(2,1)S(1)} %get-tuple-element.36), channel_id=1, source_target_pairs={{4,8},{8,4},{12,16},{16,12},{20,24},{24,20},{28,32},{32,28},{36,40... | collective-permute-start | bytes 1572872 | tf_op jit(solution)/shard_map/ppermute | solution.py:651
  60.8 20.0 %collective-permute-start.2 = (bf16[4,512,128]{2,1,0:T(8,128)(2,1)S(1)}, bf16[4,512,128]{2,1,0:T(8,128)(2,1)S(1)}, u32[]{:S(2)}, u32[]{:S(2)}) collective-permute-start(bf16[4,512,128]{2,1,0:T(8,128)(2,1)S(1)} %get-tuple-element.35), channel_id=1, source_target_pairs={{0,4},{4,0},{8,12},{12,8},{16,20},{20,16},{24,28},{28,24},{32,36},... | collective-permute-start | bytes 1572872 | tf_op jit(solution)/shard_map/ppermute | solution.py:638
  70.4 0.7 copy-start.7
  80.8 6.0 %copy-start.8 = (bf16[4,512,128]{2,1,0:T(8,128)(2,1)}, bf16[4,512,128]{2,1,0:T(8,128)(2,1)S(1)}, u32[]{:S(2)}) copy-start(bf16[4,512,128]{2,1,0:T(8,128)(2,1)S(1)} %collective-permute-done.3.second) | copy-start | bytes 1572868
  80.8 6.0 %copy-start.9 = (bf16[4,512,128]{2,1,0:T(8,128)(2,1)}, bf16[4,512,128]{2,1,0:T(8,128)(2,1)S(1)}, u32[]{:S(2)}) copy-start(bf16[4,512,128]{2,1,0:T(8,128)(2,1)S(1)} %collective-permute-done.2.first) | copy-start | bytes 1572868
  80.8 19.4 %all-to-all-start.2 = ((bf16[32,112,128]{2,1,0:T(8,128)(2,1)}), bf16[32,112,128]{2,1,0:T(8,128)(2,1)S(1)}, u32[]{:S(2)}, u32[]{:S(2)}) async-start(bf16[32,112,128]{2,1,0:T(8,128)(2,1)} %bitcast.27), calls=%async_computation.2 | async-start | bytes 1835008 | tf_op jit(solution)/shard_map/all_to_all | solution.py:701
  101.4 17.8 %all-to-all-start.3 = ((bf16[32,112,128]{2,1,0:T(8,128)(2,1)}), bf16[32,112,128]{2,1,0:T(8,128)(2,1)S(1)}, u32[]{:S(2)}, u32[]{:S(2)}) async-start(bf16[32,112,128]{2,1,0:T(8,128)(2,1)} %broadcast_in_dim.3), calls=%async_computation.3 | async-start | bytes 1835008 | tf_op jit(solution)/shard_map/all_to_all | solution.py:705

commit v5 on v4

--- a/solution.py
+++ b/solution.py
@@ -140,9 +140,9 @@
         own[one : one + 128, two : two + 128] = tap[b]
 
     def put_edge(one, two, tap, b):
-        edge[one : one + 128, two : two + 128] = tap[b]
-
-    edge[...] = jnp.zeros_like(edge)
+        one, two = (one // 256 * 128, two // 256 * 128)
+        edge[b // 2, one : one + 128, two : two + 128] = tap[b]
+
     blocks_of(dec, False, put_own)
     blocks_of(dec, True, put_edge)
     w1_f[...] = jnp.zeros_like(w1_f)
@@ -168,17 +168,35 @@
     for load in loads:
         load.wait()
     for f in range(4):
-        pre[f] = conv_rows(field, own, f)
+        both = conv_rows(field, own, f)
+        pre[0, f] = both[:, :128]
+        pre[1, f] = both[:, 128:]
     colour_rows(rgb, scr, (0, 1))
     colour[...] = scr[...].astype(BF16)
     for store in stores:
         store.wait()
 
 
+def edge_row(source, kernel, own, row, act, slope, keep):
+    for f in range(4):
+        taps = frames_of(f, 1)
+        part = kernel[row, taps[0][0] * 128 : (taps[-1][0] + 1) * 128, :]
+        wide = dot(wide_taps(source, taps), part)
+        pre = own[row, f] + before(wide[:, :128]) + wide[:, 128:256] + after(wide[:, 256:])
+        gate = sigmoid(pre)
+        act[f] = (pre * gate).astype(BF16)
+        slope[f] = slope_of(pre, gate).astype(BF16)
+        keep(f)
+
+
+def first_edge_kernel(odd_ref, first, kernel, own, act, slope):
+    edge_row(first, kernel, own, 1 - odd_ref[0], act, slope, lambda f: None)
+
+
 def edge_kernel(
-    odd_ref, first, second, kernel, own, colour, target,
+    odd_ref, first, second, kernel, own, colour, target, act_first, slope_first,
     kept, parts,
-    act_s, slope_s, field_s, t_scr, p_scr, sems,
+    act_s, slope_s, t_scr, p_scr, sems,
 ):
     odd = odd_ref[0]
     cols = first.shape[1]
@@ -187,23 +205,16 @@
     def keep(source, target):
         copies.append(start(source, target, sems.at[len(copies)]))
 
-    for f in range(4):
-        field_s[f, :, :128] = jnp.where(odd == 1, first[f], second[f])
-        field_s[f, :, 128:] = jnp.where(odd == 1, second[f], first[f])
+    def keep_frame(f):
+        keep(slope_s.at[f], kept.at[1, f])
+        keep(act_s.at[odd, f], kept.at[4 + odd, f])
+
     keep(first, kept.at[3 - odd])
     keep(second, kept.at[2 + odd])
-    for f in range(4):
-        pre = own[f] + conv_rows(field_s, kernel, f)
-        gate = sigmoid(pre)
-        act = (pre * gate).astype(BF16)
-        slope = slope_of(pre, gate).astype(BF16)
-        for r in range(2):
-            act_s[r, f] = act[:, r * 128 : (r + 1) * 128]
-            slope_s[r, f] = slope[:, r * 128 : (r + 1) * 128]
-        keep(slope_s.at[1 - odd, f], kept.at[0, f])
-        keep(slope_s.at[odd, f], kept.at[1, f])
-        keep(act_s.at[0, f], kept.at[4, f])
-        keep(act_s.at[1, f], kept.at[5, f])
+    keep(act_first, kept.at[5 - odd])
+    keep(slope_first, kept.at[0])
+    act_s[1 - odd] = act_first[...]
+    edge_row(second, kernel, own, odd, act_s.at[odd], slope_s, keep_frame)
     wide = dot(wide_act(act_s), colour[...], ((1,), (1,)))
     part = before(wide[:, :128]) + wide[:, 128:256] + after(wide[:, 256:])
     t_scr[...] = jnp.zeros_like(t_scr)
@@ -586,14 +597,13 @@
     second = lax.ppermute(sent_second, "band", second_pairs)
     rgb = rgb_kernel.transpose(0, 2, 1, 4, 3)[:, :, ::-1].reshape(9, 9, 128).astype(F32)
     big = 4 * cols * 768 * 640
-    square = shape((768, 768), BF16)
     toeplitz = shape((384, 1024), BF16)
     field = shape((4, cols, 256), BF16)
     dma = pltpu.SemaphoreType.DMA
     dec = dec_kernel.reshape(27, 128, 128)
     edge_w, pre_own, colour, branch = call(
         prepare_kernel,
-        [square, shape((4, cols, 256), F32), toeplitz, (shape((ROWS, 256), BF16), HBM)],
+        [shape((2, 384, 384), BF16), shape((2, 4, cols, 128), F32), toeplitz, (shape((ROWS, 256), BF16), HBM)],
         (latent, HBM),
         dec,
         rgb,
@@ -612,6 +622,9 @@
         macs=big,
         limit=PREPARE_MIB,
     )
+    act_first, slope_first = call(
+        first_edge_kernel, [half, half], odd_ref, first, edge_w, pre_own, macs=big // 2, limit=EDGE_MIB
+    )
     kept, parts = call(
         edge_kernel,
         [(shape((SLOTS, 4, cols, 128), BF16), HBM), shape((size, 2 * width, 128), BF16)],
@@ -622,13 +635,14 @@
         pre_own,
         colour,
         target.transpose(0, 1, 3, 2).reshape(24, cols),
+        act_first,
+        slope_first,
         scratch=[
             pltpu.VMEM((2, 4, cols, 128), BF16),
-            pltpu.VMEM((2, 4, cols, 128), BF16),
-            pltpu.VMEM((4, cols, 256), BF16),
+            pltpu.VMEM((4, cols, 128), BF16),
             pltpu.VMEM((128, cols), F32),
             pltpu.VMEM((cols + 16, 128), F32),
-            dma((18,)),
+            dma((12,)),
         ],
         macs=big,
         limit=EDGE_MIB,

time: 122 us -> 120 us (0.984)
    pallas_call x7 -> x8, Pallas kernels: 36.8 us -> 36 us  [call(): pl.pallas_call(kernel, out_shape=[o for o, _ in outs], in_specs=[pl.Block...]
  transfers between devices with their start and end apart: 8 -> 8, of which waited for: 5 -> 5; matrix products, arithmetic and copies ran while one was open for 4% -> 4% of each run, Pallas kernels for 20% -> 21%
where the time goes in v5:
time: 120 us; the launch traced here: 119 us
  starting transfers between devices  38.6 us (32%)
  Pallas kernels  36 us (30%)
  waiting for transfers between devices  30.8 us (26%)
  local copies, waits for them, and re-layouts  10.8 us (9%)
  other arithmetic  2.25 us (2%)
    pallas_call x8, Pallas kernels, call(): pl.pallas_call(kernel, out_shape=[o for o, _ in outs], in_specs=[pl.Block...  36 us
    all_to_all x1, starting transfers between devices, per_device(): parts = lax.all_to_all(parts, 'band', 0, 0)  16.3 us
    all_to_all x1, waiting for transfers between devices, per_device(): parts = lax.all_to_all(parts, 'band', 0, 0)  9.27 us
    all_to_all x1, waiting for transfers between devices, per_device(): pieces = lax.all_to_all(local.reshape(size, -1, 128), 'band', 0, 0)  7.88 us
    all_to_all x1, waiting for transfers between devices, per_device(): lax.all_to_all(jnp.broadcast_to(mine, (size,) + mine.shape), 'band', 0, 0)  7.25 us
    all_to_all x1, starting transfers between devices, per_device(): pieces = lax.all_to_all(local.reshape(size, -1, 128), 'band', 0, 0)  6 us
    unnamed x20, local copies, waits for them, and re-layouts  5.22 us
    all_to_all x1, waiting for transfers between devices, per_device(): lax.all_to_all(grad_frames.reshape(size, width, 128), 'band', 0, 0)  4.89 us
  transfers between devices with their start and end apart: 8, of which 5 were waited for; matrix products, arithmetic and copies ran while one was open for 4% of the time, Pallas kernels for 21%

profile of v5, /device:TPU:0, one launch (start us, length us, event | category | flops | bytes accessed | tf_op | source)
XLA Modules:
  0.0 119.4 jit_solution(300941375938240318)
XLA Ops:
  0.6 0.0 copy-start
  0.7 1.2 %copy-done = bf16[4,2,512,128]{3,2,1,0:T(8,128)(2,1)S(1)} copy-done((bf16[4,2,512,128]{3,2,1,0:T(8,128)(2,1)S(1)}, bf16[4,2,512,128]{3,2,1,0:T(8,128)(2,1)}, u32[]{:S(2)}) %copy-start) | copy-done | bytes 1048600
  1.9 0.1 shard_map.103
  2.0 2.1 %collective-permute-start = (bf16[4,512,128]{2,1,0:T(8,128)(2,1)S(1)}, bf16[4,512,128]{2,1,0:T(8,128)(2,1)S(1)}, u32[]{:S(2)}, u32[]{:S(2)}) collective-permute-start(bf16[4,512,128]{2,1,0:T(8,128)(2,1)S(1)} %get-tuple-element.25), channel_id=1, source_target_pairs={{0,4},{4,0},{8,12},{12,8},{16,20},{20,16},{24,28},{28,24},{32,36},... | collective-permute-start | bytes 1572872 | tf_op jit(solution)/shard_map/ppermute | solution.py:596
  4.0 0.7 collective-permute-start.1
  4.7 0.7 reshape.78
  5.5 0.1 tile.9.vgg_first
  5.6 0.8 copy.17
  6.3 0.8 reshape.79
  7.1 0.1 copy.15
  7.2 0.1 copy.16.critic
  7.3 0.8 reverse_convert_fusion
  8.1 0.0 copy-start.3
  8.1 0.0 copy-start.1
  8.1 1.2 %copy-done.1 = bf16[4,2,512,128]{3,2,1,0:T(8,128)(2,1)S(1)} copy-done((bf16[4,2,512,128]{3,2,1,0:T(8,128)(2,1)S(1)}, bf16[4,2,512,128]{3,2,1,0:T(8,128)(2,1)}, u32[]{:S(2)}) %copy-start.1) | copy-done | bytes 1048600
  9.4 0.0 copy-start.5
  9.4 1.2 copy-done.5
  10.5 0.0 copy-start.6
  10.5 0.9 copy-done.6
  11.4 2.9 %shard_map.104 = (bf16[2,384,384]{2,1,0:T(8,128)(2,1)S(1)}, f32[2,4,512,128]{3,2,1,0:T(8,128)S(1)}, bf16[384,1024]{1,0:T(8,128)(2,1)S(1)}, bf16[80000,256]{1,0:T(8,128)(2,1)}) custom-call(bf16[4,2,512,128]{3,2,1,0:T(8,128)(2,1)S(1)} %copy-done.1, bf16[27,128,128]{2,1,0:T(8,128)(2,1)S(1)} %bitcast.22, f32[9,9,128]{2,1,0:T(8,128)S(1)} %reshape.77.rgb, ...), custom_call_target="tpu_custom_call" | custom-call | flops 2013265920 | bytes 46610944 | tf_op jit(solution)/shard_map/pallas_call | solution.py:36
  14.4 0.0 copy-done.3
  14.4 0.0 copy-start.2
  14.4 1.5 %collective-permute-done.first = bf16[4,512,128]{2,1,0:T(8,128)(2,1)S(1)} collective-permute-done((bf16[4,512,128]{2,1,0:T(8,128)(2,1)S(1)}, bf16[4,512,128]{2,1,0:T(8,128)(2,1)S(1)}, u32[]{:S(2)}, u32[]{:S(2)}) %collective-permute-start) | collective-permute-done | bytes 524320 | tf_op jit(solution)/shard_map/ppermute | solution.py:596
  16.0 1.0 shard_map.105
  17.0 0.0 collective-permute-done.1.second
  17.0 3.0 %shard_map.106 = (bf16[80,4,512,128]{3,2,1,0:T(8,128)(2,1)}, bf16[32,32,128]{2,1,0:T(8,128)(2,1)}) custom-call(s32[1]{0:T(128)} %bitcast.odd_ref, bf16[4,512,128]{2,1,0:T(8,128)(2,1)S(1)} %collective-permute-done.first, bf16[4,512,128]{2,1,0:T(8,128)(2,1)S(1)} %collective-permute-done.1.second, bf16[2,384,384]{2,1,0:T(8,128)(2,1)S(1)} %get-tuple-element.27.kernel, ...), custom_call_target="tpu_custom_call" | custom-call | flops 2013265920 | bytes 47800324 | tf_op jit(solution)/shard_map/pallas_call | solution.py:36
  20.0 0.0 copy-done.2
  20.0 0.0 copy-start.4
  20.0 16.3 %all-to-all-start = ((bf16[32,32,128]{2,1,0:T(8,128)(2,1)}), bf16[32,32,128]{2,1,0:T(8,128)(2,1)S(1)}, u32[]{:S(2)}, u32[]{:S(2)}) async-start(bf16[32,32,128]{2,1,0:T(8,128)(2,1)} %get-tuple-element.32), calls=%async_computation | async-start | bytes 524288 | tf_op jit(solution)/shard_map/all_to_all | solution.py:650
  36.3 1.3 %slice_bitcast_fusion = (bf16[4,512,128]{2,1,0:T(8,128)(2,1)S(1)}, bf16[4,512,128]{2,1,0:T(8,128)(2,1)S(1)}) fusion(bf16[80,4,512,128]{3,2,1,0:T(8,128)(2,1)} %get-tuple-element.33.kept), kind=kLoop, calls=%fused_computation.1 | loop fusion | bytes 2097152 | tf_op jit(solution)/shard_map/squeeze | solution.py:664
  37.6 9.3 %all-to-all-done = bf16[32,32,128]{2,1,0:T(8,128)(2,1)S(1)} async-done(((bf16[32,32,128]{2,1,0:T(8,128)(2,1)}), bf16[32,32,128]{2,1,0:T(8,128)(2,1)S(1)}, u32[]{:S(2)}, u32[]{:S(2)}) %all-to-all-start) | async-done | bytes 262176 | tf_op jit(solution)/shard_map/all_to_all | solution.py:650
  46.9 0.0 copy-done.4
  46.9 7.6 %shard_map.107 = bf16[512,128]{1,0:T(8,128)(2,1)} custom-call(s32[1]{0:T(128)} %bitcast.1.me_ref, bf16[1024,128]{1,0:T(8,128)(2,1)S(1)} %bitcast.18, bf16[80000,256]{1,0:T(8,128)(2,1)} %get-tuple-element.35.branch_in, f32[1,64]{1,0:T(1,128)S(1)} %bitcast.19), custom_call_target="tpu_custom_call" | custom-call | flops 3303014400 | bytes 41353476 | tf_op jit(solution)/shard_map/pallas_call | solution.py:36
  54.5 3.9 %all-to-all-start.1 = ((bf16[32,16,128]{2,1,0:T(8,128)(2,1)}), bf16[32,16,128]{2,1,0:T(8,128)(2,1)S(1)}, u32[]{:S(2)}, u32[]{:S(2)}) async-start(bf16[32,16,128]{2,1,0:T(8,128)(2,1)} %bitcast.11), calls=%async_computation.1 | async-start | bytes 262144 | tf_op jit(solution)/shard_map/all_to_all | solution.py:666
  58.4 0.7 collective-permute-start.3
  59.1 4.7 %collective-permute-start.2 = (bf16[4,512,128]{2,1,0:T(8,128)(2,1)S(1)}, bf16[4,512,128]{2,1,0:T(8,128)(2,1)S(1)}, u32[]{:S(2)}, u32[]{:S(2)}) collective-permute-start(bf16[4,512,128]{2,1,0:T(8,128)(2,1)S(1)} %get-tuple-element.39), channel_id=1, source_target_pairs={{0,4},{4,0},{8,12},{12,8},{16,20},{20,16},{24,28},{28,24},{32,36},... | collective-permute-start | bytes 1572872 | tf_op jit(solution)/shard_map/ppermute | solution.py:652
  63.7 4.9 %all-to-all-done.1.grad_in = bf16[32,16,128]{2,1,0:T(8,128)(2,1)S(1)} async-done(((bf16[32,16,128]{2,1,0:T(8,128)(2,1)}), bf16[32,16,128]{2,1,0:T(8,128)(2,1)S(1)}, u32[]{:S(2)}, u32[]{:S(2)}) %all-to-all-start.1) | async-done | bytes 131104 | tf_op jit(solution)/shard_map/all_to_all | solution.py:666
  68.6 0.0 copy-start.7
  68.6 0.6 copy-done.7
  69.3 9.8 %shard_map.108 = (bf16[3584,128]{1,0:T(8,128)(2,1)}, bf16[4,512,256]{2,1,0:T(8,128)(2,1)}, bf16[32,16,128]{2,1,0:T(8,128)(2,1)}) custom-call(s32[1]{0:T(128)} %bitcast.odd_ref, bf16[32,16,128]{2,1,0:T(8,128)(2,1)} %copy-done.7, bf16[384,1024]{1,0:T(8,128)(2,1)} %copy-done.2, bf16[80,4,512,128]{3,2,1,0:T(8,128)(2,1)} %get-tuple-element.33.kept, ...), custom_call_target="tpu_custom_call" | custom-call | flops 6039797760 | bytes 46006276 | tf_op jit(solution)/shard_map/pallas_call | solution.py:36
  79.0 0.0 collective-permute-done.3.second
  79.0 0.0 copy-start.8
  79.1 0.0 collective-permute-done.2.first
  79.1 0.0 copy-start.9
  79.1 6.0 %all-to-all-start.2 = ((bf16[32,112,128]{2,1,0:T(8,128)(2,1)}), bf16[32,112,128]{2,1,0:T(8,128)(2,1)S(1)}, u32[]{:S(2)}, u32[]{:S(2)}) async-start(bf16[32,112,128]{2,1,0:T(8,128)(2,1)} %bitcast.27), calls=%async_computation.2 | async-start | bytes 1835008 | tf_op jit(solution)/shard_map/all_to_all | solution.py:715
  85.1 0.0 copy-done.8
  85.1 0.0 copy-done.9
  85.1 5.5 %shard_map.109.rest_0_ = f32[4,2,512,128]{3,2,1,0:T(8,128)} custom-call(s32[1]{0:T(128)} %bitcast.odd_ref, bf16[32,16,128]{2,1,0:T(8,128)(2,1)} %get-tuple-element.37.grad_in, bf16[27,128,128]{2,1,0:T(8,128)(2,1)} %bitcast.20, f32[9,9,128]{2,1,0:T(8,128)} %copy-done.3, bf16[4,512,128]{2,1,0:T(8,128)(2,1)} %copy-done.9, bf16[4,512,128]{2,1,0:T(8,128)(2,1)} %copy-done.8, ...), custom_call_target="tpu_custom_call" | custom-call | flops 2013265920 | bytes 5251588 | tf_op jit(solution)/shard_map/pallas_call | solution.py:36
  90.6 7.9 %all-to-all-done.2 = bf16[32,112,128]{2,1,0:T(8,128)(2,1)S(1)} async-done(((bf16[32,112,128]{2,1,0:T(8,128)(2,1)}), bf16[32,112,128]{2,1,0:T(8,128)(2,1)S(1)}, u32[]{:S(2)}, u32[]{:S(2)}) %all-to-all-start.2) | async-done | bytes 917536 | tf_op jit(solution)/shard_map/all_to_all | solution.py:715
  98.5 0.1 reduce_sum.12
  98.6 1.1 broadcast_in_dim.3
  99.7 4.4 %all-to-all-start.3 = ((bf16[32,112,128]{2,1,0:T(8,128)(2,1)}), bf16[32,112,128]{2,1,0:T(8,128)(2,1)S(1)}, u32[]{:S(2)}, u32[]{:S(2)}) async-start(bf16[32,112,128]{2,1,0:T(8,128)(2,1)} %broadcast_in_dim.3), calls=%async_computation.3 | async-start | bytes 1835008 | tf_op jit(solution)/shard_map/all_to_all | solution.py:719
  104.1 6.1 %shard_map.110 = f32[4,2,512,128]{3,2,1,0:T(8,128)} custom-call(s32[1]{0:T(128)} %bitcast.odd_ref, bf16[32,16,128]{2,1,0:T(8,128)(2,1)} %get-tuple-element.37.grad_in, bf16[27,128,128]{2,1,0:T(8,128)(2,1)} %bitcast.21, f32[9,9,128]{2,1,0:T(8,128)} %copy-done.3, bf16[4,512,128]{2,1,0:T(8,128)(2,1)} %copy-done.9, ...), custom_call_target="tpu_custom_call", output_to_operand_aliasing={{}: (7, {})} | custom-call | flops 2013265920 | bytes 7348740 | tf_op jit(solution)/shard_map/pallas_call | solution.py:36
  110.2 7.2 %all-to-all-done.3 = bf16[32,112,128]{2,1,0:T(8,128)(2,1)S(1)} async-done(((bf16[32,112,128]{2,1,0:T(8,128)(2,1)}), bf16[32,112,128]{2,1,0:T(8,128)(2,1)S(1)}, u32[]{:S(2)}, u32[]{:S(2)}) %all-to-all-start.3) | async-done | bytes 917536 | tf_op jit(solution)/shard_map/all_to_all | solution.py:719
  117.5 1.3 %convert_multiply_fusion = f32[3456,128]{1,0:T(8,128)} fusion(bf16[3584,128]{1,0:T(8,128)(2,1)S(1)} %bitcast.25), kind=kLoop, calls=%fused_computation | loop fusion | flops 884736 | bytes 2654208 | tf_op jit(solution)/shard_map/mul | solution.py:724
  118.8 0.6 mul.23
  (6 shorter events, 0.1 us)
Async XLA Ops:
  0.6 1.2 %copy-start = (bf16[4,2,512,128]{3,2,1,0:T(8,128)(2,1)S(1)}, bf16[4,2,512,128]{3,2,1,0:T(8,128)(2,1)}, u32[]{:S(2)}) copy-start(bf16[4,2,512,128]{3,2,1,0:T(8,128)(2,1)} %latent.5) | copy-start | bytes 3145732
  2.0 14.0 %collective-permute-start = (bf16[4,512,128]{2,1,0:T(8,128)(2,1)S(1)}, bf16[4,512,128]{2,1,0:T(8,128)(2,1)S(1)}, u32[]{:S(2)}, u32[]{:S(2)}) collective-permute-start(bf16[4,512,128]{2,1,0:T(8,128)(2,1)S(1)} %get-tuple-element.25), channel_id=1, source_target_pairs={{0,4},{4,0},{8,12},{12,8},{16,20},{20,16},{24,28},{28,24},{32,36},... | collective-permute-start | bytes 1572872 | tf_op jit(solution)/shard_map/ppermute | solution.py:596
  4.0 13.0 %collective-permute-start.1 = (bf16[4,512,128]{2,1,0:T(8,128)(2,1)S(1)}, bf16[4,512,128]{2,1,0:T(8,128)(2,1)S(1)}, u32[]{:S(2)}, u32[]{:S(2)}) collective-permute-start(bf16[4,512,128]{2,1,0:T(8,128)(2,1)S(1)} %get-tuple-element.26), channel_id=1, source_target_pairs={{4,8},{8,4},{12,16},{16,12},{20,24},{24,20},{28,32},{32,28},{36,40... | collective-permute-start | bytes 1572872 | tf_op jit(solution)/shard_map/ppermute | solution.py:597
  8.1 6.3 %copy-start.3 = (f32[9,9,128]{2,1,0:T(8,128)}, f32[9,9,128]{2,1,0:T(8,128)S(1)}, u32[]{:S(2)}) copy-start(f32[9,9,128]{2,1,0:T(8,128)S(1)} %reshape.77.rgb) | copy-start | bytes 124420
  8.1 1.3 %copy-start.1 = (bf16[4,2,512,128]{3,2,1,0:T(8,128)(2,1)S(1)}, bf16[4,2,512,128]{3,2,1,0:T(8,128)(2,1)}, u32[]{:S(2)}) copy-start(bf16[4,2,512,128]{3,2,1,0:T(8,128)(2,1)} %latent.5) | copy-start | bytes 3145732
  9.4 1.2 copy-start.5
  10.5 0.9 copy-start.6
  14.4 5.6 %copy-start.2 = (bf16[384,1024]{1,0:T(8,128)(2,1)}, bf16[384,1024]{1,0:T(8,128)(2,1)S(1)}, u32[]{:S(2)}) copy-start(bf16[384,1024]{1,0:T(8,128)(2,1)S(1)} %get-tuple-element.29.colour.colour_in) | copy-start | bytes 2359300
  20.0 26.9 %copy-start.4 = (f32[64]{0:T(128)S(1)}, f32[64]{0:T(128)}, u32[]{:S(2)}) copy-start(f32[64]{0:T(128)} %param.15) | copy-start | bytes 772
  20.0 26.9 %all-to-all-start = ((bf16[32,32,128]{2,1,0:T(8,128)(2,1)}), bf16[32,32,128]{2,1,0:T(8,128)(2,1)S(1)}, u32[]{:S(2)}, u32[]{:S(2)}) async-start(bf16[32,32,128]{2,1,0:T(8,128)(2,1)} %get-tuple-element.32), calls=%async_computation | async-start | bytes 524288 | tf_op jit(solution)/shard_map/all_to_all | solution.py:650
  54.5 14.1 %all-to-all-start.1 = ((bf16[32,16,128]{2,1,0:T(8,128)(2,1)}), bf16[32,16,128]{2,1,0:T(8,128)(2,1)S(1)}, u32[]{:S(2)}, u32[]{:S(2)}) async-start(bf16[32,16,128]{2,1,0:T(8,128)(2,1)} %bitcast.11), calls=%async_computation.1 | async-start | bytes 262144 | tf_op jit(solution)/shard_map/all_to_all | solution.py:666
  58.4 20.7 %collective-permute-start.3 = (bf16[4,512,128]{2,1,0:T(8,128)(2,1)S(1)}, bf16[4,512,128]{2,1,0:T(8,128)(2,1)S(1)}, u32[]{:S(2)}, u32[]{:S(2)}) collective-permute-start(bf16[4,512,128]{2,1,0:T(8,128)(2,1)S(1)} %get-tuple-element.40), channel_id=1, source_target_pairs={{4,8},{8,4},{12,16},{16,12},{20,24},{24,20},{28,32},{32,28},{36,40... | collective-permute-start | bytes 1572872 | tf_op jit(solution)/shard_map/ppermute | solution.py:665
  59.1 20.0 %collective-permute-start.2 = (bf16[4,512,128]{2,1,0:T(8,128)(2,1)S(1)}, bf16[4,512,128]{2,1,0:T(8,128)(2,1)S(1)}, u32[]{:S(2)}, u32[]{:S(2)}) collective-permute-start(bf16[4,512,128]{2,1,0:T(8,128)(2,1)S(1)} %get-tuple-element.39), channel_id=1, source_target_pairs={{0,4},{4,0},{8,12},{12,8},{16,20},{20,16},{24,28},{28,24},{32,36},... | collective-permute-start | bytes 1572872 | tf_op jit(solution)/shard_map/ppermute | solution.py:652
  68.6 0.6 copy-start.7
  79.0 6.0 %copy-start.8 = (bf16[4,512,128]{2,1,0:T(8,128)(2,1)}, bf16[4,512,128]{2,1,0:T(8,128)(2,1)S(1)}, u32[]{:S(2)}) copy-start(bf16[4,512,128]{2,1,0:T(8,128)(2,1)S(1)} %collective-permute-done.3.second) | copy-start | bytes 1572868
  79.1 6.0 %copy-start.9 = (bf16[4,512,128]{2,1,0:T(8,128)(2,1)}, bf16[4,512,128]{2,1,0:T(8,128)(2,1)S(1)}, u32[]{:S(2)}) copy-start(bf16[4,512,128]{2,1,0:T(8,128)(2,1)S(1)} %collective-permute-done.2.first) | copy-start | bytes 1572868
  79.1 19.4 %all-to-all-start.2 = ((bf16[32,112,128]{2,1,0:T(8,128)(2,1)}), bf16[32,112,128]{2,1,0:T(8,128)(2,1)S(1)}, u32[]{:S(2)}, u32[]{:S(2)}) async-start(bf16[32,112,128]{2,1,0:T(8,128)(2,1)} %bitcast.27), calls=%async_computation.2 | async-start | bytes 1835008 | tf_op jit(solution)/shard_map/all_to_all | solution.py:715
  99.7 17.8 %all-to-all-start.3 = ((bf16[32,112,128]{2,1,0:T(8,128)(2,1)}), bf16[32,112,128]{2,1,0:T(8,128)(2,1)S(1)}, u32[]{:S(2)}, u32[]{:S(2)}) async-start(bf16[32,112,128]{2,1,0:T(8,128)(2,1)} %broadcast_in_dim.3), calls=%async_computation.3 | async-start | bytes 1835008 | tf_op jit(solution)/shard_map/all_to_all | solution.py:719

commit v6 on v5

--- a/solution.py
+++ b/solution.py
@@ -1,5 +1,3 @@
-import functools
-
 import jax
 import jax.numpy as jnp
 from jax import lax
@@ -12,8 +10,9 @@
 HBM = pltpu.HBM
 PREPARE_MIB = 24
 EDGE_MIB = 24
-ROWS = 80000
-SLOTS = 80
+LATE = 110
+ROWS = 60000
+SLOTS = 60
 HALO = 4
 
 
@@ -29,7 +28,7 @@
     return lax.dot_general(left, right, (contract, ((), ())), preferred_element_type=F32)
 
 
-def call(kernel, outs, *args, scratch=(), macs=0, limit=60, aliases=None):
+def call(kernel, outs, *args, scratch=(), macs=0, limit=60):
     args = [a if isinstance(a, tuple) else (a, pltpu.VMEM) for a in args]
     outs = [o if isinstance(o, tuple) else (o, pltpu.VMEM) for o in outs]
     moved = sum(a.size * a.dtype.itemsize for a, _ in args + outs)
@@ -39,7 +38,6 @@
         in_specs=[pl.BlockSpec(memory_space=m) for _, m in args],
         out_specs=[pl.BlockSpec(memory_space=m) for _, m in outs],
         scratch_shapes=list(scratch),
-        input_output_aliases=aliases or {},
         compiler_params=pltpu.CompilerParams(vmem_limit_bytes=limit * 1024 * 1024),
         cost_estimate=pl.CostEstimate(flops=2 * macs, bytes_accessed=moved, transcendentals=0),
     )(*[a for a, _ in args])
@@ -448,15 +446,15 @@
     out[...] = turned[...].astype(BF16)
 
 
-def taps_of(grad_in, cols):
-    grad = grad_in[...].reshape(cols, 128).astype(F32)
+def taps_of(grad_in):
+    grad = grad_in[...].astype(F32)
     return jnp.concatenate([after(grad), grad, before(grad)], axis=1)
 
 
 def dec_grad_kernel(
     odd_ref, grad_in, colour_in, kept, latent,
-    local_out, grad_pre, grad_kept,
-    local, colour, slope, act, field, pre_s, moved, gram, sems,
+    local, late,
+    colour, slope, act, field, pre_s, moved, gram, sems,
 ):
     cols = act.shape[2]
     odd = odd_ref[0]
@@ -471,7 +469,7 @@
         (kept.at[3], field.at[:, :, pl.ds(384, 128)]),
     ]
     copies = [start(source, target, sems.at[k]) for k, (source, target) in enumerate(moves)]
-    taps = taps_of(grad_in, cols)
+    taps = taps_of(grad_in)
     for copy in copies[:3]:
         copy.wait()
     grad_act = dot(taps.astype(BF16), colour[...])
@@ -487,8 +485,8 @@
         sooner = jnp.where(lane >= 1, pltpu.roll(turned, 1, 1), 0.0)
         for e, value in enumerate((later, turned, sooner)):
             moved[e * 256 : (e + 1) * 256, f * cols : (f + 1) * cols] = value.astype(BF16)
-    outs = [start(pre_s, grad_pre, sems.at[8])]
-    outs.append(start(grad_in, grad_kept, sems.at[7]))
+    outs = [start(pre_s, late.at[pl.ds(0, 4)], sems.at[8])]
+    outs.append(start(grad_in, late.at[4, :, pl.ds(0, 128)], sems.at[7]))
     copies[3].wait()
     gram[...] = dot(taps.T.astype(BF16), wide_act(act))
     rows = []
@@ -511,8 +509,6 @@
     for k, value in enumerate(rows):
         gram[k * 3 : k * 3 + 3, 0:128] = value
     local[27 * 128 :, :] = gram[0:128, 0:128].astype(BF16)
-    last = pl.ds(27 * 128, 128)
-    outs.append(start(local.at[last], local_out.at[last], sems.at[36]))
     for copy in copies[4:]:
         copy.wait()
     rows_of = (2, 0, 1, 3)
@@ -527,18 +523,22 @@
                 total = wide[:128, one : one + 128] + wide[128:, two : two + 128]
                 at = ((a * 3 + b) * 3 + e) * 128
                 local[at : at + 128, :] = total.T.astype(BF16)
-                part = pl.ds(at, 128)
-                outs.append(start(local.at[part], local_out.at[part], sems.at[9 + at // 128]))
     for copy in outs:
         copy.wait()
 
 
-def latent_kernel(frames, odd_ref, grad_in, dec, rgb, first, second, pre, *rest):
-    out, own_t, edge_t, colour, edge_s, scr, out_s, sems = rest[-8:]
-    needed = range(max(0, frames[0] - 1), min(4, frames[-1] + 2))
+def latent_kernel(
+    odd_ref, late, dec, rgb, first, second,
+    out,
+    pre, grad_in, own_t, edge_t, colour, edge_s, scr, out_s, sems,
+):
     cols = first.shape[1]
     odd = odd_ref[0]
     copies = []
+    loads = [
+        start(late.at[pl.ds(0, 4)], pre, sems.at[4]),
+        start(late.at[4, :, pl.ds(0, 128)], grad_in, sems.at[5]),
+    ]
     colour_rows(rgb, scr, (-1, 2))
     colour[...] = scr[...].astype(BF16)
 
@@ -552,8 +552,10 @@
     edge_t[...] = jnp.zeros_like(edge_t)
     blocks_of(dec, False, put_own)
     blocks_of(dec, True, put_edge)
-    grad_act = dot(taps_of(grad_in, cols).astype(BF16), colour[...])
-    for f in needed:
+    for load in loads:
+        load.wait()
+    grad_act = dot(taps_of(grad_in).astype(BF16), colour[...])
+    for f in range(4):
         slopes = (
             jnp.where(odd == 1, first[f], second[f]),
             jnp.where(odd == 1, second[f], first[f]),
@@ -562,11 +564,11 @@
             at = (f * 2 + k) * 128
             value = grad_act[:, at : at + 128] * slopes[k].astype(F32)
             edge_s[f, :, k * 128 : (k + 1) * 128] = value.astype(BF16)
-    for n, f in enumerate(frames):
+    for f in range(4):
         wide = conv_rows_t([(pre, own_t), (edge_s, edge_t)], f)
-        out_s[n, 0] = wide[:, :128]
-        out_s[n, 1] = wide[:, 128:]
-        copies.append(start(out_s.at[n], out.at[f], sems.at[n]))
+        out_s[f, 0] = wide[:, :128]
+        out_s[f, 1] = wide[:, 128:]
+        copies.append(start(out_s.at[f], out.at[f], sems.at[f]))
     for copy in copies:
         copy.wait()
 
@@ -664,16 +666,16 @@
     grad_frames, sent = lax.optimization_barrier((grad_frames, kept[1]))
     second = lax.ppermute(sent, "band", second_pairs)
     grad_frames = lax.all_to_all(grad_frames.reshape(size, width, 128), "band", 0, 0)
-    local, grad_pre, grad_kept = call(
+    grad_frames = grad_frames.reshape(cols, 128)
+    local, late = call(
         dec_grad_kernel,
-        [(shape((28 * 128, 128), BF16), HBM), (field, HBM), (shape((size, width, 128), BF16), HBM)],
+        [shape((28 * 128, 128), BF16), (shape((LATE, cols, 256), BF16), HBM)],
         odd_ref,
         grad_frames,
         (colour, HBM),
         (kept, HBM),
         (latent, HBM),
         scratch=[
-            pltpu.VMEM((28 * 128, 128), BF16),
             pltpu.VMEM((384, 1024), BF16),
             pltpu.VMEM((2, 4, cols, 128), BF16),
             pltpu.VMEM((2, 4, cols, 128), BF16),
@@ -681,43 +683,38 @@
             pltpu.VMEM((4, cols, 256), BF16),
             pltpu.VMEM((768, 4 * cols), BF16),
             pltpu.VMEM((384, 1024), F32),
-            dma((37,)),
+            dma((9,)),
         ],
         macs=3 * big,
-    )
-    local, first, second = lax.optimization_barrier((local, first, second))
-    def latent_part(frames, *earlier):
-        (grad_latent,) = call(
-            functools.partial(latent_kernel, frames),
-            [(shape((4, 2, cols, 128), F32), HBM)],
-            odd_ref,
-            grad_kept,
-            dec,
-            rgb,
-            first,
-            second,
-            grad_pre,
-            *[(part, HBM) for part in earlier],
-            scratch=[
-                pltpu.VMEM((768, 768), BF16),
-                pltpu.VMEM((768, 768), BF16),
-                pltpu.VMEM((384, 1024), BF16),
-                pltpu.VMEM((4, cols, 256), BF16),
-                pltpu.VMEM((384, 1024), F32),
-                pltpu.VMEM((2, 2, cols, 128), F32),
-                dma((2,)),
-            ],
-            macs=big,
-            aliases={7: 0} if earlier else None,
-        )
-        return grad_latent
-
+        limit=40,
+    )
+    local, first = lax.optimization_barrier((local, first))
     pieces = lax.all_to_all(local.reshape(size, -1, 128), "band", 0, 0)
-    half_done = latent_part((0, 1))
+    (grad_latent,) = call(
+        latent_kernel,
+        [(shape((4, 2, cols, 128), F32), HBM)],
+        odd_ref,
+        (late, HBM),
+        dec,
+        rgb,
+        first,
+        second,
+        scratch=[
+            pltpu.VMEM((4, cols, 256), BF16),
+            pltpu.VMEM((cols, 128), BF16),
+            pltpu.VMEM((768, 768), BF16),
+            pltpu.VMEM((768, 768), BF16),
+            pltpu.VMEM((384, 1024), BF16),
+            pltpu.VMEM((4, cols, 256), BF16),
+            pltpu.VMEM((384, 1024), F32),
+            pltpu.VMEM((4, 2, cols, 128), F32),
+            dma((6,)),
+        ],
+        macs=2 * big,
+    )
     mine = jnp.sum(pieces.astype(F32), axis=0).astype(BF16)
-    mine, half_done = lax.optimization_barrier((mine, half_done))
+    mine, grad_latent = lax.optimization_barrier((mine, grad_latent))
     whole = lax.all_to_all(jnp.broadcast_to(mine, (size,) + mine.shape), "band", 0, 0)
-    grad_latent = latent_part((2, 3), half_done)
     whole = whole.reshape(28 * 128, 128)
     pixels = 4 * latent.shape[1] * size * cols
     factor = float(pixels) ** (-0.5)

time: 120 us -> 118 us (0.983)
  blocking collectives: 0 us -> 18.8 us
  waiting for transfers between devices: 30.8 us -> 19.1 us
  starting transfers between devices: 38.6 us -> 33.3 us
  Pallas kernels: 36 us -> 31.8 us
    all_to_all x0 -> x1, blocking collectives: none -> 18.8 us  [per_device(): lax.all_to_all(jnp.broadcast_to(mine, (size,) + mine.shape), 'band', 0, 0)]
    all_to_all x1 -> x0, waiting for transfers between devices: 7.25 us -> none  [per_device(): lax.all_to_all(jnp.broadcast_to(mine, (size,) + mine.shape), 'band', 0, 0)]
    all_to_all x1 -> x0, starting transfers between devices: 4.37 us -> none  [per_device(): lax.all_to_all(jnp.broadcast_to(mine, (size,) + mine.shape), 'band', 0, 0)]
    pallas_call x8 -> x7, Pallas kernels: 36 us -> 31.8 us  [call(): pl.pallas_call(kernel, out_shape=[o for o, _ in outs], in_specs=[pl.Block...]
    all_to_all x1, waiting for transfers between devices: 7.88 us -> 4.19 us  [per_device(): pieces = lax.all_to_all(local.reshape(size, -1, 128), 'band', 0, 0)]
    unnamed x20 -> x18, local copies, waits for them, and re-layouts: 5.22 us -> 5.34 us
  transfers between devices with their start and end apart: 8 -> 7, of which waited for: 5 -> 4; matrix products, arithmetic and copies ran while one was open for 4% -> 5% of each run, Pallas kernels for 21% -> 18%
where the time goes in v6:
time: 118 us; the launch traced here: 117 us
  starting transfers between devices  33.3 us (28%)
  Pallas kernels  31.8 us (27%)
  waiting for transfers between devices  19.1 us (16%)
  blocking collectives  18.8 us (16%)
  local copies, waits for them, and re-layouts  10.7 us (9%)
  other arithmetic  2.25 us (2%)
    pallas_call x7, Pallas kernels, call(): pl.pallas_call(kernel, out_shape=[o for o, _ in outs], in_specs=[pl.Block...  31.8 us
    all_to_all x1, blocking collectives, per_device(): lax.all_to_all(jnp.broadcast_to(mine, (size,) + mine.shape), 'band', 0, 0)  18.8 us
    all_to_all x1, starting transfers between devices, per_device(): parts = lax.all_to_all(parts, 'band', 0, 0)  16.3 us
    all_to_all x1, waiting for transfers between devices, per_device(): parts = lax.all_to_all(parts, 'band', 0, 0)  8.48 us
    unnamed x18, local copies, waits for them, and re-layouts  5.34 us
    all_to_all x1, starting transfers between devices, per_device(): pieces = lax.all_to_all(local.reshape(size, -1, 128), 'band', 0, 0)  5.04 us
    all_to_all x1, waiting for transfers between devices, per_device(): lax.all_to_all(grad_frames.reshape(size, width, 128), 'band', 0, 0)  4.89 us
    ppermute x1, starting transfers between devices, per_device(): first = lax.ppermute(sent, 'band', first_pairs)  4.66 us
  transfers between devices with their start and end apart: 7, of which 4 were waited for; matrix products, arithmetic and copies ran while one was open for 5% of the time, Pallas kernels for 18%

profile of v6, /device:TPU:0, one launch (start us, length us, event | category | flops | bytes accessed | tf_op | source)
XLA Modules:
  0.0 116.9 jit_solution(72492929441571320)
XLA Ops:
  0.6 0.0 copy-start
  0.7 1.2 %copy-done = bf16[4,2,512,128]{3,2,1,0:T(8,128)(2,1)S(1)} copy-done((bf16[4,2,512,128]{3,2,1,0:T(8,128)(2,1)S(1)}, bf16[4,2,512,128]{3,2,1,0:T(8,128)(2,1)}, u32[]{:S(2)}) %copy-start) | copy-done | bytes 1048600
  1.9 0.1 shard_map.103
  2.0 2.1 %collective-permute-start = (bf16[4,512,128]{2,1,0:T(8,128)(2,1)S(1)}, bf16[4,512,128]{2,1,0:T(8,128)(2,1)S(1)}, u32[]{:S(2)}, u32[]{:S(2)}) collective-permute-start(bf16[4,512,128]{2,1,0:T(8,128)(2,1)S(1)} %get-tuple-element.23), channel_id=1, source_target_pairs={{0,4},{4,0},{8,12},{12,8},{16,20},{20,16},{24,28},{28,24},{32,36},... | collective-permute-start | bytes 1572872 | tf_op jit(solution)/shard_map/ppermute | solution.py:598
  4.0 0.7 collective-permute-start.1
  4.7 0.7 reshape.82
  5.5 0.1 tile.9.vgg_first
  5.6 0.8 copy.16
  6.3 0.8 reshape.83
  7.1 0.1 copy.14
  7.2 0.1 copy.15.critic
  7.3 0.8 reverse_convert_fusion
  8.1 0.0 copy-start.4
  8.1 0.0 copy-start.1
  8.1 1.2 %copy-done.1 = bf16[4,2,512,128]{3,2,1,0:T(8,128)(2,1)S(1)} copy-done((bf16[4,2,512,128]{3,2,1,0:T(8,128)(2,1)S(1)}, bf16[4,2,512,128]{3,2,1,0:T(8,128)(2,1)}, u32[]{:S(2)}) %copy-start.1) | copy-done | bytes 1048600
  9.4 0.0 copy-start.3
  9.4 1.2 copy-done.3
  10.5 0.0 copy-start.6
  10.5 0.9 copy-done.6
  11.4 2.9 %shard_map.104 = (bf16[2,384,384]{2,1,0:T(8,128)(2,1)S(1)}, f32[2,4,512,128]{3,2,1,0:T(8,128)S(1)}, bf16[384,1024]{1,0:T(8,128)(2,1)S(1)}, bf16[60000,256]{1,0:T(8,128)(2,1)}) custom-call(bf16[4,2,512,128]{3,2,1,0:T(8,128)(2,1)S(1)} %copy-done.1, bf16[27,128,128]{2,1,0:T(8,128)(2,1)S(1)} %bitcast.21, f32[9,9,128]{2,1,0:T(8,128)S(1)} %reshape.81.rgb, ...), custom_call_target="tpu_custom_call" | custom-call | flops 2013265920 | bytes 36370944 | tf_op jit(solution)/shard_map/pallas_call | solution.py:35
  14.4 0.0 copy-done.4
  14.4 1.6 %collective-permute-done.first = bf16[4,512,128]{2,1,0:T(8,128)(2,1)S(1)} collective-permute-done((bf16[4,512,128]{2,1,0:T(8,128)(2,1)S(1)}, bf16[4,512,128]{2,1,0:T(8,128)(2,1)S(1)}, u32[]{:S(2)}, u32[]{:S(2)}) %collective-permute-start) | collective-permute-done | bytes 524320 | tf_op jit(solution)/shard_map/ppermute | solution.py:598
  16.0 1.0 shard_map.105
  17.0 0.0 collective-permute-done.1.second
  17.0 3.0 %shard_map.106 = (bf16[60,4,512,128]{3,2,1,0:T(8,128)(2,1)}, bf16[32,32,128]{2,1,0:T(8,128)(2,1)}) custom-call(s32[1]{0:T(128)} %bitcast.odd_ref, bf16[4,512,128]{2,1,0:T(8,128)(2,1)S(1)} %collective-permute-done.first, bf16[4,512,128]{2,1,0:T(8,128)(2,1)S(1)} %collective-permute-done.1.second, bf16[2,384,384]{2,1,0:T(8,128)(2,1)S(1)} %get-tuple-element.25.kernel, ...), custom_call_target="tpu_custom_call" | custom-call | flops 2013265920 | bytes 37314564 | tf_op jit(solution)/shard_map/pallas_call | solution.py:35
  20.0 0.0 copy-start.5
  20.0 16.3 %all-to-all-start = ((bf16[32,32,128]{2,1,0:T(8,128)(2,1)}), bf16[32,32,128]{2,1,0:T(8,128)(2,1)S(1)}, u32[]{:S(2)}, u32[]{:S(2)}) async-start(bf16[32,32,128]{2,1,0:T(8,128)(2,1)} %get-tuple-element.30), calls=%async_computation | async-start | bytes 524288 | tf_op jit(solution)/shard_map/all_to_all | solution.py:652
  36.3 2.1 %slice_bitcast_fusion = (bf16[4,512,128]{2,1,0:T(8,128)(2,1)S(1)}, bf16[4,512,128]{2,1,0:T(8,128)(2,1)}) fusion(bf16[60,4,512,128]{3,2,1,0:T(8,128)(2,1)} %get-tuple-element.31.kept), kind=kLoop, calls=%fused_computation.1 | loop fusion | bytes 2097152 | tf_op jit(solution)/shard_map/squeeze | solution.py:666
  38.4 8.5 %all-to-all-done = bf16[32,32,128]{2,1,0:T(8,128)(2,1)S(1)} async-done(((bf16[32,32,128]{2,1,0:T(8,128)(2,1)}), bf16[32,32,128]{2,1,0:T(8,128)(2,1)S(1)}, u32[]{:S(2)}, u32[]{:S(2)}) %all-to-all-start) | async-done | bytes 262176 | tf_op jit(solution)/shard_map/all_to_all | solution.py:652
  46.9 0.0 copy-done.5
  46.9 0.0 copy-start.2
  46.9 7.7 %shard_map.107 = bf16[512,128]{1,0:T(8,128)(2,1)} custom-call(s32[1]{0:T(128)} %bitcast.1.me_ref, bf16[1024,128]{1,0:T(8,128)(2,1)S(1)} %bitcast.19, bf16[60000,256]{1,0:T(8,128)(2,1)} %get-tuple-element.33.branch_in, f32[1,64]{1,0:T(1,128)S(1)} %bitcast.23), custom_call_target="tpu_custom_call" | custom-call | flops 3303014400 | bytes 31113476 | tf_op jit(solution)/shard_map/pallas_call | solution.py:35
  54.6 3.9 %all-to-all-start.1 = ((bf16[32,16,128]{2,1,0:T(8,128)(2,1)}), bf16[32,16,128]{2,1,0:T(8,128)(2,1)S(1)}, u32[]{:S(2)}, u32[]{:S(2)}) async-start(bf16[32,16,128]{2,1,0:T(8,128)(2,1)} %bitcast.11), calls=%async_computation.1 | async-start | bytes 262144 | tf_op jit(solution)/shard_map/all_to_all | solution.py:668
  58.5 0.7 collective-permute-start.3
  59.2 4.7 %collective-permute-start.2 = (bf16[4,512,128]{2,1,0:T(8,128)(2,1)}, bf16[4,512,128]{2,1,0:T(8,128)(2,1)S(1)}, u32[]{:S(2)}, u32[]{:S(2)}) collective-permute-start(bf16[4,512,128]{2,1,0:T(8,128)(2,1)} %get-tuple-element.36), channel_id=1, source_target_pairs={{0,4},{4,0},{8,12},{12,8},{16,20},{20,16},{24,28},{28,24},{32,36},... | collective-permute-start | bytes 1572872 | tf_op jit(solution)/shard_map/ppermute | solution.py:654
  63.8 4.9 %all-to-all-done.1 = bf16[32,16,128]{2,1,0:T(8,128)(2,1)S(1)} async-done(((bf16[32,16,128]{2,1,0:T(8,128)(2,1)}), bf16[32,16,128]{2,1,0:T(8,128)(2,1)S(1)}, u32[]{:S(2)}, u32[]{:S(2)}) %all-to-all-start.1) | async-done | bytes 131104 | tf_op jit(solution)/shard_map/all_to_all | solution.py:668
  68.7 0.0 copy-done.2
  68.7 8.7 %shard_map.108 = (bf16[3584,128]{1,0:T(8,128)(2,1)}, bf16[110,512,256]{2,1,0:T(8,128)(2,1)}) custom-call(s32[1]{0:T(128)} %bitcast.odd_ref, bf16[512,128]{1,0:T(8,128)(2,1)S(1)} %bitcast.22, bf16[384,1024]{1,0:T(8,128)(2,1)S(1)} %get-tuple-element.27.colour.colour_in, bf16[60,4,512,128]{3,2,1,0:T(8,128)(2,1)} %get-tuple-element.31.kept, ...), custom_call_target="tpu_custom_call" | custom-call | flops 6039797760 | bytes 63176708 | tf_op jit(solution)/shard_map/pallas_call | solution.py:35
  77.4 0.0 collective-permute-done.2.first
  77.4 0.0 copy-start.8
  77.4 5.0 %all-to-all-start.2 = ((bf16[32,112,128]{2,1,0:T(8,128)(2,1)}), bf16[32,112,128]{2,1,0:T(8,128)(2,1)S(1)}, u32[]{:S(2)}, u32[]{:S(2)}) async-start(bf16[32,112,128]{2,1,0:T(8,128)(2,1)} %bitcast.13), calls=%async_computation.2 | async-start | bytes 1835008 | tf_op jit(solution)/shard_map/all_to_all | solution.py:692
  82.5 0.0 collective-permute-done.3.second
  82.5 0.0 copy-start.7
  82.5 0.0 copy-done.8
  82.5 0.8 copy-done.7
  83.3 8.4 %shard_map.109 = f32[4,2,512,128]{3,2,1,0:T(8,128)} custom-call(s32[1]{0:T(128)} %bitcast.odd_ref, bf16[110,512,256]{2,1,0:T(8,128)(2,1)} %get-tuple-element.38.late, bf16[27,128,128]{2,1,0:T(8,128)(2,1)} %bitcast.20, f32[9,9,128]{2,1,0:T(8,128)} %copy-done.4, bf16[4,512,128]{2,1,0:T(8,128)(2,1)} %copy-done.8, bf16[4,512,128]{2,1,0:T(8,128)(2,1)} %copy-done.7), custom_call_target="tpu_custom_call" | custom-call | flops 4026531840 | bytes 32907780 | tf_op jit(solution)/shard_map/pallas_call | solution.py:35
  91.7 4.2 %all-to-all-done.2 = bf16[32,112,128]{2,1,0:T(8,128)(2,1)S(1)} async-done(((bf16[32,112,128]{2,1,0:T(8,128)(2,1)}), bf16[32,112,128]{2,1,0:T(8,128)(2,1)S(1)}, u32[]{:S(2)}, u32[]{:S(2)}) %all-to-all-start.2) | async-done | bytes 917536 | tf_op jit(solution)/shard_map/all_to_all | solution.py:692
  95.9 0.1 reduce_sum.12
  96.0 0.1 broadcast_in_dim.3
  96.1 18.8 %all_to_all.20 = bf16[32,112,128]{2,1,0:T(8,128)(2,1)S(1)} all-to-all(bf16[32,112,128]{2,1,0:T(8,128)(2,1)S(1)} %broadcast_in_dim.3), channel_id=1, replica_groups=mesh['band'=32,'clip'=4] {'band'}, dimensions={0} | all-to-all | bytes 1835008 | tf_op jit(solution)/shard_map/all_to_all | solution.py:717
  115.0 1.3 %convert_multiply_fusion = f32[3456,128]{1,0:T(8,128)} fusion(bf16[3584,128]{1,0:T(8,128)(2,1)S(1)} %bitcast.26), kind=kLoop, calls=%fused_computation | loop fusion | flops 884736 | bytes 2654208 | tf_op jit(solution)/shard_map/mul | solution.py:721
  116.3 0.6 mul.23
  (6 shorter events, 0.1 us)
Async XLA Ops:
  0.6 1.2 %copy-start = (bf16[4,2,512,128]{3,2,1,0:T(8,128)(2,1)S(1)}, bf16[4,2,512,128]{3,2,1,0:T(8,128)(2,1)}, u32[]{:S(2)}) copy-start(bf16[4,2,512,128]{3,2,1,0:T(8,128)(2,1)} %latent.5) | copy-start | bytes 3145732
  2.0 14.0 %collective-permute-start = (bf16[4,512,128]{2,1,0:T(8,128)(2,1)S(1)}, bf16[4,512,128]{2,1,0:T(8,128)(2,1)S(1)}, u32[]{:S(2)}, u32[]{:S(2)}) collective-permute-start(bf16[4,512,128]{2,1,0:T(8,128)(2,1)S(1)} %get-tuple-element.23), channel_id=1, source_target_pairs={{0,4},{4,0},{8,12},{12,8},{16,20},{20,16},{24,28},{28,24},{32,36},... | collective-permute-start | bytes 1572872 | tf_op jit(solution)/shard_map/ppermute | solution.py:598
  4.0 13.0 %collective-permute-start.1 = (bf16[4,512,128]{2,1,0:T(8,128)(2,1)S(1)}, bf16[4,512,128]{2,1,0:T(8,128)(2,1)S(1)}, u32[]{:S(2)}, u32[]{:S(2)}) collective-permute-start(bf16[4,512,128]{2,1,0:T(8,128)(2,1)S(1)} %get-tuple-element.24), channel_id=1, source_target_pairs={{4,8},{8,4},{12,16},{16,12},{20,24},{24,20},{28,32},{32,28},{36,40... | collective-permute-start | bytes 1572872 | tf_op jit(solution)/shard_map/ppermute | solution.py:599
  8.1 6.3 %copy-start.4 = (f32[9,9,128]{2,1,0:T(8,128)}, f32[9,9,128]{2,1,0:T(8,128)S(1)}, u32[]{:S(2)}) copy-start(f32[9,9,128]{2,1,0:T(8,128)S(1)} %reshape.81.rgb) | copy-start | bytes 124420
  8.1 1.3 %copy-start.1 = (bf16[4,2,512,128]{3,2,1,0:T(8,128)(2,1)S(1)}, bf16[4,2,512,128]{3,2,1,0:T(8,128)(2,1)}, u32[]{:S(2)}) copy-start(bf16[4,2,512,128]{3,2,1,0:T(8,128)(2,1)} %latent.5) | copy-start | bytes 3145732
  9.4 1.2 copy-start.3
  10.5 0.9 copy-start.6
  20.0 26.9 %copy-start.5 = (f32[64]{0:T(128)S(1)}, f32[64]{0:T(128)}, u32[]{:S(2)}) copy-start(f32[64]{0:T(128)} %param.15) | copy-start | bytes 772
  20.0 26.9 %all-to-all-start = ((bf16[32,32,128]{2,1,0:T(8,128)(2,1)}), bf16[32,32,128]{2,1,0:T(8,128)(2,1)S(1)}, u32[]{:S(2)}, u32[]{:S(2)}) async-start(bf16[32,32,128]{2,1,0:T(8,128)(2,1)} %get-tuple-element.30), calls=%async_computation | async-start | bytes 524288 | tf_op jit(solution)/shard_map/all_to_all | solution.py:652
  46.9 21.8 %copy-start.2 = (bf16[4,2,512,128]{3,2,1,0:T(8,128)(2,1)S(1)}, bf16[4,2,512,128]{3,2,1,0:T(8,128)(2,1)}, u32[]{:S(2)}) copy-start(bf16[4,2,512,128]{3,2,1,0:T(8,128)(2,1)} %latent.5) | copy-start | bytes 3145732
  54.6 14.1 %all-to-all-start.1 = ((bf16[32,16,128]{2,1,0:T(8,128)(2,1)}), bf16[32,16,128]{2,1,0:T(8,128)(2,1)S(1)}, u32[]{:S(2)}, u32[]{:S(2)}) async-start(bf16[32,16,128]{2,1,0:T(8,128)(2,1)} %bitcast.11), calls=%async_computation.1 | async-start | bytes 262144 | tf_op jit(solution)/shard_map/all_to_all | solution.py:668
  58.5 24.0 %collective-permute-start.3 = (bf16[4,512,128]{2,1,0:T(8,128)(2,1)S(1)}, bf16[4,512,128]{2,1,0:T(8,128)(2,1)S(1)}, u32[]{:S(2)}, u32[]{:S(2)}) collective-permute-start(bf16[4,512,128]{2,1,0:T(8,128)(2,1)S(1)} %get-tuple-element.40), channel_id=1, source_target_pairs={{4,8},{8,4},{12,16},{16,12},{20,24},{24,20},{28,32},{32,28},{36,40... | collective-permute-start | bytes 1572872 | tf_op jit(solution)/shard_map/ppermute | solution.py:667
  59.2 18.3 %collective-permute-start.2 = (bf16[4,512,128]{2,1,0:T(8,128)(2,1)}, bf16[4,512,128]{2,1,0:T(8,128)(2,1)S(1)}, u32[]{:S(2)}, u32[]{:S(2)}) collective-permute-start(bf16[4,512,128]{2,1,0:T(8,128)(2,1)} %get-tuple-element.36), channel_id=1, source_target_pairs={{0,4},{4,0},{8,12},{12,8},{16,20},{20,16},{24,28},{28,24},{32,36},... | collective-permute-start | bytes 1572872 | tf_op jit(solution)/shard_map/ppermute | solution.py:654
  77.4 5.1 %copy-start.8 = (bf16[4,512,128]{2,1,0:T(8,128)(2,1)}, bf16[4,512,128]{2,1,0:T(8,128)(2,1)S(1)}, u32[]{:S(2)}) copy-start(bf16[4,512,128]{2,1,0:T(8,128)(2,1)S(1)} %collective-permute-done.2.first) | copy-start | bytes 1572868
  77.4 18.4 %all-to-all-start.2 = ((bf16[32,112,128]{2,1,0:T(8,128)(2,1)}), bf16[32,112,128]{2,1,0:T(8,128)(2,1)S(1)}, u32[]{:S(2)}, u32[]{:S(2)}) async-start(bf16[32,112,128]{2,1,0:T(8,128)(2,1)} %bitcast.13), calls=%async_computation.2 | async-start | bytes 1835008 | tf_op jit(solution)/shard_map/all_to_all | solution.py:692
  82.5 0.8 copy-start.7

commit v7 on v6

--- a/solution.py
+++ b/solution.py
@@ -480,11 +480,12 @@
         one = (wide[:, 128:] * slope[1, f].astype(F32)).astype(BF16)
         pre_s[f, :, :128] = zero
         pre_s[f, :, 128:] = one
-        turned = jnp.concatenate([zero.astype(F32).T, one.astype(F32).T], axis=0)
-        later = jnp.where(lane < cols - 1, pltpu.roll(turned, cols - 1, 1), 0.0)
-        sooner = jnp.where(lane >= 1, pltpu.roll(turned, 1, 1), 0.0)
+        turned = jnp.concatenate([zero.T, one.T], axis=0)
+        none = jnp.zeros_like(turned)
+        later = jnp.where(lane < cols - 1, pltpu.roll(turned, cols - 1, 1), none)
+        sooner = jnp.where(lane >= 1, pltpu.roll(turned, 1, 1), none)
         for e, value in enumerate((later, turned, sooner)):
-            moved[e * 256 : (e + 1) * 256, f * cols : (f + 1) * cols] = value.astype(BF16)
+            moved[e * 256 : (e + 1) * 256, f * cols : (f + 1) * cols] = value
     outs = [start(pre_s, late.at[pl.ds(0, 4)], sems.at[8])]
     outs.append(start(grad_in, late.at[4, :, pl.ds(0, 128)], sems.at[7]))
     copies[3].wait()
@@ -516,8 +517,9 @@
         lo, hi = (max(0, 1 - a), min(4, 5 - a))
         first, last = (lo * cols, hi * cols)
         source = field[lo + a - 1 : hi + a - 1].reshape((hi - lo) * cols, 512)
+        gram_a = dot(moved[:, first:last], source)
         for e in range(3):
-            wide = dot(moved[e * 256 : (e + 1) * 256, first:last], source)
+            wide = gram_a[e * 256 : (e + 1) * 256]
             for b in range(3):
                 one, two = (rows_of[b] * 128, rows_of[b + 1] * 128)
                 total = wide[:128, one : one + 128] + wide[128:, two : two + 128]

time: 118 us -> 118 us (level)
  no operation moved by 1% of the time
where the time goes in v7:
time: 118 us; the launch traced here: 117 us
  starting transfers between devices  33.3 us (28%)
  Pallas kernels  31.7 us (27%)
  waiting for transfers between devices  19 us (16%)
  blocking collectives  19 us (16%)
  local copies, waits for them, and re-layouts  10.7 us (9%)
  other arithmetic  2.25 us (2%)
    pallas_call x7, Pallas kernels, call(): pl.pallas_call(kernel, out_shape=[o for o, _ in outs], in_specs=[pl.Block...  31.7 us
    all_to_all x1, blocking collectives, per_device(): lax.all_to_all(jnp.broadcast_to(mine, (size,) + mine.shape), 'band', 0, 0)  19 us
    all_to_all x1, starting transfers between devices, per_device(): parts = lax.all_to_all(parts, 'band', 0, 0)  16.3 us
    all_to_all x1, waiting for transfers between devices, per_device(): parts = lax.all_to_all(parts, 'band', 0, 0)  8.48 us
    unnamed x18, local copies, waits for them, and re-layouts  5.34 us
    all_to_all x1, starting transfers between devices, per_device(): pieces = lax.all_to_all(local.reshape(size, -1, 128), 'band', 0, 0)  5.26 us
    all_to_all x1, waiting for transfers between devices, per_device(): lax.all_to_all(grad_frames.reshape(size, width, 128), 'band', 0, 0)  5.11 us
    ppermute x1, starting transfers between devices, per_device(): first = lax.ppermute(sent, 'band', first_pairs)  4.44 us
  transfers between devices with their start and end apart: 7, of which 4 were waited for; matrix products, arithmetic and copies ran while one was open for 5% of the time, Pallas kernels for 18%

profile of v7, /device:TPU:0, one launch (start us, length us, event | category | flops | bytes accessed | tf_op | source)
XLA Modules:
  0.0 116.8 jit_solution(13121342099997494734)
XLA Ops:
  0.6 0.0 copy-start
  0.7 1.2 %copy-done = bf16[4,2,512,128]{3,2,1,0:T(8,128)(2,1)S(1)} copy-done((bf16[4,2,512,128]{3,2,1,0:T(8,128)(2,1)S(1)}, bf16[4,2,512,128]{3,2,1,0:T(8,128)(2,1)}, u32[]{:S(2)}) %copy-start) | copy-done | bytes 1048600
  1.9 0.1 shard_map.103
  2.0 2.1 %collective-permute-start = (bf16[4,512,128]{2,1,0:T(8,128)(2,1)S(1)}, bf16[4,512,128]{2,1,0:T(8,128)(2,1)S(1)}, u32[]{:S(2)}, u32[]{:S(2)}) collective-permute-start(bf16[4,512,128]{2,1,0:T(8,128)(2,1)S(1)} %get-tuple-element.23), channel_id=1, source_target_pairs={{0,4},{4,0},{8,12},{12,8},{16,20},{20,16},{24,28},{28,24},{32,36},... | collective-permute-start | bytes 1572872 | tf_op jit(solution)/shard_map/ppermute | solution.py:600
  4.0 0.7 collective-permute-start.1
  4.7 0.7 reshape.82
  5.5 0.1 tile.9.vgg_first
  5.6 0.8 copy.16
  6.3 0.8 reshape.83
  7.1 0.1 copy.14
  7.2 0.1 copy.15.critic
  7.3 0.8 reverse_convert_fusion
  8.1 0.0 copy-start.4
  8.1 0.0 copy-start.1
  8.1 1.2 %copy-done.1 = bf16[4,2,512,128]{3,2,1,0:T(8,128)(2,1)S(1)} copy-done((bf16[4,2,512,128]{3,2,1,0:T(8,128)(2,1)S(1)}, bf16[4,2,512,128]{3,2,1,0:T(8,128)(2,1)}, u32[]{:S(2)}) %copy-start.1) | copy-done | bytes 1048600
  9.4 0.0 copy-start.3
  9.4 1.2 copy-done.3
  10.5 0.0 copy-start.6
  10.5 0.9 copy-done.6
  11.4 2.9 %shard_map.104 = (bf16[2,384,384]{2,1,0:T(8,128)(2,1)S(1)}, f32[2,4,512,128]{3,2,1,0:T(8,128)S(1)}, bf16[384,1024]{1,0:T(8,128)(2,1)S(1)}, bf16[60000,256]{1,0:T(8,128)(2,1)}) custom-call(bf16[4,2,512,128]{3,2,1,0:T(8,128)(2,1)S(1)} %copy-done.1, bf16[27,128,128]{2,1,0:T(8,128)(2,1)S(1)} %bitcast.21, f32[9,9,128]{2,1,0:T(8,128)S(1)} %reshape.81.rgb, ...), custom_call_target="tpu_custom_call" | custom-call | flops 2013265920 | bytes 36370944 | tf_op jit(solution)/shard_map/pallas_call | solution.py:35
  14.4 0.0 copy-done.4
  14.4 1.6 %collective-permute-done.first = bf16[4,512,128]{2,1,0:T(8,128)(2,1)S(1)} collective-permute-done((bf16[4,512,128]{2,1,0:T(8,128)(2,1)S(1)}, bf16[4,512,128]{2,1,0:T(8,128)(2,1)S(1)}, u32[]{:S(2)}, u32[]{:S(2)}) %collective-permute-start) | collective-permute-done | bytes 524320 | tf_op jit(solution)/shard_map/ppermute | solution.py:600
  16.0 1.0 shard_map.105
  17.0 0.0 collective-permute-done.1.second
  17.0 3.0 %shard_map.106 = (bf16[60,4,512,128]{3,2,1,0:T(8,128)(2,1)}, bf16[32,32,128]{2,1,0:T(8,128)(2,1)}) custom-call(s32[1]{0:T(128)} %bitcast.odd_ref, bf16[4,512,128]{2,1,0:T(8,128)(2,1)S(1)} %collective-permute-done.first, bf16[4,512,128]{2,1,0:T(8,128)(2,1)S(1)} %collective-permute-done.1.second, bf16[2,384,384]{2,1,0:T(8,128)(2,1)S(1)} %get-tuple-element.25.kernel, ...), custom_call_target="tpu_custom_call" | custom-call | flops 2013265920 | bytes 37314564 | tf_op jit(solution)/shard_map/pallas_call | solution.py:35
  20.0 0.0 copy-start.5
  20.0 16.3 %all-to-all-start = ((bf16[32,32,128]{2,1,0:T(8,128)(2,1)}), bf16[32,32,128]{2,1,0:T(8,128)(2,1)S(1)}, u32[]{:S(2)}, u32[]{:S(2)}) async-start(bf16[32,32,128]{2,1,0:T(8,128)(2,1)} %get-tuple-element.30), calls=%async_computation | async-start | bytes 524288 | tf_op jit(solution)/shard_map/all_to_all | solution.py:654
  36.3 2.1 %slice_bitcast_fusion = (bf16[4,512,128]{2,1,0:T(8,128)(2,1)S(1)}, bf16[4,512,128]{2,1,0:T(8,128)(2,1)}) fusion(bf16[60,4,512,128]{3,2,1,0:T(8,128)(2,1)} %get-tuple-element.31.kept), kind=kLoop, calls=%fused_computation.1 | loop fusion | bytes 2097152 | tf_op jit(solution)/shard_map/squeeze | solution.py:668
  38.4 8.5 %all-to-all-done = bf16[32,32,128]{2,1,0:T(8,128)(2,1)S(1)} async-done(((bf16[32,32,128]{2,1,0:T(8,128)(2,1)}), bf16[32,32,128]{2,1,0:T(8,128)(2,1)S(1)}, u32[]{:S(2)}, u32[]{:S(2)}) %all-to-all-start) | async-done | bytes 262176 | tf_op jit(solution)/shard_map/all_to_all | solution.py:654
  46.9 0.0 copy-done.5
  46.9 0.0 copy-start.2
  46.9 7.7 %shard_map.107 = bf16[512,128]{1,0:T(8,128)(2,1)} custom-call(s32[1]{0:T(128)} %bitcast.1.me_ref, bf16[1024,128]{1,0:T(8,128)(2,1)S(1)} %bitcast.19, bf16[60000,256]{1,0:T(8,128)(2,1)} %get-tuple-element.33.branch_in, f32[1,64]{1,0:T(1,128)S(1)} %bitcast.23), custom_call_target="tpu_custom_call" | custom-call | flops 3303014400 | bytes 31113476 | tf_op jit(solution)/shard_map/pallas_call | solution.py:35
  54.6 3.9 %all-to-all-start.1 = ((bf16[32,16,128]{2,1,0:T(8,128)(2,1)}), bf16[32,16,128]{2,1,0:T(8,128)(2,1)S(1)}, u32[]{:S(2)}, u32[]{:S(2)}) async-start(bf16[32,16,128]{2,1,0:T(8,128)(2,1)} %bitcast.11), calls=%async_computation.1 | async-start | bytes 262144 | tf_op jit(solution)/shard_map/all_to_all | solution.py:670
  58.5 0.7 collective-permute-start.3
  59.2 4.4 %collective-permute-start.2 = (bf16[4,512,128]{2,1,0:T(8,128)(2,1)}, bf16[4,512,128]{2,1,0:T(8,128)(2,1)S(1)}, u32[]{:S(2)}, u32[]{:S(2)}) collective-permute-start(bf16[4,512,128]{2,1,0:T(8,128)(2,1)} %get-tuple-element.36), channel_id=1, source_target_pairs={{0,4},{4,0},{8,12},{12,8},{16,20},{20,16},{24,28},{28,24},{32,36},... | collective-permute-start | bytes 1572872 | tf_op jit(solution)/shard_map/ppermute | solution.py:656
  63.6 5.1 %all-to-all-done.1 = bf16[32,16,128]{2,1,0:T(8,128)(2,1)S(1)} async-done(((bf16[32,16,128]{2,1,0:T(8,128)(2,1)}), bf16[32,16,128]{2,1,0:T(8,128)(2,1)S(1)}, u32[]{:S(2)}, u32[]{:S(2)}) %all-to-all-start.1) | async-done | bytes 131104 | tf_op jit(solution)/shard_map/all_to_all | solution.py:670
  68.7 0.0 copy-done.2
  68.7 8.6 %shard_map.108 = (bf16[3584,128]{1,0:T(8,128)(2,1)}, bf16[110,512,256]{2,1,0:T(8,128)(2,1)}) custom-call(s32[1]{0:T(128)} %bitcast.odd_ref, bf16[512,128]{1,0:T(8,128)(2,1)S(1)} %bitcast.22, bf16[384,1024]{1,0:T(8,128)(2,1)S(1)} %get-tuple-element.27.colour.colour_in, bf16[60,4,512,128]{3,2,1,0:T(8,128)(2,1)} %get-tuple-element.31.kept, ...), custom_call_target="tpu_custom_call" | custom-call | flops 6039797760 | bytes 63176708 | tf_op jit(solution)/shard_map/pallas_call | solution.py:35
  77.3 0.0 collective-permute-done.2.first
  77.3 0.0 copy-start.8
  77.3 5.3 %all-to-all-start.2 = ((bf16[32,112,128]{2,1,0:T(8,128)(2,1)}), bf16[32,112,128]{2,1,0:T(8,128)(2,1)S(1)}, u32[]{:S(2)}, u32[]{:S(2)}) async-start(bf16[32,112,128]{2,1,0:T(8,128)(2,1)} %bitcast.13), calls=%async_computation.2 | async-start | bytes 1835008 | tf_op jit(solution)/shard_map/all_to_all | solution.py:694
  82.6 0.0 collective-permute-done.3.second
  82.6 0.0 copy-start.7
  82.6 0.0 copy-done.8
  82.6 0.8 copy-done.7
  83.4 8.4 %shard_map.109 = f32[4,2,512,128]{3,2,1,0:T(8,128)} custom-call(s32[1]{0:T(128)} %bitcast.odd_ref, bf16[110,512,256]{2,1,0:T(8,128)(2,1)} %get-tuple-element.38.late, bf16[27,128,128]{2,1,0:T(8,128)(2,1)} %bitcast.20, f32[9,9,128]{2,1,0:T(8,128)} %copy-done.4, bf16[4,512,128]{2,1,0:T(8,128)(2,1)} %copy-done.8, bf16[4,512,128]{2,1,0:T(8,128)(2,1)} %copy-done.7), custom_call_target="tpu_custom_call" | custom-call | flops 4026531840 | bytes 32907780 | tf_op jit(solution)/shard_map/pallas_call | solution.py:35
  91.8 3.8 %all-to-all-done.2 = bf16[32,112,128]{2,1,0:T(8,128)(2,1)S(1)} async-done(((bf16[32,112,128]{2,1,0:T(8,128)(2,1)}), bf16[32,112,128]{2,1,0:T(8,128)(2,1)S(1)}, u32[]{:S(2)}, u32[]{:S(2)}) %all-to-all-start.2) | async-done | bytes 917536 | tf_op jit(solution)/shard_map/all_to_all | solution.py:694
  95.6 0.1 reduce_sum.12
  95.7 0.1 broadcast_in_dim.3
  95.9 19.0 %all_to_all.20 = bf16[32,112,128]{2,1,0:T(8,128)(2,1)S(1)} all-to-all(bf16[32,112,128]{2,1,0:T(8,128)(2,1)S(1)} %broadcast_in_dim.3), channel_id=1, replica_groups=mesh['band'=32,'clip'=4] {'band'}, dimensions={0} | all-to-all | bytes 1835008 | tf_op jit(solution)/shard_map/all_to_all | solution.py:719
  114.8 1.3 %convert_multiply_fusion = f32[3456,128]{1,0:T(8,128)} fusion(bf16[3584,128]{1,0:T(8,128)(2,1)S(1)} %bitcast.26), kind=kLoop, calls=%fused_computation | loop fusion | flops 884736 | bytes 2654208 | tf_op jit(solution)/shard_map/mul | solution.py:723
  116.2 0.6 mul.23
  (6 shorter events, 0.1 us)
Async XLA Ops:
  0.6 1.2 %copy-start = (bf16[4,2,512,128]{3,2,1,0:T(8,128)(2,1)S(1)}, bf16[4,2,512,128]{3,2,1,0:T(8,128)(2,1)}, u32[]{:S(2)}) copy-start(bf16[4,2,512,128]{3,2,1,0:T(8,128)(2,1)} %latent.5) | copy-start | bytes 3145732
  2.0 14.0 %collective-permute-start = (bf16[4,512,128]{2,1,0:T(8,128)(2,1)S(1)}, bf16[4,512,128]{2,1,0:T(8,128)(2,1)S(1)}, u32[]{:S(2)}, u32[]{:S(2)}) collective-permute-start(bf16[4,512,128]{2,1,0:T(8,128)(2,1)S(1)} %get-tuple-element.23), channel_id=1, source_target_pairs={{0,4},{4,0},{8,12},{12,8},{16,20},{20,16},{24,28},{28,24},{32,36},... | collective-permute-start | bytes 1572872 | tf_op jit(solution)/shard_map/ppermute | solution.py:600
  4.0 13.0 %collective-permute-start.1 = (bf16[4,512,128]{2,1,0:T(8,128)(2,1)S(1)}, bf16[4,512,128]{2,1,0:T(8,128)(2,1)S(1)}, u32[]{:S(2)}, u32[]{:S(2)}) collective-permute-start(bf16[4,512,128]{2,1,0:T(8,128)(2,1)S(1)} %get-tuple-element.24), channel_id=1, source_target_pairs={{4,8},{8,4},{12,16},{16,12},{20,24},{24,20},{28,32},{32,28},{36,40... | collective-permute-start | bytes 1572872 | tf_op jit(solution)/shard_map/ppermute | solution.py:601
  8.1 6.3 %copy-start.4 = (f32[9,9,128]{2,1,0:T(8,128)}, f32[9,9,128]{2,1,0:T(8,128)S(1)}, u32[]{:S(2)}) copy-start(f32[9,9,128]{2,1,0:T(8,128)S(1)} %reshape.81.rgb) | copy-start | bytes 124420
  8.1 1.3 %copy-start.1 = (bf16[4,2,512,128]{3,2,1,0:T(8,128)(2,1)S(1)}, bf16[4,2,512,128]{3,2,1,0:T(8,128)(2,1)}, u32[]{:S(2)}) copy-start(bf16[4,2,512,128]{3,2,1,0:T(8,128)(2,1)} %latent.5) | copy-start | bytes 3145732
  9.4 1.2 copy-start.3
  10.5 0.9 copy-start.6
  20.0 26.9 %copy-start.5 = (f32[64]{0:T(128)S(1)}, f32[64]{0:T(128)}, u32[]{:S(2)}) copy-start(f32[64]{0:T(128)} %param.15) | copy-start | bytes 772
  20.0 26.9 %all-to-all-start = ((bf16[32,32,128]{2,1,0:T(8,128)(2,1)}), bf16[32,32,128]{2,1,0:T(8,128)(2,1)S(1)}, u32[]{:S(2)}, u32[]{:S(2)}) async-start(bf16[32,32,128]{2,1,0:T(8,128)(2,1)} %get-tuple-element.30), calls=%async_computation | async-start | bytes 524288 | tf_op jit(solution)/shard_map/all_to_all | solution.py:654
  46.9 21.8 %copy-start.2 = (bf16[4,2,512,128]{3,2,1,0:T(8,128)(2,1)S(1)}, bf16[4,2,512,128]{3,2,1,0:T(8,128)(2,1)}, u32[]{:S(2)}) copy-start(bf16[4,2,512,128]{3,2,1,0:T(8,128)(2,1)} %latent.5) | copy-start | bytes 3145732
  54.6 14.1 %all-to-all-start.1 = ((bf16[32,16,128]{2,1,0:T(8,128)(2,1)}), bf16[32,16,128]{2,1,0:T(8,128)(2,1)S(1)}, u32[]{:S(2)}, u32[]{:S(2)}) async-start(bf16[32,16,128]{2,1,0:T(8,128)(2,1)} %bitcast.11), calls=%async_computation.1 | async-start | bytes 262144 | tf_op jit(solution)/shard_map/all_to_all | solution.py:670
  58.5 24.1 %collective-permute-start.3 = (bf16[4,512,128]{2,1,0:T(8,128)(2,1)S(1)}, bf16[4,512,128]{2,1,0:T(8,128)(2,1)S(1)}, u32[]{:S(2)}, u32[]{:S(2)}) collective-permute-start(bf16[4,512,128]{2,1,0:T(8,128)(2,1)S(1)} %get-tuple-element.40), channel_id=1, source_target_pairs={{4,8},{8,4},{12,16},{16,12},{20,24},{24,20},{28,32},{32,28},{36,40... | collective-permute-start | bytes 1572872 | tf_op jit(solution)/shard_map/ppermute | solution.py:669
  59.2 18.1 %collective-permute-start.2 = (bf16[4,512,128]{2,1,0:T(8,128)(2,1)}, bf16[4,512,128]{2,1,0:T(8,128)(2,1)S(1)}, u32[]{:S(2)}, u32[]{:S(2)}) collective-permute-start(bf16[4,512,128]{2,1,0:T(8,128)(2,1)} %get-tuple-element.36), channel_id=1, source_target_pairs={{0,4},{4,0},{8,12},{12,8},{16,20},{20,16},{24,28},{28,24},{32,36},... | collective-permute-start | bytes 1572872 | tf_op jit(solution)/shard_map/ppermute | solution.py:656
  77.3 5.3 %copy-start.8 = (bf16[4,512,128]{2,1,0:T(8,128)(2,1)}, bf16[4,512,128]{2,1,0:T(8,128)(2,1)S(1)}, u32[]{:S(2)}) copy-start(bf16[4,512,128]{2,1,0:T(8,128)(2,1)S(1)} %collective-permute-done.2.first) | copy-start | bytes 1572868
  77.3 18.3 %all-to-all-start.2 = ((bf16[32,112,128]{2,1,0:T(8,128)(2,1)}), bf16[32,112,128]{2,1,0:T(8,128)(2,1)S(1)}, u32[]{:S(2)}, u32[]{:S(2)}) async-start(bf16[32,112,128]{2,1,0:T(8,128)(2,1)} %bitcast.13), calls=%async_computation.2 | async-start | bytes 1835008 | tf_op jit(solution)/shard_map/all_to_all | solution.py:694
  82.6 0.8 copy-start.7
